TPU v7x, 32 devices: a whole 2x2x4 slice. The times are simulated.
32 devices in a mesh: de: 8 (over y, x, core), et: 4 (over z).
Axes of the slice: x: 2, y: 2, z: 4, core: 2. Of those that a mesh axis runs over, the one named last changes fastest.
Arguments:
- tokens: bfloat16 [64, 6144], P('de', 'et'), may hold values from -6 to 6
- expert_ids: int32 [64, 2], P('de'), may hold values from 0 to 3, all different within a row; in each aligned block of 8 rows (0 to 7, 8 to 15, ...) at most 5 rows name the same one
- gate_probs: float32 [64, 2], P('de'), may hold values from 0.1 to 1
- w_gate: bfloat16 [6144, 65536], P(None, ('de', 'et')), may hold values from -0.078125 to 0.078125
- w_up: bfloat16 [6144, 65536], P(None, ('de', 'et')), may hold values from -0.078125 to 0.078125
- w_down: bfloat16 [65536, 6144], P(('de', 'et')), may hold values from -0.046875 to 0.046875
- out_grad: bfloat16 [64, 6144], P('de', 'et'), may hold values from -6 to 6
Outputs:
- mixed: bfloat16 [64, 6144], P('de', 'et')
- token_grad: bfloat16 [64, 6144], P('de', 'et')
- prob_grad: float32 [64, 2], P('de')
Inputs may be any that keep to these rules, and one draw needn't show every extreme that they name: `expert_ids`: the 2 entries of a token are different. Among the 8 tokens of one index of de, no expert is named by more than 5 tokens, a bound that some expert reaches in some of these blocks.
All inputs are finite; a program needn't handle non-finite values.
Results may differ from a plain program's by a relative error of at most 0.02.
Values may be sent and summed in bfloat16 or wider, within the bound.
No kernel may reach another device: no remote copies, remote signals or barrier semaphores. Data moves between devices by JAX's collectives and lax.ppermute only.
A program may use at most 128 MiB of HBM per device.

v0:
```python
import jax
import jax.numpy as jnp
from jax import lax
from jax.sharding import PartitionSpec as P

EXPERTS = 4
CAP = 5


def activate(gate, up, d_hidden):
    sig = jax.nn.sigmoid(gate)
    hidden = (gate * sig * up).astype(jnp.bfloat16)
    d_gate = (d_hidden * up * sig * (1.0 + gate * (1.0 - sig))).astype(jnp.bfloat16)
    d_up = (d_hidden * gate * sig).astype(jnp.bfloat16)
    return (hidden, d_gate, d_up)


def input_terms(d_gate, d_up, w_gate, w_up):
    first = lax.dot_general(
        d_gate, w_gate, (((1,), (1,)), ((), ())), preferred_element_type=jnp.float32
    )
    return first + lax.dot_general(
        d_up, w_up, (((1,), (1,)), ((), ())), preferred_element_type=jnp.float32
    )


def body(tokens, expert_ids, gate_probs, w_gate, w_up, w_down, out_grad):
    n_de = lax.axis_size("de")
    members = n_de // EXPERTS
    width = tokens.shape[1]
    picks = (expert_ids[:, :, None] == jnp.arange(EXPERTS, dtype=jnp.int32)[None, None, :]).astype(
        jnp.float32
    )
    named = jnp.sum(picks, axis=1)
    weight = jnp.sum(picks * gate_probs[:, :, None], axis=1)
    rank = jnp.cumsum(named.astype(jnp.int32), axis=0) - 1
    place = named.T[:, None, :] * (
        rank.T[:, None, :] == jnp.arange(CAP, dtype=jnp.int32)[None, :, None]
    ).astype(jnp.float32)
    grad_f = out_grad.astype(jnp.float32)
    highest = lax.Precision.HIGHEST
    x_slots = jnp.einsum(
        "ect,td->ecd", place, tokens.astype(jnp.float32), precision=highest
    ).astype(jnp.bfloat16)
    scaled = weight[:, :, None] * grad_f[:, None, :]
    g_slots = jnp.einsum("ect,ted->ecd", place, scaled, precision=highest).astype(jnp.bfloat16)
    x_send = jnp.repeat(x_slots, members, axis=0).reshape(n_de * CAP, width)
    g_send = jnp.repeat(g_slots, members, axis=0).reshape(n_de * CAP, width)
    x_recv, g_recv = (
        lax.all_to_all(x_send, "de", split_axis=0, concat_axis=0, tiled=True),
        lax.all_to_all(g_send, "de", split_axis=0, concat_axis=0, tiled=True),
    )
    x_piece = lax.all_gather(x_recv, "et", axis=1, tiled=True)
    g_piece = lax.all_gather(g_recv, "et", axis=1, tiled=True)
    gate = jnp.dot(x_piece, w_gate, preferred_element_type=jnp.float32)
    up = jnp.dot(x_piece, w_up, preferred_element_type=jnp.float32)
    back = lax.dot_general(
        g_piece, w_down, (((1,), (1,)), ((), ())), preferred_element_type=jnp.float32
    )
    gate, up, d_hidden = (gate, up, back)
    hidden, d_gate, d_up = activate(gate, up, d_hidden)
    y_term = jnp.dot(hidden, w_down, preferred_element_type=jnp.float32)
    x_term = input_terms(d_gate, d_up, w_gate, w_up)
    y_part, x_part = (
        lax.psum_scatter(y_term.astype(jnp.bfloat16), "et", scatter_dimension=1, tiled=True).astype(
            jnp.float32
        ),
        lax.psum_scatter(x_term.astype(jnp.bfloat16), "et", scatter_dimension=1, tiled=True).astype(
            jnp.float32
        ),
    )
    y_back, x_back = (
        lax.all_to_all(
            y_part.astype(jnp.bfloat16), "de", split_axis=0, concat_axis=0, tiled=True
        ).astype(y_part.dtype),
        lax.all_to_all(
            x_part.astype(jnp.bfloat16), "de", split_axis=0, concat_axis=0, tiled=True
        ).astype(x_part.dtype),
    )
    y_sum = jnp.sum(y_back.reshape(EXPERTS, members, CAP, width), axis=1)
    x_sum = jnp.sum(x_back.reshape(EXPERTS, members, CAP, width), axis=1)
    weighted = place * weight.T[:, None, :]
    mixed = jnp.einsum("ect,ecd->td", weighted, y_sum, precision=highest).astype(jnp.bfloat16)
    token_grad = jnp.einsum("ect,ecd->td", place, x_sum, precision=highest).astype(jnp.bfloat16)
    products = jnp.einsum("ecd,td->ect", y_sum, grad_f, precision=highest)
    scores = jnp.sum(place * products, axis=1).T
    partial_grad = jnp.sum(picks * scores[:, None, :], axis=2)
    prob_grad = lax.psum(partial_grad, "et")
    return (mixed, token_grad, prob_grad)


def solution(mesh):
    return jax.shard_map(
        body,
        mesh=mesh,
        in_specs=(
            P("de", "et"),
            P("de", None),
            P("de", None),
            P(None, ("de", "et")),
            P(None, ("de", "et")),
            P(("de", "et"), None),
            P("de", "et"),
        ),
        out_specs=(P("de", "et"), P("de", "et"), P("de", None)),
        check_vma=False,
    )
```

profile of v0, /device:TPU:0, one launch (start us, length us, event | category | flops | bytes accessed | tf_op | source)
XLA Modules:
  0.0 204.9 jit_solution(12318046724433169837)
XLA Ops:
  7.2 0.0 copy-start
  7.2 0.0 reduce-scatter.3.cloned.1.call-start
  7.2 0.7 convert_reduce_fusion.2
  7.9 0.2 reduce_window_sum.11
  8.1 0.2 convolution_convert_fusion.2
  8.4 11.2 %all_to_all.42 = bf16[8,5,1536]{2,1,0:T(8,128)(2,1)S(1)} all-to-all(bf16[8,5,1536]{2,1,0:T(8,128)(2,1)S(1)} %bitcast.39), channel_id=1, replica_groups=mesh['de'=8,'et'=4] {'de'}, dimensions={0} | all-to-all | bytes 245760 | tf_op jit(solution)/shard_map/all_to_all | solution.py:50
  19.6 0.1 all_to_all.30
  19.6 15.4 %all_gather.6 = bf16[40,6144]{1,0:T(8,128)(2,1)S(1)} all-gather(bf16[40,1536]{1,0:T(8,128)(2,1)S(1)} %all_to_all.30), channel_id=1, replica_groups=mesh['de'=8,'et'=4] {'et'}, dimensions={1}, use_global_device_ids=true | all-gather | bytes 614400 | tf_op jit(solution)/shard_map/all_gather | solution.py:53
  35.0 10.4 %fusion.36 = f32[40,2048]{1,0:T(8,128)S(1)} fusion(bf16[40,6144]{1,0:T(8,128)(2,1)S(1)} %all_gather.6, bf16[6144,2048]{1,0:T(8,128)(2,1)} %param.10), kind=kOutput, calls=%fused_computation.56 | convolution fusion | flops 1006632960 | bytes 25985024 | tf_op jit(solution)/shard_map/dot_general | solution.py:55
  45.5 10.5 %fusion.37 = f32[40,2048]{1,0:T(8,128)S(1)} fusion(bf16[40,6144]{1,0:T(8,128)(2,1)S(1)} %all_gather.6, bf16[6144,2048]{1,0:T(8,128)(2,1)} %param.11), kind=kOutput, calls=%fused_computation.57 | convolution fusion | flops 1006632960 | bytes 25985024 | tf_op jit(solution)/shard_map/dot_general | solution.py:56
  56.0 11.3 %convolution_convert_fusion = bf16[40,6144]{1,0:T(8,128)(2,1)} fusion(bf16[2048,6144]{1,0:T(8,128)(2,1)} %param.12, f32[40,2048]{1,0:T(8,128)S(1)} %fusion.37, f32[40,2048]{1,0:T(8,128)S(1)} %fusion.36), kind=kOutput, calls=%fused_computation.2 | convolution fusion | flops 1007370240 | bytes 26312704 | tf_op jit(solution)/shard_map/dot_general | solution.py:62
  67.3 0.0 reduce-scatter.3.cloned.1.call-update
  67.3 21.5 %reduce-scatter.3.cloned.1.call-done = bf16[40,1536]{1,0:T(8,128)(2,1)} async-done(((bf16[40,6144]{1,0:T(8,128)(2,1)}), bf16[40,1536]{1,0:T(8,128)(2,1)}) %reduce-scatter.3.cloned.1.call-update) | async-done | bytes 122896 | tf_op jit(solution)/shard_map/reduce_scatter | solution.py:65
  88.8 1.6 all_to_all.31
  90.4 3.7 %all-to-all-start.1 = ((bf16[8,5,1536]{2,1,0:T(8,128)(2,1)}), bf16[8,5,1536]{2,1,0:T(8,128)(2,1)S(1)}, u32[]{:S(2)}, u32[]{:S(2)}) async-start(bf16[8,5,1536]{2,1,0:T(8,128)(2,1)} %all_to_all.31), calls=%async_computation.2 | async-start | bytes 393216 | tf_op jit(solution)/shard_map/all_to_all | solution.py:73
  94.1 0.0 reduce-scatter.5.cloned.1.call-start
  94.2 6.2 %all-to-all-done.1 = bf16[8,5,1536]{2,1,0:T(8,128)(2,1)S(1)} async-done(((bf16[8,5,1536]{2,1,0:T(8,128)(2,1)}), bf16[8,5,1536]{2,1,0:T(8,128)(2,1)S(1)}, u32[]{:S(2)}, u32[]{:S(2)}) %all-to-all-start.1) | async-done | bytes 122912 | tf_op jit(solution)/shard_map/all_to_all | solution.py:73
  100.4 0.3 fusion.3
  100.7 0.4 convolution_convert_fusion.1
  101.1 8.6 %all_to_all.43 = bf16[8,5,1536]{2,1,0:T(8,128)(2,1)S(1)} all-to-all(bf16[8,5,1536]{2,1,0:T(8,128)(2,1)S(1)} %bitcast.40), channel_id=1, replica_groups=mesh['de'=8,'et'=4] {'de'}, dimensions={0} | all-to-all | bytes 245760 | tf_op jit(solution)/shard_map/all_to_all | solution.py:51
  109.8 0.1 all_to_all.35
  109.8 15.9 %all_gather.7 = bf16[40,6144]{1,0:T(8,128)(2,1)S(1)} all-gather(bf16[40,1536]{1,0:T(8,128)(2,1)S(1)} %all_to_all.35), channel_id=1, replica_groups=mesh['de'=8,'et'=4] {'et'}, dimensions={1}, use_global_device_ids=true | all-gather | bytes 614400 | tf_op jit(solution)/shard_map/all_gather | solution.py:54
  125.7 12.3 %fusion.38 = f32[40,2048]{1,0:T(8,128)S(1)} fusion(bf16[40,6144]{1,0:T(8,128)(2,1)S(1)} %all_gather.7, bf16[2048,6144]{1,0:T(8,128)(2,1)} %param.12), kind=kOutput, calls=%fused_computation.58 | convolution fusion | flops 1006632960 | bytes 25985024 | tf_op jit(solution)/shard_map/dot_general | solution.py:57
  138.0 12.3 %fusion.5 = f32[40,6144]{1,0:T(8,128)S(1)} fusion(bf16[6144,2048]{1,0:T(8,128)(2,1)} %param.10, f32[40,2048]{1,0:T(8,128)S(1)} %fusion.36, f32[40,2048]{1,0:T(8,128)S(1)} %fusion.38, f32[40,2048]{1,0:T(8,128)S(1)} %fusion.37), kind=kOutput, calls=%fused_computation.18 | convolution fusion | flops 1007452160 | bytes 27131904 | tf_op jit(solution)/shard_map/dot_general | solution.py:19
  150.3 13.3 %fusion = bf16[40,6144]{1,0:T(8,128)(2,1)} fusion(f32[40,6144]{1,0:T(8,128)S(1)} %fusion.5, bf16[6144,2048]{1,0:T(8,128)(2,1)} %param.11, f32[40,2048]{1,0:T(8,128)S(1)} %fusion.38, f32[40,2048]{1,0:T(8,128)S(1)} %fusion.36), kind=kOutput, calls=%fused_computation.1 | convolution fusion | flops 1007616000 | bytes 27295744 | tf_op jit(solution)/shard_map/dot_general | solution.py:22
  163.6 0.0 reduce-scatter.5.cloned.1.call-update
  163.6 18.0 %reduce-scatter.5.cloned.1.call-done = bf16[40,1536]{1,0:T(8,128)(2,1)} async-done(((bf16[40,6144]{1,0:T(8,128)(2,1)}), bf16[40,1536]{1,0:T(8,128)(2,1)}) %reduce-scatter.5.cloned.1.call-update) | async-done | bytes 122896 | tf_op jit(solution)/shard_map/reduce_scatter | solution.py:68
  181.6 1.6 all_to_all.36
  183.2 3.8 %all-to-all-start.3 = ((bf16[8,5,1536]{2,1,0:T(8,128)(2,1)}), bf16[8,5,1536]{2,1,0:T(8,128)(2,1)S(1)}, u32[]{:S(2)}, u32[]{:S(2)}) async-start(bf16[8,5,1536]{2,1,0:T(8,128)(2,1)} %all_to_all.36), calls=%async_computation.5 | async-start | bytes 393216 | tf_op jit(solution)/shard_map/all_to_all | solution.py:76
  187.0 0.9 fusion.1
  187.9 9.2 %psum.7 = f32[8,2]{0,1:T(2,128)} all-reduce(f32[8,2]{0,1:T(2,128)S(1)} %get-tuple-element.3), channel_id=1, replica_groups=mesh['de'=8,'et'=4] {'et'}, use_global_device_ids=true, to_apply=%region_9.10 | all-reduce | flops 16 | bytes 128 | tf_op jit(solution)/shard_map/psum | solution.py:88
  197.1 0.9 fusion.2
  (18 shorter events, 0.2 us)
Async XLA Ops:
  7.2 1.0 copy-start
  7.2 81.6 %reduce-scatter.3.cloned.1.call-start = ((), (), s32[]{:S(2)}) async-start(), calls=%async_computation.6 | async-start | bytes 614400 | tf_op jit(solution)/shard_map/reduce_scatter | solution.py:65
  56.0 38.2 %copy-start.2 = (bf16[8,1536]{1,0:T(8,128)(2,1)S(1)}, bf16[8,1536]{1,0:T(8,128)(2,1)}, u32[]{:S(2)}) copy-start(bf16[8,1536]{1,0:T(8,128)(2,1)} %param.13) | copy-start | bytes 73732
  56.0 44.7 %copy-start.3 = (s32[8,2]{0,1:T(2,128)S(1)}, s32[8,2]{0,1:T(2,128)}, u32[]{:S(2)}) copy-start(s32[8,2]{0,1:T(2,128)} %param.8) | copy-start | bytes 196
  56.0 44.7 %copy-start.4 = (f32[8,2]{0,1:T(2,128)S(1)}, f32[8,2]{0,1:T(2,128)}, u32[]{:S(2)}) copy-start(f32[8,2]{0,1:T(2,128)} %param.9) | copy-start | bytes 196
  90.4 9.9 %all-to-all-start.1 = ((bf16[8,5,1536]{2,1,0:T(8,128)(2,1)}), bf16[8,5,1536]{2,1,0:T(8,128)(2,1)S(1)}, u32[]{:S(2)}, u32[]{:S(2)}) async-start(bf16[8,5,1536]{2,1,0:T(8,128)(2,1)} %all_to_all.31), calls=%async_computation.2 | async-start | bytes 393216 | tf_op jit(solution)/shard_map/all_to_all | solution.py:73
  94.1 87.5 %reduce-scatter.5.cloned.1.call-start = ((), (), s32[]{:S(2)}) async-start(), calls=%async_computation.7 | async-start | bytes 614400 | tf_op jit(solution)/shard_map/reduce_scatter | solution.py:68
  138.0 60.0 %copy-start.1 = (bf16[8,1536]{1,0:T(8,128)(2,1)S(1)}, bf16[8,1536]{1,0:T(8,128)(2,1)}, u32[]{:S(2)}) copy-start(bf16[8,1536]{1,0:T(8,128)(2,1)} %param.7) | copy-start | bytes 73732
  183.2 13.8 %all-to-all-start.3 = ((bf16[8,5,1536]{2,1,0:T(8,128)(2,1)}), bf16[8,5,1536]{2,1,0:T(8,128)(2,1)S(1)}, u32[]{:S(2)}, u32[]{:S(2)}) async-start(bf16[8,5,1536]{2,1,0:T(8,128)(2,1)} %all_to_all.36), calls=%async_computation.5 | async-start | bytes 393216 | tf_op jit(solution)/shard_map/all_to_all | solution.py:76
Sparse Core Ops, SparseCore 0:
  67.4 21.3 reduce-scatter.2
  163.7 17.8 reduce-scatter.4
where the time goes:
time: 205 us
  matrix products  72.7 us (35%)
  blocking collectives  60.3 us (29%)
  waiting for transfers between devices  45.7 us (22%)
  between operations  14.2 us (7%)
  starting transfers between devices  7.53 us (4%)
  local copies, waits for them, and re-layouts  3.44 us (2%)
    reduce_scatter x1, waiting for transfers between devices, body(): lax.psum_scatter(y_term.astype(jnp.bfloat16), 'et', scatter_dimension=1,...  21.5 us
    reduce_scatter x1, waiting for transfers between devices, body(): lax.psum_scatter(x_term.astype(jnp.bfloat16), 'et', scatter_dimension=1,...  18 us
    all_gather x1, blocking collectives, body(): g_piece = lax.all_gather(g_recv, 'et', axis=1, tiled=True)  15.9 us
    all_gather x1, blocking collectives, body(): x_piece = lax.all_gather(x_recv, 'et', axis=1, tiled=True)  15.4 us
    dot_general x1, matrix products, input_terms(): lax.dot_general(d_up, w_up, (((1,), (1,)), ((), ())), preferred_element_t...  13.3 us
    dot_general x1, matrix products, input_terms(): lax.dot_general(d_gate, w_gate, (((1,), (1,)), ((), ())), preferred_eleme...  12.3 us
    dot_general x1, matrix products, body(): lax.dot_general(g_piece, w_down, (((1,), (1,)), ((), ())), preferred_elem...  12.3 us
    dot_general x1, matrix products, body(): y_term = jnp.dot(hidden, w_down, preferred_element_type=jnp.float32)  11.3 us
  transfers between devices with their start and end apart: 4, of which 3 were waited for; matrix products, arithmetic and copies ran while one was open for 0% of the time, Pallas kernels for 0%

commit v1 on v0

v1 whole, which is shorter than its diff:
```python
import functools

import jax
import jax.numpy as jnp
from jax import lax
from jax.experimental import pallas as pl
from jax.experimental.pallas import tpu as pltpu
from jax.sharding import PartitionSpec as P

EXPERTS = 4
CAP = 5
BF16 = jnp.bfloat16
F32 = jnp.float32


def dot(a, b):
    return jnp.dot(a, b, preferred_element_type=F32)


def dot_t(a, b):
    return lax.dot_general(a, b, (((1,), (1,)), ((), ())), preferred_element_type=F32)


def expert_kernel(n_et, width, xg_ref, wg_ref, wu_ref, wd_ref, out_ref, score_ref, acc_ref):
    step = pl.program_id(0)
    t = lax.axis_index("et")

    def piece(i):
        start = lax.rem(t + i, n_et) * width
        return pl.ds(pl.multiple_of(start, 128), width)

    gate, up, d_hidden = 0.0, 0.0, 0.0
    for i in range(n_et):
        x, g = xg_ref[i, :, :width], xg_ref[i, :, width:]
        gate += dot(x, wg_ref[piece(i), :])
        up += dot(x, wu_ref[piece(i), :])
        d_hidden += dot_t(g, wd_ref[:, piece(i)])
    sig = jax.nn.sigmoid(gate)
    silu = gate * sig
    hidden = (silu * up).astype(BF16)
    d_gate = (d_hidden * up * sig * (1.0 + gate * (1.0 - sig))).astype(BF16)
    d_up = (d_hidden * silu).astype(BF16)
    score = jnp.sum(hidden.astype(F32) * d_hidden, axis=1, keepdims=True)

    @pl.when(step == 0)
    def _():
        score_ref[...] = jnp.zeros_like(score_ref)
        acc_ref[...] = jnp.zeros_like(acc_ref)

    score_ref[...] += jnp.broadcast_to(score, score_ref.shape)
    for i in range(n_et):
        acc_ref[i, :, :width] += dot(hidden, wd_ref[:, piece(i)])
        acc_ref[i, :, width:] += dot_t(d_gate, wg_ref[piece(i), :]) + dot_t(d_up, wu_ref[piece(i), :])

    @pl.when(step == pl.num_programs(0) - 1)
    def _():
        out_ref[...] = acc_ref[...].astype(BF16)


def experts(n_et, xg, w_gate, w_up, w_down):
    rows, width = xg.shape[1], xg.shape[2] // 2
    d, ff = w_gate.shape
    chunk = min(256, ff)
    return pl.pallas_call(
        functools.partial(expert_kernel, n_et, width),
        grid=(ff // chunk,),
        in_specs=[
            pl.BlockSpec(xg.shape, lambda j: (0, 0, 0)),
            pl.BlockSpec((d, chunk), lambda j: (0, j)),
            pl.BlockSpec((d, chunk), lambda j: (0, j)),
            pl.BlockSpec((chunk, d), lambda j: (j, 0)),
        ],
        out_specs=[
            pl.BlockSpec(xg.shape, lambda j: (0, 0, 0)),
            pl.BlockSpec((rows, 128), lambda j: (0, 0)),
        ],
        out_shape=[
            jax.ShapeDtypeStruct(xg.shape, BF16),
            jax.ShapeDtypeStruct((rows, 128), F32),
        ],
        scratch_shapes=[pltpu.VMEM(xg.shape, F32)],
        compiler_params=pltpu.CompilerParams(vmem_limit_bytes=56 * 2**20),
        cost_estimate=pl.CostEstimate(
            flops=12 * rows * d * ff, bytes_accessed=6 * d * ff, transcendentals=rows * ff
        ),
    )(xg, w_gate, w_up, w_down)


def body(tokens, expert_ids, gate_probs, w_gate, w_up, w_down, out_grad):
    n_de, n_et = lax.axis_size("de"), lax.axis_size("et")
    members = n_de // EXPERTS
    width = tokens.shape[1]
    count = tokens.shape[0]
    q = lax.axis_index("de") // members

    def to_expert(r):
        return [(i, ((i // members) ^ r) * members + i % members) for i in range(n_de)]

    def to_member(k):
        return [(i, i ^ k) for i in range(n_de)]

    def to_slice(i):
        return [(z, (z + i) % n_et) for z in range(n_et)]

    rel = jnp.bitwise_xor(expert_ids, q)
    picks = (rel[:, :, None] == jnp.arange(EXPERTS, dtype=jnp.int32)).astype(F32)
    named = jnp.sum(picks, axis=1)
    weight = jnp.sum(picks * gate_probs[:, :, None], axis=1)
    order = jnp.arange(count)
    before = (order[:, None] > order[None, :]).astype(F32)
    rank = jnp.sum(before[:, :, None] * named[None, :, :], axis=1)
    place = (
        named.T[:, None, :]
        * (rank.T[:, None, :] == jnp.arange(CAP, dtype=F32)[None, :, None]).astype(F32)
    )
    slot_weight = jnp.sum(place * weight.T[:, None, :], axis=2).reshape(EXPERTS * CAP, 1)
    onehot = place.reshape(EXPERTS * CAP, count)
    both = jnp.concatenate([tokens, out_grad], axis=1)
    slots = dot(onehot.astype(BF16), both)
    column = lax.broadcasted_iota(jnp.int32, (1, 2 * width), 1)
    slots = (slots * jnp.where(column < width, 1.0, slot_weight)).astype(BF16)

    mine = [slots[:CAP]] + [
        lax.ppermute(slots[r * CAP : (r + 1) * CAP], "de", to_expert(r)) for r in range(1, EXPERTS)
    ]
    mine = jnp.concatenate(mine, axis=0)
    own = mine.shape[0]
    pieces = [mine] + [lax.ppermute(mine, "et", to_slice(-i)) for i in range(1, n_et)]
    rows = members * own
    pad = -rows % 16
    full = []
    for piece in pieces:
        parts = [piece] + [lax.ppermute(piece, "de", to_member(k)) for k in range(1, members)]
        if pad:
            parts.append(jnp.zeros((pad, 2 * width), BF16))
        full.append(jnp.concatenate(parts, axis=0))
    xg = jnp.stack(full)

    out, score = experts(n_et, xg, w_gate, w_up, w_down)

    high = score[:rows].astype(BF16)
    low = (score[:rows] - high.astype(F32)).astype(BF16)
    lane = lax.broadcasted_iota(jnp.int32, (1, 128), 1)
    tail = jnp.where(lane == 0, high, jnp.where(lane == 1, low, jnp.zeros_like(low)))

    def add_tail(a):
        return jnp.concatenate([a, jnp.broadcast_to(tail, (n_et, rows, 128))], axis=2)

    out = add_tail(out[:, :rows])
    total = out[:, :own].astype(F32)
    for k in range(1, members):
        got = lax.ppermute(out[:, k * own : (k + 1) * own], "de", to_member(k))
        total += got.astype(F32)

    def send_form(a):
        s = a[..., 2 * width : 2 * width + 1] + a[..., 2 * width + 1 : 2 * width + 2]
        hi = s.astype(BF16)
        lo = (s - hi.astype(F32)).astype(BF16)
        end = jnp.where(lane == 0, hi, jnp.where(lane == 1, lo, jnp.zeros_like(lo)))
        return jnp.concatenate([a[..., : 2 * width].astype(BF16), end], axis=-1)

    sent = send_form(total)
    summed = sent[0].astype(F32)
    for i in range(1, n_et):
        summed += lax.ppermute(sent[i], "et", to_slice(i)).astype(F32)
    back = send_form(summed)
    back = [back[:CAP]] + [
        lax.ppermute(back[r * CAP : (r + 1) * CAP], "de", to_expert(r)) for r in range(1, EXPERTS)
    ]
    back = jnp.concatenate(back, axis=0).astype(F32)
    scores = back[:, 2 * width] + back[:, 2 * width + 1]
    highest = lax.Precision.HIGHEST
    mixed = jnp.dot(onehot.T * slot_weight[:, 0], back[:, :width], precision=highest).astype(BF16)
    token_grad = jnp.dot(onehot.T, back[:, width : 2 * width], precision=highest).astype(BF16)
    by_token = jnp.sum(place * scores.reshape(EXPERTS, CAP, 1), axis=1).T / jnp.where(
        named > 0, weight, 1.0
    )
    prob_grad = jnp.sum(picks * by_token[:, None, :], axis=2)
    return (mixed, token_grad, prob_grad)


def solution(mesh):
    return jax.shard_map(
        body,
        mesh=mesh,
        in_specs=(
            P("de", "et"),
            P("de", None),
            P("de", None),
            P(None, ("de", "et")),
            P(None, ("de", "et")),
            P(("de", "et"), None),
            P("de", "et"),
        ),
        out_specs=(P("de", "et"), P("de", "et"), P("de", None)),
        check_vma=False,
    )
```

time: 205 us -> 115 us (0.56)
  matrix products: 72.7 us -> 2.54 us
  blocking collectives: 60.3 us -> 0 us
  Pallas kernels: 0 us -> 53.4 us
  waiting for transfers between devices: 45.7 us -> 30.2 us
  between operations: 14.2 us -> 0.82 us
  starting transfers between devices: 7.53 us -> 20.1 us
  other arithmetic: 0.99 us -> 4.98 us
    dot_general x11 -> x3, matrix products: 72.7 us -> 2.54 us  [the longest x1 1 us: dot(): return jnp.dot(a, b, preferred_element_type=F32)]
    pallas_call x0 -> x1, Pallas kernels: none -> 53.4 us  [experts(): pl.pallas_call(functools.partial(expert_kernel, n_et, width), grid=(ff //...]
    reduce_scatter x2 -> x0, waiting for transfers between devices: 39.5 us -> none  [the longest x1 21.5 us: body(): lax.psum_scatter(y_term.astype(jnp.bfloat16), 'et', scatter_dimension=1,...]
    all_gather x2 -> x0, blocking collectives: 31.3 us -> none  [the longest x1 15.9 us: body(): g_piece = lax.all_gather(g_recv, 'et', axis=1, tiled=True)]
    ppermute x0 -> x17, waiting for transfers between devices: none -> 30.2 us  [the longest x3 13.8 us: body(): summed += lax.ppermute(sent[i], 'et', to_slice(i)).astype(F32)]
    ppermute x0 -> x17, starting transfers between devices: none -> 20.1 us  [the longest x3 5.57 us: body(): lax.ppermute(mine, 'et', to_slice(-i))]
    all_to_all x2 -> x0, blocking collectives: 19.8 us -> none  [the longest x1 11.2 us: body(): lax.all_to_all(x_send, 'de', split_axis=0, concat_axis=0, tiled=True)]
    psum x1 -> x0, blocking collectives: 9.15 us -> none  [body(): prob_grad = lax.psum(partial_grad, 'et')]
  transfers between devices with their start and end apart: 4 -> 17, of which waited for: 3 -> 14; matrix products, arithmetic and copies ran while one was open for 0% -> 1% of each run, Pallas kernels for 0% -> 0%
where the time goes in v1:
time: 115 us
  Pallas kernels  53.4 us (46%)
  waiting for transfers between devices  30.2 us (26%)
  starting transfers between devices  20.1 us (17%)
  other arithmetic  4.98 us (4%)
  local copies, waits for them, and re-layouts  3.24 us (3%)
  matrix products  2.54 us (2%)
    pallas_call x1, Pallas kernels, experts(): pl.pallas_call(functools.partial(expert_kernel, n_et, width), grid=(ff //...  53.4 us
    ppermute x3, waiting for transfers between devices, body(): summed += lax.ppermute(sent[i], 'et', to_slice(i)).astype(F32)  13.8 us
    ppermute x3, waiting for transfers between devices, body(): lax.ppermute(mine, 'et', to_slice(-i))  6.87 us
    ppermute x3, starting transfers between devices, body(): lax.ppermute(mine, 'et', to_slice(-i))  5.57 us
    ppermute x3, starting transfers between devices, body(): summed += lax.ppermute(sent[i], 'et', to_slice(i)).astype(F32)  5.47 us
    ppermute x3, starting transfers between devices, body(): lax.ppermute(slots[r * CAP:(r + 1) * CAP], 'de', to_expert(r))  4.6 us
    ppermute x3, waiting for transfers between devices, body(): lax.ppermute(slots[r * CAP:(r + 1) * CAP], 'de', to_expert(r))  3.95 us
    ppermute x3, waiting for transfers between devices, body(): lax.ppermute(back[r * CAP:(r + 1) * CAP], 'de', to_expert(r))  3.68 us
  transfers between devices with their start and end apart: 17, of which 14 were waited for; matrix products, arithmetic and copies ran while one was open for 1% of the time, Pallas kernels for 0%

profile of v1, /device:TPU:0, one launch (start us, length us, event | category | flops | bytes accessed | tf_op | source)
XLA Modules:
  0.0 115.2 jit_solution(8200317296497608856)
XLA Ops:
  0.8 0.7 broadcast_xor_fusion
  1.4 0.7 convert_reduce_fusion
  3.0 1.0 fusion
  4.0 4.0 %collective-permute-start.2 = (bf16[5,3072]{1,0:T(8,128)(2,1)S(1)}, bf16[5,3072]{1,0:T(8,128)(2,1)S(1)}, u32[]{:S(2)}, u32[]{:S(2)}) collective-permute-start(bf16[5,3072]{1,0:T(8,128)(2,1)S(1)} %get-tuple-element.23), channel_id=1, source_target_pairs={{0,24},{4,28},{8,16},{12,20},{16,8},{20,12},{24,0},{28,4},{1,25},{... | collective-permute-start | bytes 92168 | tf_op jit(solution)/shard_map/ppermute | solution.py:124
  8.0 0.5 collective-permute-start.1
  8.6 1.4 %collective-permute-done.2 = bf16[5,3072]{1,0:T(8,128)(2,1)S(1)} collective-permute-done((bf16[5,3072]{1,0:T(8,128)(2,1)S(1)}, bf16[5,3072]{1,0:T(8,128)(2,1)S(1)}, u32[]{:S(2)}, u32[]{:S(2)}) %collective-permute-start.2) | collective-permute-done | bytes 30752 | tf_op jit(solution)/shard_map/ppermute | solution.py:124
  10.1 2.0 %collective-permute-done.1 = bf16[5,3072]{1,0:T(8,128)(2,1)S(1)} collective-permute-done((bf16[5,3072]{1,0:T(8,128)(2,1)S(1)}, bf16[5,3072]{1,0:T(8,128)(2,1)S(1)}, u32[]{:S(2)}, u32[]{:S(2)}) %collective-permute-start.1) | collective-permute-done | bytes 30752 | tf_op jit(solution)/shard_map/ppermute | solution.py:124
  12.1 0.5 collective-permute-done
  12.7 1.6 %collective-permute-start.8 = (bf16[20,3072]{1,0:T(8,128)(2,1)S(1)}, bf16[20,3072]{1,0:T(8,128)(2,1)S(1)}, u32[]{:S(2)}, u32[]{:S(2)}) collective-permute-start(bf16[20,3072]{1,0:T(8,128)(2,1)S(1)} %pad_maximum_fusion.7), channel_id=1, source_target_pairs={{0,1},{1,2},{2,3},{3,0},{4,5},{5,6},{6,7},{7,4},{8,9},{9,10},{10,1... | collective-permute-start | bytes 368648 | tf_op jit(solution)/shard_map/ppermute | solution.py:128
  14.3 2.6 %collective-permute-start.6 = (bf16[20,3072]{1,0:T(8,128)(2,1)S(1)}, bf16[20,3072]{1,0:T(8,128)(2,1)S(1)}, u32[]{:S(2)}, u32[]{:S(2)}) collective-permute-start(bf16[20,3072]{1,0:T(8,128)(2,1)S(1)} %pad_maximum_fusion.7), channel_id=1, source_target_pairs={{0,2},{1,3},{2,0},{3,1},{4,6},{5,7},{6,4},{7,5},{8,10},{9,11},{10,... | collective-permute-start | bytes 368648 | tf_op jit(solution)/shard_map/ppermute | solution.py:128
  16.9 1.3 %collective-permute-start.4 = (bf16[20,3072]{1,0:T(8,128)(2,1)S(1)}, bf16[20,3072]{1,0:T(8,128)(2,1)S(1)}, u32[]{:S(2)}, u32[]{:S(2)}) collective-permute-start(bf16[20,3072]{1,0:T(8,128)(2,1)S(1)} %pad_maximum_fusion.7), channel_id=1, source_target_pairs={{0,3},{1,0},{2,1},{3,2},{4,7},{5,4},{6,5},{7,6},{8,11},{9,8},{10,9... | collective-permute-start | bytes 368648 | tf_op jit(solution)/shard_map/ppermute | solution.py:128
  18.2 3.2 %collective-permute-done.8 = bf16[20,3072]{1,0:T(8,128)(2,1)S(1)} collective-permute-done((bf16[20,3072]{1,0:T(8,128)(2,1)S(1)}, bf16[20,3072]{1,0:T(8,128)(2,1)S(1)}, u32[]{:S(2)}, u32[]{:S(2)}) %collective-permute-start.8) | collective-permute-done | bytes 122912 | tf_op jit(solution)/shard_map/ppermute | solution.py:128
  21.4 3.7 %collective-permute-done.6 = bf16[20,3072]{1,0:T(8,128)(2,1)S(1)} collective-permute-done((bf16[20,3072]{1,0:T(8,128)(2,1)S(1)}, bf16[20,3072]{1,0:T(8,128)(2,1)S(1)}, u32[]{:S(2)}, u32[]{:S(2)}) %collective-permute-start.6) | collective-permute-done | bytes 122912 | tf_op jit(solution)/shard_map/ppermute | solution.py:128
  25.1 0.5 collective-permute-start.5
  25.6 0.7 concatenate.33
  26.9 1.2 %pad_maximum_fusion.xg_ref = bf16[4,48,3072]{2,1,0:T(8,128)(2,1)} fusion(bf16[1,48,3072]{2,1,0:T(8,128)(2,1)S(1)} %get-tuple-element.28, bf16[1,48,3072]{2,1,0:T(8,128)(2,1)S(1)} %get-tuple-element.27, bf16[1,48,3072]{2,1,0:T(8,128)(2,1)S(1)} %get-tuple-element.26, bf16[1,48,3072]{2,1,0:T(8,128)(2,1)S(1)} %bitcast.28), kind=kLoop, calls=%fused_computation.6 | loop fusion | flops 1769472 | bytes 2359296 | tf_op jit(solution)/shard_map/stack | solution.py:137
  28.0 53.4 %shard_map.94 = (bf16[4,48,3072]{2,1,0:T(8,128)(2,1)}, f32[48,128]{1,0:T(8,128)}) custom-call(bf16[4,48,3072]{2,1,0:T(8,128)(2,1)} %pad_maximum_fusion.xg_ref, bf16[6144,2048]{1,0:T(8,128)(2,1)} %wg_ref.1, bf16[6144,2048]{1,0:T(8,128)(2,1)} %wu_ref.1, bf16[2048,6144]{1,0:T(8,128)(2,1)} %wd_ref.1), custom_call_target="tpu_custom_call" | custom-call | flops 7247757312 | bytes 75497472 | tf_op jit(solution)/shard_map/pallas_call | solution.py:64
  81.4 1.3 %slice.85 = bf16[4,40,3072]{2,1,0:T(8,128)(2,1)S(1)} slice(bf16[4,48,3072]{2,1,0:T(8,128)(2,1)} %get-tuple-element.5), slice={[0:4], [0:40], [0:3072]} | slice | bytes 1966080 | tf_op jit(solution)/shard_map/slice | solution.py:149
  83.5 1.6 %collective-permute-done.10 = bf16[4,20,3200]{2,0,1:T(4,128)(2,1)S(1)} collective-permute-done((bf16[4,20,3200]{2,0,1:T(4,128)(2,1)S(1)}, bf16[4,20,3200]{2,0,1:T(4,128)(2,1)S(1)}, u32[]{:S(2)}, u32[]{:S(2)}) %collective-permute-start.10) | collective-permute-done | bytes 512032 | tf_op jit(solution)/shard_map/ppermute | solution.py:152
  85.6 3.6 %collective-permute-start.11 = (bf16[20,3200]{1,0:T(8,128)(2,1)S(1)}, bf16[20,3200]{1,0:T(8,128)(2,1)S(1)}, u32[]{:S(2)}, u32[]{:S(2)}) collective-permute-start(bf16[20,3200]{1,0:T(8,128)(2,1)S(1)} %get-tuple-element.15), channel_id=1, source_target_pairs={{0,1},{1,2},{2,3},{3,0},{4,5},{5,6},{6,7},{7,4},{8,9},{9,10},{10,1... | collective-permute-start | bytes 384008 | tf_op jit(solution)/shard_map/ppermute | solution.py:165
  89.2 1.3 %collective-permute-start.13 = (bf16[20,3200]{1,0:T(8,128)(2,1)S(1)}, bf16[20,3200]{1,0:T(8,128)(2,1)S(1)}, u32[]{:S(2)}, u32[]{:S(2)}) collective-permute-start(bf16[20,3200]{1,0:T(8,128)(2,1)S(1)} %get-tuple-element.16), channel_id=1, source_target_pairs={{0,3},{1,0},{2,1},{3,2},{4,7},{5,4},{6,5},{7,6},{8,11},{9,8},{10,9... | collective-permute-start | bytes 384008 | tf_op jit(solution)/shard_map/ppermute | solution.py:165
  90.5 0.5 collective-permute-start.12
  91.0 4.2 %collective-permute-done.11 = bf16[20,3200]{1,0:T(8,128)(2,1)S(1)} collective-permute-done((bf16[20,3200]{1,0:T(8,128)(2,1)S(1)}, bf16[20,3200]{1,0:T(8,128)(2,1)S(1)}, u32[]{:S(2)}, u32[]{:S(2)}) %collective-permute-start.11) | collective-permute-done | bytes 128032 | tf_op jit(solution)/shard_map/ppermute | solution.py:165
  95.3 3.0 %collective-permute-done.13 = bf16[20,3200]{1,0:T(8,128)(2,1)S(1)} collective-permute-done((bf16[20,3200]{1,0:T(8,128)(2,1)S(1)}, bf16[20,3200]{1,0:T(8,128)(2,1)S(1)}, u32[]{:S(2)}, u32[]{:S(2)}) %collective-permute-start.13) | collective-permute-done | bytes 128032 | tf_op jit(solution)/shard_map/ppermute | solution.py:165
  98.2 6.6 %collective-permute-done.12 = bf16[20,3200]{1,0:T(8,128)(2,1)S(1)} collective-permute-done((bf16[20,3200]{1,0:T(8,128)(2,1)S(1)}, bf16[20,3200]{1,0:T(8,128)(2,1)S(1)}, u32[]{:S(2)}, u32[]{:S(2)}) %collective-permute-start.12) | collective-permute-done | bytes 128032 | tf_op jit(solution)/shard_map/ppermute | solution.py:165
  105.6 2.7 %collective-permute-start.16 = (bf16[5,3200]{1,0:T(8,128)(2,1)S(1)}, bf16[5,3200]{1,0:T(8,128)(2,1)S(1)}, u32[]{:S(2)}, u32[]{:S(2)}) collective-permute-start(bf16[5,3200]{1,0:T(8,128)(2,1)S(1)} %get-tuple-element.20), channel_id=1, source_target_pairs={{0,24},{4,28},{8,16},{12,20},{16,8},{20,12},{24,0},{28,4},{1,25},{... | collective-permute-start | bytes 96008 | tf_op jit(solution)/shard_map/ppermute | solution.py:168
  108.8 0.7 collective-permute-done.14
  109.5 1.8 %collective-permute-done.16 = bf16[5,3200]{1,0:T(8,128)(2,1)S(1)} collective-permute-done((bf16[5,3200]{1,0:T(8,128)(2,1)S(1)}, bf16[5,3200]{1,0:T(8,128)(2,1)S(1)}, u32[]{:S(2)}, u32[]{:S(2)}) %collective-permute-start.16) | collective-permute-done | bytes 32032 | tf_op jit(solution)/shard_map/ppermute | solution.py:168
  111.2 1.2 %collective-permute-done.15 = bf16[5,3200]{1,0:T(8,128)(2,1)S(1)} collective-permute-done((bf16[5,3200]{1,0:T(8,128)(2,1)S(1)}, bf16[5,3200]{1,0:T(8,128)(2,1)S(1)}, u32[]{:S(2)}, u32[]{:S(2)}) %collective-permute-start.15) | collective-permute-done | bytes 32032 | tf_op jit(solution)/shard_map/ppermute | solution.py:168
  112.5 0.8 convolution_convert_fusion.1
  113.3 0.8 convolution_convert_fusion
  114.6 0.6 select_reduce_fusion
  (54 shorter events, 4.8 us)
Async XLA Ops:
  4.0 6.0 %collective-permute-start.2 = (bf16[5,3072]{1,0:T(8,128)(2,1)S(1)}, bf16[5,3072]{1,0:T(8,128)(2,1)S(1)}, u32[]{:S(2)}, u32[]{:S(2)}) collective-permute-start(bf16[5,3072]{1,0:T(8,128)(2,1)S(1)} %get-tuple-element.23), channel_id=1, source_target_pairs={{0,24},{4,28},{8,16},{12,20},{16,8},{20,12},{24,0},{28,4},{1,25},{... | collective-permute-start | bytes 92168 | tf_op jit(solution)/shard_map/ppermute | solution.py:124
  8.0 4.1 %collective-permute-start.1 = (bf16[5,3072]{1,0:T(8,128)(2,1)S(1)}, bf16[5,3072]{1,0:T(8,128)(2,1)S(1)}, u32[]{:S(2)}, u32[]{:S(2)}) collective-permute-start(bf16[5,3072]{1,0:T(8,128)(2,1)S(1)} %get-tuple-element.24), channel_id=1, source_target_pairs={{0,16},{4,20},{8,24},{12,28},{16,0},{20,4},{24,8},{28,12},{1,17},{... | collective-permute-start | bytes 92168 | tf_op jit(solution)/shard_map/ppermute | solution.py:124
  8.5 4.1 %collective-permute-start = (bf16[5,3072]{1,0:T(8,128)(2,1)S(1)}, bf16[5,3072]{1,0:T(8,128)(2,1)S(1)}, u32[]{:S(2)}, u32[]{:S(2)}) collective-permute-start(bf16[5,3072]{1,0:T(8,128)(2,1)S(1)} %get-tuple-element.25), channel_id=1, source_target_pairs={{0,8},{4,12},{8,0},{12,4},{16,24},{20,28},{24,16},{28,20},{1,9},{5... | collective-permute-start | bytes 92168 | tf_op jit(solution)/shard_map/ppermute | solution.py:124
  12.7 8.7 %collective-permute-start.8 = (bf16[20,3072]{1,0:T(8,128)(2,1)S(1)}, bf16[20,3072]{1,0:T(8,128)(2,1)S(1)}, u32[]{:S(2)}, u32[]{:S(2)}) collective-permute-start(bf16[20,3072]{1,0:T(8,128)(2,1)S(1)} %pad_maximum_fusion.7), channel_id=1, source_target_pairs={{0,1},{1,2},{2,3},{3,0},{4,5},{5,6},{6,7},{7,4},{8,9},{9,10},{10,1... | collective-permute-start | bytes 368648 | tf_op jit(solution)/shard_map/ppermute | solution.py:128
  14.3 10.8 %collective-permute-start.6 = (bf16[20,3072]{1,0:T(8,128)(2,1)S(1)}, bf16[20,3072]{1,0:T(8,128)(2,1)S(1)}, u32[]{:S(2)}, u32[]{:S(2)}) collective-permute-start(bf16[20,3072]{1,0:T(8,128)(2,1)S(1)} %pad_maximum_fusion.7), channel_id=1, source_target_pairs={{0,2},{1,3},{2,0},{3,1},{4,6},{5,7},{6,4},{7,5},{8,10},{9,11},{10,... | collective-permute-start | bytes 368648 | tf_op jit(solution)/shard_map/ppermute | solution.py:128
  16.9 8.2 %collective-permute-start.4 = (bf16[20,3072]{1,0:T(8,128)(2,1)S(1)}, bf16[20,3072]{1,0:T(8,128)(2,1)S(1)}, u32[]{:S(2)}, u32[]{:S(2)}) collective-permute-start(bf16[20,3072]{1,0:T(8,128)(2,1)S(1)} %pad_maximum_fusion.7), channel_id=1, source_target_pairs={{0,3},{1,0},{2,1},{3,2},{4,7},{5,4},{6,5},{7,6},{8,11},{9,8},{10,9... | collective-permute-start | bytes 368648 | tf_op jit(solution)/shard_map/ppermute | solution.py:128
  18.2 7.4 %collective-permute-start.3 = (bf16[20,3072]{1,0:T(8,128)(2,1)S(1)}, bf16[20,3072]{1,0:T(8,128)(2,1)S(1)}, u32[]{:S(2)}, u32[]{:S(2)}) collective-permute-start(bf16[20,3072]{1,0:T(8,128)(2,1)S(1)} %pad_maximum_fusion.7), channel_id=1, source_target_pairs={{0,4},{4,0},{8,12},{12,8},{16,20},{20,16},{24,28},{28,24},{1,5},{5... | collective-permute-start | bytes 368648 | tf_op jit(solution)/shard_map/ppermute | solution.py:133
  21.4 5.0 %collective-permute-start.9 = (bf16[20,3072]{1,0:T(8,128)(2,1)S(1)}, bf16[20,3072]{1,0:T(8,128)(2,1)S(1)}, u32[]{:S(2)}, u32[]{:S(2)}) collective-permute-start(bf16[20,3072]{1,0:T(8,128)(2,1)S(1)} %collective-permute-done.8), channel_id=1, source_target_pairs={{0,4},{4,0},{8,12},{12,8},{16,20},{20,16},{24,28},{28,24},{1,5},{5... | collective-permute-start | bytes 368648 | tf_op jit(solution)/shard_map/ppermute | solution.py:133
  25.1 1.4 %collective-permute-start.7 = (bf16[20,3072]{1,0:T(8,128)(2,1)S(1)}, bf16[20,3072]{1,0:T(8,128)(2,1)S(1)}, u32[]{:S(2)}, u32[]{:S(2)}) collective-permute-start(bf16[20,3072]{1,0:T(8,128)(2,1)S(1)} %collective-permute-done.6), channel_id=1, source_target_pairs={{0,4},{4,0},{8,12},{12,8},{16,20},{20,16},{24,28},{28,24},{1,5},{5... | collective-permute-start | bytes 368648 | tf_op jit(solution)/shard_map/ppermute | solution.py:133
  25.1 1.6 %collective-permute-start.5 = (bf16[20,3072]{1,0:T(8,128)(2,1)S(1)}, bf16[20,3072]{1,0:T(8,128)(2,1)S(1)}, u32[]{:S(2)}, u32[]{:S(2)}) collective-permute-start(bf16[20,3072]{1,0:T(8,128)(2,1)S(1)} %collective-permute-done.4), channel_id=1, source_target_pairs={{0,4},{4,0},{8,12},{12,8},{16,20},{20,16},{24,28},{28,24},{1,5},{5... | collective-permute-start | bytes 368648 | tf_op jit(solution)/shard_map/ppermute | solution.py:133
  81.4 1.3 %copy-start = (f32[48,128]{1,0:T(8,128)S(1)}, f32[48,128]{1,0:T(8,128)}, u32[]{:S(2)}) copy-start(f32[48,128]{1,0:T(8,128)} %get-tuple-element.6) | copy-start | bytes 73732
  83.1 2.0 %collective-permute-start.10 = (bf16[4,20,3200]{2,0,1:T(4,128)(2,1)S(1)}, bf16[4,20,3200]{2,0,1:T(4,128)(2,1)S(1)}, u32[]{:S(2)}, u32[]{:S(2)}) collective-permute-start(bf16[4,20,3200]{2,0,1:T(4,128)(2,1)S(1)} %copy.29), channel_id=1, source_target_pairs={{0,4},{4,0},{8,12},{12,8},{16,20},{20,16},{24,28},{28,24},{1,5},{5... | collective-permute-start | bytes 1536008 | tf_op jit(solution)/shard_map/ppermute | solution.py:152
  85.6 9.7 %collective-permute-start.11 = (bf16[20,3200]{1,0:T(8,128)(2,1)S(1)}, bf16[20,3200]{1,0:T(8,128)(2,1)S(1)}, u32[]{:S(2)}, u32[]{:S(2)}) collective-permute-start(bf16[20,3200]{1,0:T(8,128)(2,1)S(1)} %get-tuple-element.15), channel_id=1, source_target_pairs={{0,1},{1,2},{2,3},{3,0},{4,5},{5,6},{6,7},{7,4},{8,9},{9,10},{10,1... | collective-permute-start | bytes 384008 | tf_op jit(solution)/shard_map/ppermute | solution.py:165
  89.2 9.0 %collective-permute-start.13 = (bf16[20,3200]{1,0:T(8,128)(2,1)S(1)}, bf16[20,3200]{1,0:T(8,128)(2,1)S(1)}, u32[]{:S(2)}, u32[]{:S(2)}) collective-permute-start(bf16[20,3200]{1,0:T(8,128)(2,1)S(1)} %get-tuple-element.16), channel_id=1, source_target_pairs={{0,3},{1,0},{2,1},{3,2},{4,7},{5,4},{6,5},{7,6},{8,11},{9,8},{10,9... | collective-permute-start | bytes 384008 | tf_op jit(solution)/shard_map/ppermute | solution.py:165
  90.5 14.3 %collective-permute-start.12 = (bf16[20,3200]{1,0:T(8,128)(2,1)S(1)}, bf16[20,3200]{1,0:T(8,128)(2,1)S(1)}, u32[]{:S(2)}, u32[]{:S(2)}) collective-permute-start(bf16[20,3200]{1,0:T(8,128)(2,1)S(1)} %get-tuple-element.17), channel_id=1, source_target_pairs={{0,2},{1,3},{2,0},{3,1},{4,6},{5,7},{6,4},{7,5},{8,10},{9,11},{10,... | collective-permute-start | bytes 384008 | tf_op jit(solution)/shard_map/ppermute | solution.py:165
  105.2 4.3 %collective-permute-start.14 = (bf16[5,3200]{1,0:T(8,128)(2,1)S(1)}, bf16[5,3200]{1,0:T(8,128)(2,1)S(1)}, u32[]{:S(2)}, u32[]{:S(2)}) collective-permute-start(bf16[5,3200]{1,0:T(8,128)(2,1)S(1)} %get-tuple-element.19), channel_id=1, source_target_pairs={{0,8},{4,12},{8,0},{12,4},{16,24},{20,28},{24,16},{28,20},{1,9},{5... | collective-permute-start | bytes 96008 | tf_op jit(solution)/shard_map/ppermute | solution.py:168
  105.6 5.6 %collective-permute-start.16 = (bf16[5,3200]{1,0:T(8,128)(2,1)S(1)}, bf16[5,3200]{1,0:T(8,128)(2,1)S(1)}, u32[]{:S(2)}, u32[]{:S(2)}) collective-permute-start(bf16[5,3200]{1,0:T(8,128)(2,1)S(1)} %get-tuple-element.20), channel_id=1, source_target_pairs={{0,24},{4,28},{8,16},{12,20},{16,8},{20,12},{24,0},{28,4},{1,25},{... | collective-permute-start | bytes 96008 | tf_op jit(solution)/shard_map/ppermute | solution.py:168
  108.3 4.1 %collective-permute-start.15 = (bf16[5,3200]{1,0:T(8,128)(2,1)S(1)}, bf16[5,3200]{1,0:T(8,128)(2,1)S(1)}, u32[]{:S(2)}, u32[]{:S(2)}) collective-permute-start(bf16[5,3200]{1,0:T(8,128)(2,1)S(1)} %get-tuple-element.21), channel_id=1, source_target_pairs={{0,16},{4,20},{8,24},{12,28},{16,0},{20,4},{24,8},{28,12},{1,17},{... | collective-permute-start | bytes 96008 | tf_op jit(solution)/shard_map/ppermute | solution.py:168

commit v2 on v1

v2 whole, which is shorter than its diff:
```python
import functools

import jax
import jax.numpy as jnp
from jax import lax
from jax.experimental import pallas as pl
from jax.experimental.pallas import tpu as pltpu
from jax.sharding import PartitionSpec as P

EXPERTS = 4
CAP = 5
BF16 = jnp.bfloat16
F32 = jnp.float32


def dot(a, b):
    return jnp.dot(a, b, preferred_element_type=F32)


def dot_t(a, b):
    return lax.dot_general(a, b, (((1,), (1,)), ((), ())), preferred_element_type=F32)


def expert_kernel(n_et, width, xg_ref, wg_ref, wu_ref, wd_ref, out_ref, score_ref, acc_ref):
    step = pl.program_id(0)
    t = lax.axis_index("et")

    def piece(i):
        start = jnp.bitwise_xor(t, i) * width
        return pl.ds(pl.multiple_of(start, 128), width)

    gate, up, d_hidden = 0.0, 0.0, 0.0
    for i in range(n_et):
        x, g = xg_ref[i, :, :width], xg_ref[i, :, width:]
        gate += dot(x, wg_ref[piece(i), :])
        up += dot(x, wu_ref[piece(i), :])
        d_hidden += dot_t(g, wd_ref[:, piece(i)])
    sig = jax.nn.sigmoid(gate)
    silu = gate * sig
    hidden = (silu * up).astype(BF16)
    d_gate = (d_hidden * up * sig * (1.0 + gate * (1.0 - sig))).astype(BF16)
    d_up = (d_hidden * silu).astype(BF16)
    score = jnp.sum(hidden.astype(F32) * d_hidden, axis=1, keepdims=True)

    @pl.when(step == 0)
    def _():
        score_ref[...] = jnp.zeros_like(score_ref)
        acc_ref[...] = jnp.zeros_like(acc_ref)

    score_ref[...] += jnp.broadcast_to(score, score_ref.shape)
    for i in range(n_et):
        acc_ref[i, :, :width] += dot(hidden, wd_ref[:, piece(i)])
        acc_ref[i, :, width:] += dot_t(d_gate, wg_ref[piece(i), :]) + dot_t(d_up, wu_ref[piece(i), :])

    @pl.when(step == pl.num_programs(0) - 1)
    def _():
        out_ref[...] = acc_ref[...].astype(BF16)


def experts(n_et, xg, w_gate, w_up, w_down):
    rows, width = xg.shape[1], xg.shape[2] // 2
    d, ff = w_gate.shape
    chunk = min(256, ff)
    return pl.pallas_call(
        functools.partial(expert_kernel, n_et, width),
        grid=(ff // chunk,),
        in_specs=[
            pl.BlockSpec(xg.shape, lambda j: (0, 0, 0)),
            pl.BlockSpec((d, chunk), lambda j: (0, j)),
            pl.BlockSpec((d, chunk), lambda j: (0, j)),
            pl.BlockSpec((chunk, d), lambda j: (j, 0)),
        ],
        out_specs=[
            pl.BlockSpec(xg.shape, lambda j: (0, 0, 0)),
            pl.BlockSpec((rows, 128), lambda j: (0, 0)),
        ],
        out_shape=[
            jax.ShapeDtypeStruct(xg.shape, BF16),
            jax.ShapeDtypeStruct((rows, 128), F32),
        ],
        scratch_shapes=[pltpu.VMEM(xg.shape, F32)],
        compiler_params=pltpu.CompilerParams(vmem_limit_bytes=56 * 2**20),
        cost_estimate=pl.CostEstimate(
            flops=12 * rows * d * ff, bytes_accessed=6 * d * ff, transcendentals=rows * ff
        ),
    )(xg, w_gate, w_up, w_down)


TILE = 256
GROUP = 4


def tiles_fit(members, rows, n_et, width, ff):
    sent = n_et * CAP + -(n_et * CAP) % 8
    if members * EXPERTS * sent > TILE or n_et * rows > TILE:
        return False
    return rows <= 128 and members == 2 and width % TILE == 0 and ff % (2 * TILE) == 0 and n_et * (width // TILE) % (2 * GROUP) == 0


def sorter(n_et, members, rows, sent, turned):
    shape = (TILE, TILE)
    to = lax.broadcasted_iota(jnp.int32, shape, turned)
    at = lax.broadcasted_iota(jnp.int32, shape, 1 - turned)
    hit = jnp.zeros(shape, F32)
    for i in range(n_et):
        for k in range(members * EXPERTS):
            there, here = to - (i * rows + k * CAP), at - (k * sent + i * CAP)
            hit = jnp.where((there == here) & (there >= 0) & (there < CAP), 1.0, hit)
    return hit.astype(BF16)


def select_kernel(width, pick_ref, scale_ref, *refs):
    pieces, outs = refs[: len(refs) - EXPERTS], refs[len(refs) - EXPERTS :]
    sent = outs[0].shape[0]
    pick = pick_ref[...]
    for half in (0, 1):
        cols = slice(half * width, (half + 1) * width)
        raw = jnp.concatenate([p[:, cols].astype(F32) for p in pieces], axis=0).astype(BF16)
        block = dot(pick, raw)
        if half:
            block = block * scale_ref[...]
        for r in range(EXPERTS):
            outs[r][:, cols] = block[r * sent : (r + 1) * sent].astype(BF16)


def select(pick, scale, pieces):
    sent = pick.shape[0] // EXPERTS
    out = jax.ShapeDtypeStruct((sent, pieces[0].shape[1]), BF16)
    return pl.pallas_call(
        functools.partial(select_kernel, pieces[0].shape[1] // 2),
        out_shape=[out] * EXPERTS,
        compiler_params=pltpu.CompilerParams(vmem_limit_bytes=16 * 2**20),
    )(pick, scale, *pieces)


def combine_kernel(width, count, pick_ref, named_ref, scale_ref, *refs):
    parts, outs = refs[:EXPERTS], refs[EXPERTS:]
    highest = lax.Precision.HIGHEST
    for side in (0, 1):
        cols = slice(side * width, (side + 1) * width)
        block = jnp.concatenate([p[:, cols].astype(F32) for p in parts], axis=0)
        if side == 0:
            block = block * scale_ref[...]
        block = jnp.dot(pick_ref[...], block, precision=highest, preferred_element_type=F32)
        for i, out in enumerate(outs):
            out[:, cols] = block[i * count : (i + 1) * count].astype(BF16)
    tail = jnp.concatenate([p[:, 2 * width :].astype(F32) for p in parts], axis=0)
    scores = jnp.dot(named_ref[...], tail, precision=highest, preferred_element_type=F32)
    lane = lax.broadcasted_iota(jnp.int32, (count, 128), 1)
    ends = jnp.where(lane == 0, scores[:count], scores[count:])
    for out in outs:
        out[:, 2 * width :] = ends.astype(BF16)


def combine(count, n_et, pick, named, scale, parts):
    columns = parts[0].shape[1]
    out = jax.ShapeDtypeStruct((count, columns), BF16)
    return pl.pallas_call(
        functools.partial(combine_kernel, (columns - 128) // 2, count),
        out_shape=[out] * n_et,
        compiler_params=pltpu.CompilerParams(vmem_limit_bytes=24 * 2**20),
    )(pick, named, scale, *parts)


def tiled_kernel(n_et, width, members, accs, *refs):
    wg_hbm, wu_hbm, wd_hbm = refs[:3]
    parts = refs[3 : 3 + EXPERTS * members]
    (out_ref, sib_ref, xg_ref, wg_buf, wu_buf, wd_buf, gt_ref, h_ref, dg_ref, du_ref, dgt_ref, dut_ref,
     y_ref, dx_ref, dxt_ref, score_ref, sems) = refs[3 + EXPERTS * members :]
    t = lax.axis_index("et")
    rows = xg_ref.shape[1]
    chunk = 2 * TILE
    steps = wg_hbm.shape[1] // chunk
    per = width // TILE
    tiles = n_et * per

    def piece(i):
        start = jnp.bitwise_xor(t, i) * width
        return pl.ds(pl.multiple_of(start, 128), width)

    def at(k):
        return pl.ds(pl.multiple_of(k * TILE, TILE), TILE)

    def turned(a):
        pad = jnp.zeros((128 - rows, a.shape[1]), F32)
        return jnp.concatenate([a, pad], axis=0).T

    def copies(c, slot, i):
        cols = pl.ds(pl.multiple_of(c * chunk, chunk), chunk)
        d = piece(i)
        return (
            pltpu.make_async_copy(wd_hbm.at[cols, d], wd_buf.at[slot, :, d], sems.at[slot, i, 0]),
            pltpu.make_async_copy(wg_hbm.at[d, cols], wg_buf.at[slot, d, :], sems.at[slot, i, 1]),
            pltpu.make_async_copy(wu_hbm.at[d, cols], wu_buf.at[slot, d, :], sems.at[slot, i, 2]),
        )

    def fetch(c, slot):
        for i in range(n_et):
            for copy in copies(c, slot, i):
                copy.start()

    fetch(0, 0)
    score_ref[...] = jnp.zeros_like(score_ref)
    y_ref[...] = jnp.zeros_like(y_ref)
    dx_ref[...] = jnp.zeros_like(dx_ref)
    dxt_ref[...] = jnp.zeros_like(dxt_ref)
    gt_ref[:, 128:] = jnp.zeros((gt_ref.shape[0], 128), BF16)
    dgt_ref[:, 128:] = jnp.zeros((2 * TILE, 128), BF16)
    dut_ref[:, 128:] = jnp.zeros((2 * TILE, 128), BF16)
    sent = parts[0].shape[0]

    def inner(wide0, wide1, a0, a1, b0, b1):
        wide, first, second = (wide0, wide1), (a0, a1), (b0, b1)

        def sort(m, a, block):
            pltpu.matmul_push_rhs(block, 0, m)
            pltpu.matmul_acc_lhs(wide[m], a, load_staged_rhs=0)
            return pltpu.matmul_pop(wide[m])

        shuffle = sorter(n_et, members, rows, sent, 0)
        below = jnp.zeros((TILE - members * EXPERTS * sent, TILE), F32)
        for u in range(2 * per):
            cols = slice(u * TILE, (u + 1) * TILE)
            block = jnp.concatenate([p[:, cols].astype(F32) for p in parts] + [below], axis=0)
            block = sort(u % 2, shuffle, block.astype(BF16))
            for i in range(n_et):
                some = block[i * rows : (i + 1) * rows]
                xg_ref[i, :, cols] = some.astype(BF16)
                if u >= per:
                    gt_ref[at(i * per + u - per), :128] = turned(some).astype(BF16)

        @pl.loop(0, steps)
        def _(c):
            slot = lax.rem(c, 2)

            @pl.when(c + 1 < steps)
            def _():
                fetch(c + 1, 1 - slot)

            wg_ref, wu_ref, wd_ref = wg_buf.at[slot], wu_buf.at[slot], wd_buf.at[slot]
            one_chunk(c, slot, wide, first, second, wg_ref, wu_ref, wd_ref)

        @pl.loop(0, tiles // GROUP)
        def _(g):
            for j in range(GROUP - 1):
                d = at(g * GROUP + j)
                dx_ref[:, d] = dxt_ref[d, :].T[:rows]

        back = sorter(n_et, members, rows, sent, 1)
        half = EXPERTS * sent
        below = jnp.zeros((TILE - n_et * rows, TILE), F32)
        for u in range(2 * per):
            source, v = (y_ref, u) if u < per else (dx_ref, u - per)
            cols = slice(u * TILE, (u + 1) * TILE)
            block = [source[:, at(jnp.bitwise_xor(t, i) * per + v)] for i in range(n_et)]
            block = jnp.concatenate(block + [below], axis=0)
            block = sort(u % 2, back, block.astype(BF16)).astype(BF16)
            out_ref[:, cols] = block[:half]
            sib_ref[:, cols] = block[half : 2 * half]
        block = jnp.concatenate([score_ref[...]] * n_et + [below[:, :128]], axis=0)
        block = jnp.concatenate([block, block], axis=1)
        block = sort(0, back, block.astype(BF16)).astype(BF16)
        out_ref[:, 2 * width :] = block[:half, :128]
        sib_ref[:, 2 * width :] = block[half : 2 * half, :128]

    def one_chunk(c, slot, wide, first, second, wg_ref, wu_ref, wd_ref):
        @pl.loop(0, n_et)
        def _(i):
            for copy in copies(c, slot, i):
                copy.wait()
            turn = 0
            for u in range(per):
                k = at(jnp.bitwise_xor(t, i) * per + u)
                kg = at(i * per + u)
                x = xg_ref[i, :, u * TILE : (u + 1) * TILE]
                for what in range(3):
                    s = turn % 2
                    turn += 1
                    for m in (0, 1):
                        block = slice(m * TILE, (m + 1) * TILE)
                        if what == 0:
                            pltpu.matmul_push_rhs(gt_ref[kg, :], s, m)
                            pltpu.matmul_acc_lhs(wide[m], wd_ref[block, k], load_staged_rhs=s)
                        elif what == 1:
                            pltpu.matmul_push_rhs(wg_ref[k, block], s, m)
                            pltpu.matmul_acc_lhs(first[m], x, load_staged_rhs=s)
                        else:
                            pltpu.matmul_push_rhs(wu_ref[k, block], s, m)
                            pltpu.matmul_acc_lhs(second[m], x, load_staged_rhs=s)

        score = jnp.zeros((rows, 1), F32)
        for m in (0, 1):
            block = slice(m * TILE, (m + 1) * TILE)
            gate, up = pltpu.matmul_pop(first[m]), pltpu.matmul_pop(second[m])
            d_hidden = pltpu.matmul_pop(wide[m])[:, :128].T[:rows]
            sig = jax.nn.sigmoid(gate)
            silu = gate * sig
            hidden = (silu * up).astype(BF16)
            d_gate = d_hidden * up * sig * (1.0 + gate * (1.0 - sig))
            d_up = d_hidden * silu
            score += jnp.sum(hidden.astype(F32) * d_hidden, axis=1, keepdims=True)
            h_ref[:, block] = hidden
            dg_ref[:, block] = d_gate.astype(BF16)
            du_ref[:, block] = d_up.astype(BF16)
            dgt_ref[block, :128] = turned(d_gate).astype(BF16)
            dut_ref[block, :128] = turned(d_up).astype(BF16)
        score_ref[...] += jnp.broadcast_to(score, score_ref.shape)

        @pl.loop(0, tiles // (2 * GROUP))
        def _(pair):
            def plan(m):
                base = (2 * pair + m) * GROUP
                y_ops, long_ops, short_ops = [], [], []

                def y_op(d, kt, s):
                    ks = slice(kt * TILE, (kt + 1) * TILE)
                    pltpu.matmul_push_rhs(wd_ref[ks, d], s, m)
                    pltpu.matmul_acc_lhs(first[m], h_ref[:, ks], load_staged_rhs=s)

                def y_end(d):
                    y_ref[:, d] += pltpu.matmul_pop(first[m])

                def long_op(d, w, a, kt, s):
                    ks = slice(kt * TILE, (kt + 1) * TILE)
                    pltpu.matmul_push_rhs(a[ks, :], s, m)
                    pltpu.matmul_acc_lhs(wide[m], w[d, ks], load_staged_rhs=s)

                def long_end(d):
                    dxt_ref[d, :] += pltpu.matmul_pop(wide[m])[:, :128]

                def short_op(d, w, a, kt, s):
                    ks = slice(kt * TILE, (kt + 1) * TILE)
                    pltpu.matmul_push_rhs(w[d, ks], s, m, transpose=True)
                    pltpu.matmul_acc_lhs(second[m], a[:, ks], load_staged_rhs=s)

                def short_end(d):
                    dx_ref[:, d] += pltpu.matmul_pop(second[m])

                for j in range(GROUP):
                    d = at(base + j)
                    for kt in (0, 1):
                        y_ops.append((functools.partial(y_op, d, kt), functools.partial(y_end, d) if kt else None))
                    if j < GROUP - 1:
                        ops, op, end, sides = long_ops, long_op, long_end, ((wg_ref, dgt_ref), (wu_ref, dut_ref))
                    else:
                        ops, op, end, sides = short_ops, short_op, short_end, ((wg_ref, dg_ref), (wu_ref, du_ref))
                    for side, (w, a) in enumerate(sides):
                        for kt in (0, 1):
                            last = side == 1 and kt == 1
                            ops.append((functools.partial(op, d, w, a, kt), functools.partial(end, d) if last else None))
                lists, taken, order = (long_ops, y_ops, short_ops), [0, 0, 0], []
                total = sum(len(l) for l in lists)
                for i in range(total):
                    open_lists = [n for n in range(3) if taken[n] < len(lists[n])]
                    best = max(open_lists, key=lambda n: (i + 1) * len(lists[n]) / total - taken[n])
                    order.append(lists[best][taken[best]])
                    taken[best] += 1
                return order

            for i, both in enumerate(zip(plan(0), plan(1))):
                for op, _ in both:
                    op(i % 2)
                for _, end in both:
                    if end is not None:
                        end()

    pl.run_scoped(inner, *accs)


def tiled_experts(mesh, n_et, members, parts, w_gate, w_up, w_down):
    sent, width = parts[0].shape[0], parts[0].shape[1] // 2
    rows = members * EXPERTS * CAP + -(members * EXPERTS * CAP) % 16
    d, ff = w_gate.shape
    chunk = 2 * TILE
    with jax.sharding.use_abstract_mesh(mesh.abstract_mesh):
        accs = [pltpu.ACC(m)((n, TILE), F32) for n in (TILE, rows, rows) for m in (0, 1)]
    vmem, hbm = pl.BlockSpec(memory_space=pltpu.VMEM), pl.BlockSpec(memory_space=pl.ANY)
    out = jax.ShapeDtypeStruct((EXPERTS * sent, 2 * width + 128), BF16)
    return pl.pallas_call(
        functools.partial(tiled_kernel, n_et, width, members, accs),
        in_specs=[hbm] * 3 + [vmem] * len(parts),
        out_specs=[vmem, vmem],
        out_shape=[out, out],
        scratch_shapes=[
            pltpu.VMEM((n_et, rows, 2 * width), BF16),
            pltpu.VMEM((2, d, chunk), BF16),
            pltpu.VMEM((2, d, chunk), BF16),
            pltpu.VMEM((2, chunk, d), BF16),
            pltpu.VMEM((d, TILE), BF16),
            pltpu.VMEM((rows, chunk), BF16),
            pltpu.VMEM((rows, chunk), BF16),
            pltpu.VMEM((rows, chunk), BF16),
            pltpu.VMEM((chunk, TILE), BF16),
            pltpu.VMEM((chunk, TILE), BF16),
            pltpu.VMEM((rows, d), F32),
            pltpu.VMEM((rows, d), F32),
            pltpu.VMEM((d, 128), F32),
            pltpu.VMEM((rows, 128), F32),
            pltpu.SemaphoreType.DMA((2, n_et, 3)),
        ],
        compiler_params=pltpu.CompilerParams(vmem_limit_bytes=56 * 2**20),
        cost_estimate=pl.CostEstimate(
            flops=12 * rows * d * ff, bytes_accessed=6 * d * ff, transcendentals=rows * ff
        ),
    )(w_gate, w_up, w_down, *parts)


def body(mesh, tokens, expert_ids, gate_probs, w_gate, w_up, w_down, out_grad):
    n_de, n_et = lax.axis_size("de"), lax.axis_size("et")
    members = n_de // EXPERTS
    width = tokens.shape[1]
    count = tokens.shape[0]
    top = expert_ids.shape[1]
    q = lax.axis_index("de") // members

    def to_expert(r):
        return [(i, ((i // members) ^ r) * members + i % members) for i in range(n_de)]

    def to_member(k):
        return [(i, i ^ k) for i in range(n_de)]

    def to_slice(i):
        return [(z, z ^ i) for z in range(n_et)]

    both = jnp.concatenate([tokens, out_grad], axis=1)
    pieces = [both] + [lax.ppermute(both, "et", to_slice(i)) for i in range(1, n_et)]

    rel = jnp.bitwise_xor(expert_ids, q)
    picks = (rel[:, :, None] == jnp.arange(EXPERTS, dtype=jnp.int32)).astype(F32)
    named = jnp.sum(picks, axis=1)
    weight = jnp.sum(picks * gate_probs[:, :, None], axis=1)
    order = jnp.arange(count)
    before = (order[:, None] > order[None, :]).astype(F32)
    rank = jnp.sum(before[:, :, None] * named[None, :, :], axis=1)
    place = (
        named.T[:, None, :]
        * (rank.T[:, None, :] == jnp.arange(CAP, dtype=F32)[None, :, None]).astype(F32)
    )
    slot_weight = jnp.sum(place * weight.T[:, None, :], axis=2)
    used = n_et * CAP
    sent = used + -used % 8

    def padded(a, axis):
        return jnp.pad(a, [(0, sent - used if d == axis else 0) for d in range(a.ndim)])

    same = jnp.eye(n_et, dtype=F32)
    pick = place[:, None, :, None, :] * same[None, :, None, :, None]
    pick = padded(pick.reshape(EXPERTS, used, n_et * count), 1).reshape(EXPERTS * sent, n_et * count)
    scale = jnp.broadcast_to(slot_weight[:, None, :], (EXPERTS, n_et, CAP)).reshape(EXPERTS, used)
    scale = padded(scale, 1).reshape(EXPERTS * sent, 1)
    first = place * picks.transpose(1, 2, 0)[:, :, None, :]
    first = jnp.pad(first, [(0, 0), (0, 0), (0, sent - CAP), (0, 0)])
    first = first.transpose(0, 3, 1, 2).reshape(top * count, EXPERTS * sent)

    rows_of = select(pick.astype(BF16), scale, pieces)
    mine = [rows_of[0]] + [lax.ppermute(rows_of[r], "de", to_expert(r)) for r in range(1, EXPERTS)]
    parts = mine + [
        lax.ppermute(a, "de", to_member(k)) for k in range(1, members) for a in mine
    ]
    rows = members * EXPERTS * CAP
    pad = -rows % 16
    if tiles_fit(members, rows + pad, n_et, width, w_gate.shape[1]):
        kept, *others = tiled_experts(mesh, n_et, members, parts, w_gate, w_up, w_down)
    else:
        xg = jnp.stack(parts)[:, :used].reshape(members * EXPERTS, n_et, CAP, 2 * width)
        xg = xg.transpose(1, 0, 2, 3).reshape(n_et, rows, 2 * width)
        xg = jnp.pad(xg, [(0, 0), (0, pad), (0, 0)])
        out, score = experts(n_et, xg, w_gate, w_up, w_down)
        score = jnp.broadcast_to(score[:rows].astype(BF16), (n_et, rows, 128))
        out = jnp.concatenate([out[:, :rows], score], axis=2)
        out = out.reshape(n_et, members, EXPERTS, CAP, 2 * width + 128).transpose(1, 2, 0, 3, 4)
        out = padded(out.reshape(members, EXPERTS, used, 2 * width + 128), 2)
        kept, *others = out.reshape(members, EXPERTS * sent, 2 * width + 128)

    total = kept.astype(F32)
    for k, other in enumerate(others, 1):
        total += lax.ppermute(other, "de", to_member(k)).astype(F32)
    back = [total[r * sent : (r + 1) * sent].astype(BF16) for r in range(EXPERTS)]
    back = [back[0]] + [lax.ppermute(back[r], "de", to_expert(r)) for r in range(1, EXPERTS)]
    ends = combine(count, n_et, pick.T, first, scale, back)
    result = ends[0].astype(F32)
    for i in range(1, n_et):
        result += lax.ppermute(ends[i], "et", to_slice(i)).astype(F32)
    mixed = result[:, :width].astype(BF16)
    token_grad = result[:, width : 2 * width].astype(BF16)
    prob_grad = result[:, 2 * width : 2 * width + top] / gate_probs
    return (mixed, token_grad, prob_grad)


def solution(mesh):
    return jax.shard_map(
        functools.partial(body, mesh),
        mesh=mesh,
        in_specs=(
            P("de", "et"),
            P("de", None),
            P("de", None),
            P(None, ("de", "et")),
            P(None, ("de", "et")),
            P(("de", "et"), None),
            P("de", "et"),
        ),
        out_specs=(P("de", "et"), P("de", "et"), P("de", None)),
        check_vma=False,
    )
```

time: 115 us -> 88.7 us (0.77)
  Pallas kernels: 53.4 us -> 40.9 us
  waiting for transfers between devices: 30.2 us -> 20.6 us
  matrix products: 2.54 us -> 0 us
  starting transfers between devices: 20.1 us -> 17.9 us
  other arithmetic: 4.98 us -> 2.98 us
  local copies, waits for them, and re-layouts: 3.24 us -> 5.11 us
    pallas_call x1 -> x3, Pallas kernels: 53.4 us -> 40.9 us  [the longest x1 40 us: tiled_experts(): pl.pallas_call(functools.partial(tiled_kernel, n_et, width, members, accs...]
    ppermute x17, waiting for transfers between devices: 30.2 us -> 20.6 us  [the longest x3 6.1 us: body(): lax.ppermute(back[r], 'de', to_expert(r))]
    unnamed x2 -> x24, local copies, waits for them, and re-layouts: 0.01 us -> 2.67 us
    dot_general x3 -> x0, matrix products: 2.54 us -> none  [the longest x1 1 us: dot(): return jnp.dot(a, b, preferred_element_type=F32)]
    ppermute x17, starting transfers between devices: 20.1 us -> 17.9 us  [the longest x3 5.62 us: body(): lax.ppermute(both, 'et', to_slice(i))]
  transfers between devices with their start and end apart: 17 -> 17, of which waited for: 14 -> 11; matrix products, arithmetic and copies ran while one was open for 1% -> 3% of each run, Pallas kernels for 0% -> 0%
where the time goes in v2:
time: 88.7 us; the launch traced here: 88.4 us
  Pallas kernels  40.9 us (46%)
  waiting for transfers between devices  20.6 us (23%)
  starting transfers between devices  17.9 us (20%)
  local copies, waits for them, and re-layouts  5.11 us (6%)
  other arithmetic  2.98 us (3%)
    pallas_call x1, Pallas kernels, tiled_experts(): pl.pallas_call(functools.partial(tiled_kernel, n_et, width, members, accs...  40 us
    ppermute x3, waiting for transfers between devices, body(): lax.ppermute(back[r], 'de', to_expert(r))  6.1 us
    ppermute x3, waiting for transfers between devices, body(): lax.ppermute(rows_of[r], 'de', to_expert(r))  5.69 us
    ppermute x3, starting transfers between devices, body(): lax.ppermute(both, 'et', to_slice(i))  5.62 us
    ppermute x3, starting transfers between devices, body(): result += lax.ppermute(ends[i], 'et', to_slice(i)).astype(F32)  4.45 us
    ppermute x3, starting transfers between devices, body(): lax.ppermute(rows_of[r], 'de', to_expert(r))  3.55 us
    ppermute x3, starting transfers between devices, body(): lax.ppermute(back[r], 'de', to_expert(r))  3.55 us
    ppermute x3, waiting for transfers between devices, body(): lax.ppermute(both, 'et', to_slice(i))  3.3 us
  transfers between devices with their start and end apart: 17, of which 11 were waited for; matrix products, arithmetic and copies ran while one was open for 3% of the time, Pallas kernels for 0%

profile of v2, /device:TPU:0, one launch (start us, length us, event | category | flops | bytes accessed | tf_op | source)
XLA Modules:
  0.0 88.4 jit_solution(143117088055714879)
XLA Ops:
  0.6 0.7 constant_dynamic-update-slice_fusion.1
  1.4 0.7 constant_dynamic-update-slice_fusion.refs_0_
  2.1 3.0 %collective-permute-start = (bf16[8,3072]{1,0:T(8,128)(2,1)S(1)}, bf16[8,3072]{1,0:T(8,128)(2,1)S(1)}, u32[]{:S(2)}, u32[]{:S(2)}) collective-permute-start(bf16[8,3072]{1,0:T(8,128)(2,1)S(1)} %constant_dynamic-update-slice_fusion.refs_0_), channel_id=1, source_target_pairs={{0,1},{1,0},{2,3},{3,2},{4,5},{5,4},{6,7},{7,6},{8,9},{9,8},{10,11... | collective-permute-start | bytes 147464 | tf_op jit(solution)/shard_map/ppermute | solution.py:426
  5.1 2.6 %collective-permute-start.1 = (bf16[8,3072]{1,0:T(8,128)(2,1)S(1)}, bf16[8,3072]{1,0:T(8,128)(2,1)S(1)}, u32[]{:S(2)}, u32[]{:S(2)}) collective-permute-start(bf16[8,3072]{1,0:T(8,128)(2,1)S(1)} %constant_dynamic-update-slice_fusion.refs_0_), channel_id=1, source_target_pairs={{0,2},{1,3},{2,0},{3,1},{4,6},{5,7},{6,4},{7,5},{8,10},{9,11},{10,... | collective-permute-start | bytes 147464 | tf_op jit(solution)/shard_map/ppermute | solution.py:426
  7.8 0.7 broadcast_xor_fusion
  8.4 0.7 select_reduce_fusion
  10.3 0.7 collective-permute-done.1.refs_2_
  11.1 2.6 %collective-permute-done.2.refs_3_ = bf16[8,3072]{1,0:T(8,128)(2,1)S(1)} collective-permute-done((bf16[8,3072]{1,0:T(8,128)(2,1)S(1)}, bf16[8,3072]{1,0:T(8,128)(2,1)S(1)}, u32[]{:S(2)}, u32[]{:S(2)}) %collective-permute-start.2) | collective-permute-done | bytes 49184 | tf_op jit(solution)/shard_map/ppermute | solution.py:426
  13.6 0.3 shard_map.94
  13.9 1.6 %collective-permute-start.3 = (bf16[24,3072]{1,0:T(8,128)(2,1)S(1)}, bf16[24,3072]{1,0:T(8,128)(2,1)S(1)}, u32[]{:S(2)}, u32[]{:S(2)}) collective-permute-start(bf16[24,3072]{1,0:T(8,128)(2,1)S(1)} %get-tuple-element.14), channel_id=1, source_target_pairs={{0,8},{4,12},{8,0},{12,4},{16,24},{20,28},{24,16},{28,20},{1,9},{5... | collective-permute-start | bytes 442376 | tf_op jit(solution)/shard_map/ppermute | solution.py:456
  15.5 1.5 %collective-permute-start.4 = (bf16[24,3072]{1,0:T(8,128)(2,1)S(1)}, bf16[24,3072]{1,0:T(8,128)(2,1)S(1)}, u32[]{:S(2)}, u32[]{:S(2)}) collective-permute-start(bf16[24,3072]{1,0:T(8,128)(2,1)S(1)} %get-tuple-element.15), channel_id=1, source_target_pairs={{0,16},{4,20},{8,24},{12,28},{16,0},{20,4},{24,8},{28,12},{1,17},{... | collective-permute-start | bytes 442376 | tf_op jit(solution)/shard_map/ppermute | solution.py:456
  17.0 0.5 collective-permute-start.5
  17.5 2.9 %collective-permute-done.3.refs_4_ = bf16[24,3072]{1,0:T(8,128)(2,1)S(1)} collective-permute-done((bf16[24,3072]{1,0:T(8,128)(2,1)S(1)}, bf16[24,3072]{1,0:T(8,128)(2,1)S(1)}, u32[]{:S(2)}, u32[]{:S(2)}) %collective-permute-start.3) | collective-permute-done | bytes 147488 | tf_op jit(solution)/shard_map/ppermute | solution.py:456
  20.4 2.8 %collective-permute-done.4.refs_5_ = bf16[24,3072]{1,0:T(8,128)(2,1)S(1)} collective-permute-done((bf16[24,3072]{1,0:T(8,128)(2,1)S(1)}, bf16[24,3072]{1,0:T(8,128)(2,1)S(1)}, u32[]{:S(2)}, u32[]{:S(2)}) %collective-permute-start.4) | collective-permute-done | bytes 147488 | tf_op jit(solution)/shard_map/ppermute | solution.py:456
  23.2 0.5 collective-permute-start.9
  23.7 0.8 collective-permute-done.8.refs_9_
  24.8 0.4 copy-done.6
  25.2 0.7 copy-done.7
  25.9 40.0 %shard_map.95 = (bf16[96,3200]{1,0:T(8,128)(2,1)}, bf16[96,3200]{1,0:T(8,128)(2,1)}) custom-call(bf16[6144,2048]{1,0:T(8,128)(2,1)} %refs_0_.1, bf16[6144,2048]{1,0:T(8,128)(2,1)} %refs_1_.1, bf16[2048,6144]{1,0:T(8,128)(2,1)} %refs_2_.1, bf16[24,3072]{1,0:T(8,128)(2,1)} %copy-done, bf16[24,3072]{1,0:T(8,128)(2,1)} %copy-done.1, bf16[24,3072]{1,0:T(8,128)(2,1)} %copy-done.2, ...), custom_call_target="tpu_custom_call" | custom-call | flops 7247757312 | bytes 75497472 | tf_op jit(solution)/shard_map/pallas_call | solution.py:379
  66.2 1.9 %collective-permute-done.10 = bf16[96,3200]{1,0:T(8,128)(2,1)S(1)} collective-permute-done((bf16[96,3200]{1,0:T(8,128)(2,1)}, bf16[96,3200]{1,0:T(8,128)(2,1)S(1)}, u32[]{:S(2)}, u32[]{:S(2)}) %collective-permute-start.10) | collective-permute-done | bytes 614432 | tf_op jit(solution)/shard_map/ppermute | solution.py:477
  68.1 1.2 %add_convert_fusion = bf16[96,3200]{1,0:T(8,128)(2,1)S(1)} fusion(bf16[96,3200]{1,0:T(8,128)(2,1)S(1)} %collective-permute-done.10, bf16[96,3200]{1,0:T(8,128)(2,1)} %get-tuple-element.17), kind=kLoop, calls=%fused_computation | loop fusion | flops 1228800 | bytes 1843200 | tf_op jit(solution)/shard_map/convert.5
  69.5 1.2 %collective-permute-start.12 = (bf16[24,3200]{1,0:T(8,128)(2,1)S(1)}, bf16[24,3200]{1,0:T(8,128)(2,1)S(1)}, u32[]{:S(2)}, u32[]{:S(2)}) collective-permute-start(bf16[24,3200]{1,0:T(8,128)(2,1)S(1)} %get-tuple-element.43), channel_id=1, source_target_pairs={{0,16},{4,20},{8,24},{12,28},{16,0},{20,4},{24,8},{28,12},{1,17},{... | collective-permute-start | bytes 460808 | tf_op jit(solution)/shard_map/ppermute | solution.py:479
  70.7 2.3 %collective-permute-start.13 = (bf16[24,3200]{1,0:T(8,128)(2,1)S(1)}, bf16[24,3200]{1,0:T(8,128)(2,1)S(1)}, u32[]{:S(2)}, u32[]{:S(2)}) collective-permute-start(bf16[24,3200]{1,0:T(8,128)(2,1)S(1)} %get-tuple-element.42), channel_id=1, source_target_pairs={{0,24},{4,28},{8,16},{12,20},{16,8},{20,12},{24,0},{28,4},{1,25},{... | collective-permute-start | bytes 460808 | tf_op jit(solution)/shard_map/ppermute | solution.py:479
  73.1 3.1 %collective-permute-done.11.refs_1_ = bf16[24,3200]{1,0:T(8,128)(2,1)S(1)} collective-permute-done((bf16[24,3200]{1,0:T(8,128)(2,1)S(1)}, bf16[24,3200]{1,0:T(8,128)(2,1)S(1)}, u32[]{:S(2)}, u32[]{:S(2)}) %collective-permute-start.11) | collective-permute-done | bytes 153632 | tf_op jit(solution)/shard_map/ppermute | solution.py:479
  76.3 2.9 %collective-permute-done.13.refs_3_ = bf16[24,3200]{1,0:T(8,128)(2,1)S(1)} collective-permute-done((bf16[24,3200]{1,0:T(8,128)(2,1)S(1)}, bf16[24,3200]{1,0:T(8,128)(2,1)S(1)}, u32[]{:S(2)}, u32[]{:S(2)}) %collective-permute-start.13) | collective-permute-done | bytes 153632 | tf_op jit(solution)/shard_map/ppermute | solution.py:479
  79.2 0.7 shard_map.96
  80.0 1.2 %collective-permute-start.16 = (bf16[8,3200]{1,0:T(8,128)(2,1)S(1)}, bf16[8,3200]{1,0:T(8,128)(2,1)S(1)}, u32[]{:S(2)}, u32[]{:S(2)}) collective-permute-start(bf16[8,3200]{1,0:T(8,128)(2,1)S(1)} %get-tuple-element.22), channel_id=1, source_target_pairs={{0,3},{1,2},{2,1},{3,0},{4,7},{5,6},{6,5},{7,4},{8,11},{9,10},{10,... | collective-permute-start | bytes 153608 | tf_op jit(solution)/shard_map/ppermute | solution.py:483
  81.2 3.2 %collective-permute-start.14 = (bf16[8,3200]{1,0:T(8,128)(2,1)S(1)}, bf16[8,3200]{1,0:T(8,128)(2,1)S(1)}, u32[]{:S(2)}, u32[]{:S(2)}) collective-permute-start(bf16[8,3200]{1,0:T(8,128)(2,1)S(1)} %get-tuple-element.20), channel_id=1, source_target_pairs={{0,1},{1,0},{2,3},{3,2},{4,5},{5,4},{6,7},{7,6},{8,9},{9,8},{10,11... | collective-permute-start | bytes 153608 | tf_op jit(solution)/shard_map/ppermute | solution.py:483
  84.5 1.5 %collective-permute-done.16 = bf16[8,3200]{1,0:T(8,128)(2,1)S(1)} collective-permute-done((bf16[8,3200]{1,0:T(8,128)(2,1)S(1)}, bf16[8,3200]{1,0:T(8,128)(2,1)S(1)}, u32[]{:S(2)}, u32[]{:S(2)}) %collective-permute-start.16) | collective-permute-done | bytes 51232 | tf_op jit(solution)/shard_map/ppermute | solution.py:483
  86.0 1.1 %collective-permute-done.15 = bf16[8,3200]{1,0:T(8,128)(2,1)S(1)} collective-permute-done((bf16[8,3200]{1,0:T(8,128)(2,1)S(1)}, bf16[8,3200]{1,0:T(8,128)(2,1)S(1)}, u32[]{:S(2)}, u32[]{:S(2)}) %collective-permute-start.15) | collective-permute-done | bytes 51232 | tf_op jit(solution)/shard_map/ppermute | solution.py:483
  87.1 0.6 fusion.6
  87.7 0.6 copy.53
  (61 shorter events, 2.2 us)
Async XLA Ops:
  2.1 8.2 %collective-permute-start = (bf16[8,3072]{1,0:T(8,128)(2,1)S(1)}, bf16[8,3072]{1,0:T(8,128)(2,1)S(1)}, u32[]{:S(2)}, u32[]{:S(2)}) collective-permute-start(bf16[8,3072]{1,0:T(8,128)(2,1)S(1)} %constant_dynamic-update-slice_fusion.refs_0_), channel_id=1, source_target_pairs={{0,1},{1,0},{2,3},{3,2},{4,5},{5,4},{6,7},{7,6},{8,9},{9,8},{10,11... | collective-permute-start | bytes 147464 | tf_op jit(solution)/shard_map/ppermute | solution.py:426
  5.1 5.9 %collective-permute-start.1 = (bf16[8,3072]{1,0:T(8,128)(2,1)S(1)}, bf16[8,3072]{1,0:T(8,128)(2,1)S(1)}, u32[]{:S(2)}, u32[]{:S(2)}) collective-permute-start(bf16[8,3072]{1,0:T(8,128)(2,1)S(1)} %constant_dynamic-update-slice_fusion.refs_0_), channel_id=1, source_target_pairs={{0,2},{1,3},{2,0},{3,1},{4,6},{5,7},{6,4},{7,5},{8,10},{9,11},{10,... | collective-permute-start | bytes 147464 | tf_op jit(solution)/shard_map/ppermute | solution.py:426
  7.7 5.9 %collective-permute-start.2 = (bf16[8,3072]{1,0:T(8,128)(2,1)S(1)}, bf16[8,3072]{1,0:T(8,128)(2,1)S(1)}, u32[]{:S(2)}, u32[]{:S(2)}) collective-permute-start(bf16[8,3072]{1,0:T(8,128)(2,1)S(1)} %constant_dynamic-update-slice_fusion.refs_0_), channel_id=1, source_target_pairs={{0,3},{1,2},{2,1},{3,0},{4,7},{5,6},{6,5},{7,4},{8,11},{9,10},{10,... | collective-permute-start | bytes 147464 | tf_op jit(solution)/shard_map/ppermute | solution.py:426
  13.9 10.9 %copy-start = (bf16[24,3072]{1,0:T(8,128)(2,1)}, bf16[24,3072]{1,0:T(8,128)(2,1)S(1)}, u32[]{:S(2)}) copy-start(bf16[24,3072]{1,0:T(8,128)(2,1)S(1)} %get-tuple-element.13.refs_3_) | copy-start | bytes 442372
  13.9 6.4 %collective-permute-start.3 = (bf16[24,3072]{1,0:T(8,128)(2,1)S(1)}, bf16[24,3072]{1,0:T(8,128)(2,1)S(1)}, u32[]{:S(2)}, u32[]{:S(2)}) collective-permute-start(bf16[24,3072]{1,0:T(8,128)(2,1)S(1)} %get-tuple-element.14), channel_id=1, source_target_pairs={{0,8},{4,12},{8,0},{12,4},{16,24},{20,28},{24,16},{28,20},{1,9},{5... | collective-permute-start | bytes 442376 | tf_op jit(solution)/shard_map/ppermute | solution.py:456
  15.5 7.7 %collective-permute-start.4 = (bf16[24,3072]{1,0:T(8,128)(2,1)S(1)}, bf16[24,3072]{1,0:T(8,128)(2,1)S(1)}, u32[]{:S(2)}, u32[]{:S(2)}) collective-permute-start(bf16[24,3072]{1,0:T(8,128)(2,1)S(1)} %get-tuple-element.15), channel_id=1, source_target_pairs={{0,16},{4,20},{8,24},{12,28},{16,0},{20,4},{24,8},{28,12},{1,17},{... | collective-permute-start | bytes 442376 | tf_op jit(solution)/shard_map/ppermute | solution.py:456
  17.0 6.2 %collective-permute-start.5 = (bf16[24,3072]{1,0:T(8,128)(2,1)S(1)}, bf16[24,3072]{1,0:T(8,128)(2,1)S(1)}, u32[]{:S(2)}, u32[]{:S(2)}) collective-permute-start(bf16[24,3072]{1,0:T(8,128)(2,1)S(1)} %get-tuple-element.16), channel_id=1, source_target_pairs={{0,24},{4,28},{8,16},{12,20},{16,8},{20,12},{24,0},{28,4},{1,25},{... | collective-permute-start | bytes 442376 | tf_op jit(solution)/shard_map/ppermute | solution.py:456
  17.5 48.7 %copy-start.8 = (s32[8,2]{0,1:T(2,128)S(1)}, s32[8,2]{0,1:T(2,128)}, u32[]{:S(2)}) copy-start(s32[8,2]{0,1:T(2,128)} %param.8) | copy-start | bytes 196
  17.5 66.9 %copy-start.9 = (f32[8,2]{0,1:T(2,128)S(1)}, f32[8,2]{0,1:T(2,128)}, u32[]{:S(2)}) copy-start(f32[8,2]{0,1:T(2,128)} %param.9) | copy-start | bytes 196
  17.5 6.2 %collective-permute-start.6 = (bf16[24,3072]{1,0:T(8,128)(2,1)S(1)}, bf16[24,3072]{1,0:T(8,128)(2,1)S(1)}, u32[]{:S(2)}, u32[]{:S(2)}) collective-permute-start(bf16[24,3072]{1,0:T(8,128)(2,1)S(1)} %get-tuple-element.13.refs_3_), channel_id=1, source_target_pairs={{0,4},{4,0},{8,12},{12,8},{16,20},{20,16},{24,28},{28,24},{1,5},{5... | collective-permute-start | bytes 442376 | tf_op jit(solution)/shard_map/ppermute | solution.py:458
  20.4 4.4 %copy-start.1 = (bf16[24,3072]{1,0:T(8,128)(2,1)}, bf16[24,3072]{1,0:T(8,128)(2,1)S(1)}, u32[]{:S(2)}) copy-start(bf16[24,3072]{1,0:T(8,128)(2,1)S(1)} %collective-permute-done.3.refs_4_) | copy-start | bytes 442372
  20.4 3.3 %collective-permute-start.7 = (bf16[24,3072]{1,0:T(8,128)(2,1)S(1)}, bf16[24,3072]{1,0:T(8,128)(2,1)S(1)}, u32[]{:S(2)}, u32[]{:S(2)}) collective-permute-start(bf16[24,3072]{1,0:T(8,128)(2,1)S(1)} %collective-permute-done.3.refs_4_), channel_id=1, source_target_pairs={{0,4},{4,0},{8,12},{12,8},{16,20},{20,16},{24,28},{28,24},{1,5},{5... | collective-permute-start | bytes 442376 | tf_op jit(solution)/shard_map/ppermute | solution.py:458
  23.2 1.6 %copy-start.2 = (bf16[24,3072]{1,0:T(8,128)(2,1)}, bf16[24,3072]{1,0:T(8,128)(2,1)S(1)}, u32[]{:S(2)}) copy-start(bf16[24,3072]{1,0:T(8,128)(2,1)S(1)} %collective-permute-done.4.refs_5_) | copy-start | bytes 442372
  23.2 1.4 %collective-permute-start.8 = (bf16[24,3072]{1,0:T(8,128)(2,1)S(1)}, bf16[24,3072]{1,0:T(8,128)(2,1)S(1)}, u32[]{:S(2)}, u32[]{:S(2)}) collective-permute-start(bf16[24,3072]{1,0:T(8,128)(2,1)S(1)} %collective-permute-done.4.refs_5_), channel_id=1, source_target_pairs={{0,4},{4,0},{8,12},{12,8},{16,20},{20,16},{24,28},{28,24},{1,5},{5... | collective-permute-start | bytes 442376 | tf_op jit(solution)/shard_map/ppermute | solution.py:458
  23.2 1.6 %copy-start.3 = (bf16[24,3072]{1,0:T(8,128)(2,1)}, bf16[24,3072]{1,0:T(8,128)(2,1)S(1)}, u32[]{:S(2)}) copy-start(bf16[24,3072]{1,0:T(8,128)(2,1)S(1)} %collective-permute-done.5.refs_6_) | copy-start | bytes 442372
  23.2 1.6 %collective-permute-start.9 = (bf16[24,3072]{1,0:T(8,128)(2,1)S(1)}, bf16[24,3072]{1,0:T(8,128)(2,1)S(1)}, u32[]{:S(2)}, u32[]{:S(2)}) collective-permute-start(bf16[24,3072]{1,0:T(8,128)(2,1)S(1)} %collective-permute-done.5.refs_6_), channel_id=1, source_target_pairs={{0,4},{4,0},{8,12},{12,8},{16,20},{20,16},{24,28},{28,24},{1,5},{5... | collective-permute-start | bytes 442376 | tf_op jit(solution)/shard_map/ppermute | solution.py:458
  23.7 1.1 %copy-start.4 = (bf16[24,3072]{1,0:T(8,128)(2,1)}, bf16[24,3072]{1,0:T(8,128)(2,1)S(1)}, u32[]{:S(2)}) copy-start(bf16[24,3072]{1,0:T(8,128)(2,1)S(1)} %collective-permute-done.6.refs_7_) | copy-start | bytes 442372
  23.7 1.1 %copy-start.5 = (bf16[24,3072]{1,0:T(8,128)(2,1)}, bf16[24,3072]{1,0:T(8,128)(2,1)S(1)}, u32[]{:S(2)}) copy-start(bf16[24,3072]{1,0:T(8,128)(2,1)S(1)} %collective-permute-done.7.refs_8_) | copy-start | bytes 442372
  24.5 0.7 copy-start.6
  25.2 0.7 copy-start.7
  65.8 2.3 %collective-permute-start.10 = (bf16[96,3200]{1,0:T(8,128)(2,1)}, bf16[96,3200]{1,0:T(8,128)(2,1)S(1)}, u32[]{:S(2)}, u32[]{:S(2)}) collective-permute-start(bf16[96,3200]{1,0:T(8,128)(2,1)} %get-tuple-element.18), channel_id=1, source_target_pairs={{0,4},{4,0},{8,12},{12,8},{16,20},{20,16},{24,28},{28,24},{1,5},{5... | collective-permute-start | bytes 1843208 | tf_op jit(solution)/shard_map/ppermute | solution.py:477
  69.4 6.9 %collective-permute-start.11 = (bf16[24,3200]{1,0:T(8,128)(2,1)S(1)}, bf16[24,3200]{1,0:T(8,128)(2,1)S(1)}, u32[]{:S(2)}, u32[]{:S(2)}) collective-permute-start(bf16[24,3200]{1,0:T(8,128)(2,1)S(1)} %get-tuple-element.44), channel_id=1, source_target_pairs={{0,8},{4,12},{8,0},{12,4},{16,24},{20,28},{24,16},{28,20},{1,9},{5... | collective-permute-start | bytes 460808 | tf_op jit(solution)/shard_map/ppermute | solution.py:479
  69.5 6.8 %collective-permute-start.12 = (bf16[24,3200]{1,0:T(8,128)(2,1)S(1)}, bf16[24,3200]{1,0:T(8,128)(2,1)S(1)}, u32[]{:S(2)}, u32[]{:S(2)}) collective-permute-start(bf16[24,3200]{1,0:T(8,128)(2,1)S(1)} %get-tuple-element.43), channel_id=1, source_target_pairs={{0,16},{4,20},{8,24},{12,28},{16,0},{20,4},{24,8},{28,12},{1,17},{... | collective-permute-start | bytes 460808 | tf_op jit(solution)/shard_map/ppermute | solution.py:479
  70.7 8.5 %collective-permute-start.13 = (bf16[24,3200]{1,0:T(8,128)(2,1)S(1)}, bf16[24,3200]{1,0:T(8,128)(2,1)S(1)}, u32[]{:S(2)}, u32[]{:S(2)}) collective-permute-start(bf16[24,3200]{1,0:T(8,128)(2,1)S(1)} %get-tuple-element.42), channel_id=1, source_target_pairs={{0,24},{4,28},{8,16},{12,20},{16,8},{20,12},{24,0},{28,4},{1,25},{... | collective-permute-start | bytes 460808 | tf_op jit(solution)/shard_map/ppermute | solution.py:479
  80.0 6.1 %collective-permute-start.16 = (bf16[8,3200]{1,0:T(8,128)(2,1)S(1)}, bf16[8,3200]{1,0:T(8,128)(2,1)S(1)}, u32[]{:S(2)}, u32[]{:S(2)}) collective-permute-start(bf16[8,3200]{1,0:T(8,128)(2,1)S(1)} %get-tuple-element.22), channel_id=1, source_target_pairs={{0,3},{1,2},{2,1},{3,0},{4,7},{5,6},{6,5},{7,4},{8,11},{9,10},{10,... | collective-permute-start | bytes 153608 | tf_op jit(solution)/shard_map/ppermute | solution.py:483
  81.2 5.9 %collective-permute-start.15 = (bf16[8,3200]{1,0:T(8,128)(2,1)S(1)}, bf16[8,3200]{1,0:T(8,128)(2,1)S(1)}, u32[]{:S(2)}, u32[]{:S(2)}) collective-permute-start(bf16[8,3200]{1,0:T(8,128)(2,1)S(1)} %get-tuple-element.21), channel_id=1, source_target_pairs={{0,2},{1,3},{2,0},{3,1},{4,6},{5,7},{6,4},{7,5},{8,10},{9,11},{10,... | collective-permute-start | bytes 153608 | tf_op jit(solution)/shard_map/ppermute | solution.py:483
  81.2 5.9 %collective-permute-start.14 = (bf16[8,3200]{1,0:T(8,128)(2,1)S(1)}, bf16[8,3200]{1,0:T(8,128)(2,1)S(1)}, u32[]{:S(2)}, u32[]{:S(2)}) collective-permute-start(bf16[8,3200]{1,0:T(8,128)(2,1)S(1)} %get-tuple-element.20), channel_id=1, source_target_pairs={{0,1},{1,0},{2,3},{3,2},{4,5},{5,4},{6,7},{7,6},{8,9},{9,8},{10,11... | collective-permute-start | bytes 153608 | tf_op jit(solution)/shard_map/ppermute | solution.py:483

commit v3 on v2

--- a/solution.py
+++ b/solution.py
@@ -209,8 +209,8 @@
     dut_ref[:, 128:] = jnp.zeros((2 * TILE, 128), BF16)
     sent = parts[0].shape[0]
 
-    def inner(wide0, wide1, a0, a1, b0, b1):
-        wide, first, second = (wide0, wide1), (a0, a1), (b0, b1)
+    def inner(wide0, wide1, spare0, spare1, a0, a1, b0, b1):
+        wide, spare, first, second = (wide0, wide1), (spare0, spare1), (a0, a1), (b0, b1)
 
         def sort(m, a, block):
             pltpu.matmul_push_rhs(block, 0, m)
@@ -229,22 +229,18 @@
                 if u >= per:
                     gt_ref[at(i * per + u - per), :128] = turned(some).astype(BF16)
 
-        @pl.loop(0, steps)
+        def chunk_at(c, last):
+            slot = lax.rem(c, 2)
+            if not last:
+                fetch(c + 1, 1 - slot)
+            wg_ref, wu_ref, wd_ref = wg_buf.at[slot], wu_buf.at[slot], wd_buf.at[slot]
+            one_chunk(c, slot, last, wide, spare, first, second, wg_ref, wu_ref, wd_ref)
+
+        @pl.loop(0, steps - 1)
         def _(c):
-            slot = lax.rem(c, 2)
-
-            @pl.when(c + 1 < steps)
-            def _():
-                fetch(c + 1, 1 - slot)
-
-            wg_ref, wu_ref, wd_ref = wg_buf.at[slot], wu_buf.at[slot], wd_buf.at[slot]
-            one_chunk(c, slot, wide, first, second, wg_ref, wu_ref, wd_ref)
-
-        @pl.loop(0, tiles // GROUP)
-        def _(g):
-            for j in range(GROUP - 1):
-                d = at(g * GROUP + j)
-                dx_ref[:, d] = dxt_ref[d, :].T[:rows]
+            chunk_at(c, False)
+
+        chunk_at(steps - 1, True)
 
         back = sorter(n_et, members, rows, sent, 1)
         half = EXPERTS * sent
@@ -263,7 +259,7 @@
         out_ref[:, 2 * width :] = block[:half, :128]
         sib_ref[:, 2 * width :] = block[half : 2 * half, :128]
 
-    def one_chunk(c, slot, wide, first, second, wg_ref, wu_ref, wd_ref):
+    def one_chunk(c, slot, last, wide, spare, first, second, wg_ref, wu_ref, wd_ref):
         @pl.loop(0, n_et)
         def _(i):
             for copy in copies(c, slot, i):
@@ -288,45 +284,68 @@
                             pltpu.matmul_push_rhs(wu_ref[k, block], s, m)
                             pltpu.matmul_acc_lhs(second[m], x, load_staged_rhs=s)
 
+        gates, backs = [], []
+        for m in (0, 1):
+            gate, up = pltpu.matmul_pop(first[m]), pltpu.matmul_pop(second[m])
+            backs.append(pltpu.matmul_pop(wide[m])[:, :128])
+            sig = jax.nn.sigmoid(gate)
+            silu = gate * sig
+            hidden = (silu * up).astype(BF16)
+            h_ref[:, m * TILE : (m + 1) * TILE] = hidden
+            gates.append((gate, up, sig, silu, hidden))
+
+        def y_tile(j):
+            d, m, acc = slice(j * TILE, (j + 1) * TILE), j % 2, (first, second)[j // 2 % 2]
+            for kt in (0, 1):
+                ks = slice(kt * TILE, (kt + 1) * TILE)
+                pltpu.matmul_push_rhs(wd_ref[ks, d], kt, m)
+                pltpu.matmul_acc_lhs(acc[m], h_ref[:, ks], load_staged_rhs=kt)
+            return lambda: y_ref.__setitem__((slice(None), d), y_ref[:, d] + pltpu.matmul_pop(acc[m]))
+
+        waiting = []
+
+        def y_tiles(some):
+            for j in some:
+                waiting.append(y_tile(j))
+                if len(waiting) > 2:
+                    waiting.pop(0)()
+
+        cuts = [tiles * n // 3 // 2 * 2 for n in range(4)]
+        y_tiles(range(cuts[0], cuts[1]))
         score = jnp.zeros((rows, 1), F32)
         for m in (0, 1):
             block = slice(m * TILE, (m + 1) * TILE)
-            gate, up = pltpu.matmul_pop(first[m]), pltpu.matmul_pop(second[m])
-            d_hidden = pltpu.matmul_pop(wide[m])[:, :128].T[:rows]
-            sig = jax.nn.sigmoid(gate)
-            silu = gate * sig
-            hidden = (silu * up).astype(BF16)
+            gate, up, sig, silu, hidden = gates[m]
+            d_hidden = backs[m].T[:rows]
             d_gate = d_hidden * up * sig * (1.0 + gate * (1.0 - sig))
             d_up = d_hidden * silu
             score += jnp.sum(hidden.astype(F32) * d_hidden, axis=1, keepdims=True)
-            h_ref[:, block] = hidden
             dg_ref[:, block] = d_gate.astype(BF16)
             du_ref[:, block] = d_up.astype(BF16)
             dgt_ref[block, :128] = turned(d_gate).astype(BF16)
             dut_ref[block, :128] = turned(d_up).astype(BF16)
+            y_tiles(range(cuts[m + 1], cuts[m + 2]))
+        for end in waiting:
+            end()
         score_ref[...] += jnp.broadcast_to(score, score_ref.shape)
 
         @pl.loop(0, tiles // (2 * GROUP))
         def _(pair):
             def plan(m):
                 base = (2 * pair + m) * GROUP
-                y_ops, long_ops, short_ops = [], [], []
-
-                def y_op(d, kt, s):
-                    ks = slice(kt * TILE, (kt + 1) * TILE)
-                    pltpu.matmul_push_rhs(wd_ref[ks, d], s, m)
-                    pltpu.matmul_acc_lhs(first[m], h_ref[:, ks], load_staged_rhs=s)
-
-                def y_end(d):
-                    y_ref[:, d] += pltpu.matmul_pop(first[m])
-
-                def long_op(d, w, a, kt, s):
+                long_ops, short_ops = [], []
+
+                def long_op(d, acc, w, a, kt, s):
                     ks = slice(kt * TILE, (kt + 1) * TILE)
                     pltpu.matmul_push_rhs(a[ks, :], s, m)
-                    pltpu.matmul_acc_lhs(wide[m], w[d, ks], load_staged_rhs=s)
-
-                def long_end(d):
-                    dxt_ref[d, :] += pltpu.matmul_pop(wide[m])[:, :128]
+                    pltpu.matmul_acc_lhs(acc[m], w[d, ks], load_staged_rhs=s)
+
+                def long_end(d, acc):
+                    total = dxt_ref[d, :] + pltpu.matmul_pop(acc[m])[:, :128]
+                    if last:
+                        dx_ref[:, d] = total.T[:rows]
+                    else:
+                        dxt_ref[d, :] = total
 
                 def short_op(d, w, a, kt, s):
                     ks = slice(kt * TILE, (kt + 1) * TILE)
@@ -338,31 +357,37 @@
 
                 for j in range(GROUP):
                     d = at(base + j)
-                    for kt in (0, 1):
-                        y_ops.append((functools.partial(y_op, d, kt), functools.partial(y_end, d) if kt else None))
                     if j < GROUP - 1:
-                        ops, op, end, sides = long_ops, long_op, long_end, ((wg_ref, dgt_ref), (wu_ref, dut_ref))
+                        acc = (wide, spare)[j % 2]
+                        ops, op = long_ops, functools.partial(long_op, d, acc)
+                        end, sides = functools.partial(long_end, d, acc), ((wg_ref, dgt_ref), (wu_ref, dut_ref))
                     else:
-                        ops, op, end, sides = short_ops, short_op, short_end, ((wg_ref, dg_ref), (wu_ref, du_ref))
+                        ops, op = short_ops, functools.partial(short_op, d)
+                        end, sides = functools.partial(short_end, d), ((wg_ref, dg_ref), (wu_ref, du_ref))
                     for side, (w, a) in enumerate(sides):
                         for kt in (0, 1):
-                            last = side == 1 and kt == 1
-                            ops.append((functools.partial(op, d, w, a, kt), functools.partial(end, d) if last else None))
-                lists, taken, order = (long_ops, y_ops, short_ops), [0, 0, 0], []
+                            done = side == 1 and kt == 1
+                            ops.append((functools.partial(op, w, a, kt), end if done else None))
+                lists, taken, order = (long_ops, short_ops), [0, 0], []
                 total = sum(len(l) for l in lists)
                 for i in range(total):
-                    open_lists = [n for n in range(3) if taken[n] < len(lists[n])]
+                    open_lists = [n for n in range(2) if taken[n] < len(lists[n])]
                     best = max(open_lists, key=lambda n: (i + 1) * len(lists[n]) / total - taken[n])
                     order.append(lists[best][taken[best]])
                     taken[best] += 1
                 return order
 
+            late = []
             for i, both in enumerate(zip(plan(0), plan(1))):
                 for op, _ in both:
                     op(i % 2)
-                for _, end in both:
-                    if end is not None:
+                late.append([end for _, end in both if end is not None])
+                if len(late) > 2:
+                    for end in late.pop(0):
                         end()
+            for ends in late:
+                for end in ends:
+                    end()
 
     pl.run_scoped(inner, *accs)
 
@@ -373,7 +398,7 @@
     d, ff = w_gate.shape
     chunk = 2 * TILE
     with jax.sharding.use_abstract_mesh(mesh.abstract_mesh):
-        accs = [pltpu.ACC(m)((n, TILE), F32) for n in (TILE, rows, rows) for m in (0, 1)]
+        accs = [pltpu.ACC(m)((n, TILE), F32) for n in (TILE, TILE, rows, rows) for m in (0, 1)]
     vmem, hbm = pl.BlockSpec(memory_space=pltpu.VMEM), pl.BlockSpec(memory_space=pl.ANY)
     out = jax.ShapeDtypeStruct((EXPERTS * sent, 2 * width + 128), BF16)
     return pl.pallas_call(
@@ -398,7 +423,7 @@
             pltpu.VMEM((rows, 128), F32),
             pltpu.SemaphoreType.DMA((2, n_et, 3)),
         ],
-        compiler_params=pltpu.CompilerParams(vmem_limit_bytes=56 * 2**20),
+        compiler_params=pltpu.CompilerParams(vmem_limit_bytes=50 * 2**20),
         cost_estimate=pl.CostEstimate(
             flops=12 * rows * d * ff, bytes_accessed=6 * d * ff, transcendentals=rows * ff
         ),

time: 88.7 us -> 83.2 us (0.938)
  Pallas kernels: 40.9 us -> 37.6 us
  local copies, waits for them, and re-layouts: 5.11 us -> 4.02 us
  other arithmetic: 2.98 us -> 1.91 us
    pallas_call x1, Pallas kernels: 40 us -> 36.6 us  [tiled_experts(): pl.pallas_call(functools.partial(tiled_kernel, n_et, width, members, accs...]
    unnamed x24 -> x8, local copies, waits for them, and re-layouts: 2.67 us -> 1.58 us
    another operation x2, other arithmetic: 1.25 us -> 0.17 us
  transfers between devices with their start and end apart: 17 -> 17, of which waited for: 11 -> 11; matrix products, arithmetic and copies ran while one was open for 3% -> 4% of each run, Pallas kernels for 0% -> 0%
where the time goes in v3:
time: 83.2 us; the launch traced here: 82.9 us
  Pallas kernels  37.6 us (45%)
  waiting for transfers between devices  20.6 us (25%)
  starting transfers between devices  18.1 us (22%)
  local copies, waits for them, and re-layouts  4.02 us (5%)
  other arithmetic  1.91 us (2%)
    pallas_call x1, Pallas kernels, tiled_experts(): pl.pallas_call(functools.partial(tiled_kernel, n_et, width, members, accs...  36.6 us
    ppermute x3, waiting for transfers between devices, body(): lax.ppermute(back[r], 'de', to_expert(r))  6.25 us
    ppermute x3, waiting for transfers between devices, body(): lax.ppermute(rows_of[r], 'de', to_expert(r))  5.69 us
    ppermute x3, starting transfers between devices, body(): lax.ppermute(both, 'et', to_slice(i))  5.62 us
    ppermute x3, starting transfers between devices, body(): result += lax.ppermute(ends[i], 'et', to_slice(i)).astype(F32)  4.45 us
    ppermute x3, starting transfers between devices, body(): lax.ppermute(rows_of[r], 'de', to_expert(r))  3.55 us
    ppermute x3, starting transfers between devices, body(): lax.ppermute(back[r], 'de', to_expert(r))  3.55 us
    ppermute x3, waiting for transfers between devices, body(): lax.ppermute(both, 'et', to_slice(i))  3.3 us
  transfers between devices with their start and end apart: 17, of which 11 were waited for; matrix products, arithmetic and copies ran while one was open for 4% of the time, Pallas kernels for 0%

profile of v3, /device:TPU:0, one launch (start us, length us, event | category | flops | bytes accessed | tf_op | source)
XLA Modules:
  0.0 82.9 jit_solution(9390082273091425253)
XLA Ops:
  0.6 0.7 constant_dynamic-update-slice_fusion.1
  1.4 0.7 constant_dynamic-update-slice_fusion.refs_0_
  2.1 3.0 %collective-permute-start = (bf16[8,3072]{1,0:T(8,128)(2,1)S(1)}, bf16[8,3072]{1,0:T(8,128)(2,1)S(1)}, u32[]{:S(2)}, u32[]{:S(2)}) collective-permute-start(bf16[8,3072]{1,0:T(8,128)(2,1)S(1)} %constant_dynamic-update-slice_fusion.refs_0_), channel_id=1, source_target_pairs={{0,1},{1,0},{2,3},{3,2},{4,5},{5,4},{6,7},{7,6},{8,9},{9,8},{10,11... | collective-permute-start | bytes 147464 | tf_op jit(solution)/shard_map/ppermute | solution.py:451
  5.1 2.6 %collective-permute-start.1 = (bf16[8,3072]{1,0:T(8,128)(2,1)S(1)}, bf16[8,3072]{1,0:T(8,128)(2,1)S(1)}, u32[]{:S(2)}, u32[]{:S(2)}) collective-permute-start(bf16[8,3072]{1,0:T(8,128)(2,1)S(1)} %constant_dynamic-update-slice_fusion.refs_0_), channel_id=1, source_target_pairs={{0,2},{1,3},{2,0},{3,1},{4,6},{5,7},{6,4},{7,5},{8,10},{9,11},{10,... | collective-permute-start | bytes 147464 | tf_op jit(solution)/shard_map/ppermute | solution.py:451
  7.8 0.7 broadcast_xor_fusion
  8.4 0.7 select_reduce_fusion
  10.3 0.7 collective-permute-done.1.refs_2_
  11.1 2.6 %collective-permute-done.2.refs_3_ = bf16[8,3072]{1,0:T(8,128)(2,1)S(1)} collective-permute-done((bf16[8,3072]{1,0:T(8,128)(2,1)S(1)}, bf16[8,3072]{1,0:T(8,128)(2,1)S(1)}, u32[]{:S(2)}, u32[]{:S(2)}) %collective-permute-start.2) | collective-permute-done | bytes 49184 | tf_op jit(solution)/shard_map/ppermute | solution.py:451
  13.6 0.3 shard_map.94
  13.9 1.6 %collective-permute-start.3 = (bf16[24,3072]{1,0:T(8,128)(2,1)S(1)}, bf16[24,3072]{1,0:T(8,128)(2,1)S(1)}, u32[]{:S(2)}, u32[]{:S(2)}) collective-permute-start(bf16[24,3072]{1,0:T(8,128)(2,1)S(1)} %get-tuple-element.14), channel_id=1, source_target_pairs={{0,8},{4,12},{8,0},{12,4},{16,24},{20,28},{24,16},{28,20},{1,9},{5... | collective-permute-start | bytes 442376 | tf_op jit(solution)/shard_map/ppermute | solution.py:481
  15.5 1.5 %collective-permute-start.4 = (bf16[24,3072]{1,0:T(8,128)(2,1)S(1)}, bf16[24,3072]{1,0:T(8,128)(2,1)S(1)}, u32[]{:S(2)}, u32[]{:S(2)}) collective-permute-start(bf16[24,3072]{1,0:T(8,128)(2,1)S(1)} %get-tuple-element.15), channel_id=1, source_target_pairs={{0,16},{4,20},{8,24},{12,28},{16,0},{20,4},{24,8},{28,12},{1,17},{... | collective-permute-start | bytes 442376 | tf_op jit(solution)/shard_map/ppermute | solution.py:481
  17.0 0.5 collective-permute-start.5
  17.5 2.9 %collective-permute-done.3.refs_4_ = bf16[24,3072]{1,0:T(8,128)(2,1)S(1)} collective-permute-done((bf16[24,3072]{1,0:T(8,128)(2,1)S(1)}, bf16[24,3072]{1,0:T(8,128)(2,1)S(1)}, u32[]{:S(2)}, u32[]{:S(2)}) %collective-permute-start.3) | collective-permute-done | bytes 147488 | tf_op jit(solution)/shard_map/ppermute | solution.py:481
  20.4 2.8 %collective-permute-done.4.refs_5_ = bf16[24,3072]{1,0:T(8,128)(2,1)S(1)} collective-permute-done((bf16[24,3072]{1,0:T(8,128)(2,1)S(1)}, bf16[24,3072]{1,0:T(8,128)(2,1)S(1)}, u32[]{:S(2)}, u32[]{:S(2)}) %collective-permute-start.4) | collective-permute-done | bytes 147488 | tf_op jit(solution)/shard_map/ppermute | solution.py:481
  23.2 0.5 collective-permute-start.9
  23.7 0.9 %collective-permute-done.8.refs_9_ = bf16[24,3072]{1,0:T(8,128)(2,1)S(1)} collective-permute-done((bf16[24,3072]{1,0:T(8,128)(2,1)S(1)}, bf16[24,3072]{1,0:T(8,128)(2,1)S(1)}, u32[]{:S(2)}, u32[]{:S(2)}) %collective-permute-start.8) | collective-permute-done | bytes 147488 | tf_op jit(solution)/shard_map/ppermute | solution.py:483
  24.5 0.2 collective-permute-done.9.refs_10_
  24.7 36.6 %shard_map.95 = (bf16[96,3200]{1,0:T(8,128)(2,1)S(1)}, bf16[96,3200]{1,0:T(8,128)(2,1)S(1)}) custom-call(bf16[6144,2048]{1,0:T(8,128)(2,1)} %refs_0_.1, bf16[6144,2048]{1,0:T(8,128)(2,1)} %refs_1_.1, bf16[2048,6144]{1,0:T(8,128)(2,1)} %refs_2_.1, bf16[24,3072]{1,0:T(8,128)(2,1)S(1)} %get-tuple-element.13.refs_3_, ...), custom_call_target="tpu_custom_call" | custom-call | flops 7247757312 | bytes 75497472 | tf_op jit(solution)/shard_map/pallas_call | solution.py:404
  61.4 0.4 collective-permute-start.10
  61.9 1.6 %collective-permute-done.10 = bf16[96,3200]{1,0:T(8,128)(2,1)S(1)} collective-permute-done((bf16[96,3200]{1,0:T(8,128)(2,1)S(1)}, bf16[96,3200]{1,0:T(8,128)(2,1)S(1)}, u32[]{:S(2)}, u32[]{:S(2)}) %collective-permute-start.10) | collective-permute-done | bytes 614432 | tf_op jit(solution)/shard_map/ppermute | solution.py:502
  63.7 0.3 collective-permute-start.11
  63.9 1.0 %collective-permute-start.12 = (bf16[24,3200]{1,0:T(8,128)(2,1)S(1)}, bf16[24,3200]{1,0:T(8,128)(2,1)S(1)}, u32[]{:S(2)}, u32[]{:S(2)}) collective-permute-start(bf16[24,3200]{1,0:T(8,128)(2,1)S(1)} %get-tuple-element.43), channel_id=1, source_target_pairs={{0,16},{4,20},{8,24},{12,28},{16,0},{20,4},{24,8},{28,12},{1,17},{... | collective-permute-start | bytes 460808 | tf_op jit(solution)/shard_map/ppermute | solution.py:504
  65.0 2.3 %collective-permute-start.13 = (bf16[24,3200]{1,0:T(8,128)(2,1)S(1)}, bf16[24,3200]{1,0:T(8,128)(2,1)S(1)}, u32[]{:S(2)}, u32[]{:S(2)}) collective-permute-start(bf16[24,3200]{1,0:T(8,128)(2,1)S(1)} %get-tuple-element.42), channel_id=1, source_target_pairs={{0,24},{4,28},{8,16},{12,20},{16,8},{20,12},{24,0},{28,4},{1,25},{... | collective-permute-start | bytes 460808 | tf_op jit(solution)/shard_map/ppermute | solution.py:504
  67.4 3.1 %collective-permute-done.11.refs_1_ = bf16[24,3200]{1,0:T(8,128)(2,1)S(1)} collective-permute-done((bf16[24,3200]{1,0:T(8,128)(2,1)S(1)}, bf16[24,3200]{1,0:T(8,128)(2,1)S(1)}, u32[]{:S(2)}, u32[]{:S(2)}) %collective-permute-start.11) | collective-permute-done | bytes 153632 | tf_op jit(solution)/shard_map/ppermute | solution.py:504
  70.6 3.1 %collective-permute-done.13.refs_3_ = bf16[24,3200]{1,0:T(8,128)(2,1)S(1)} collective-permute-done((bf16[24,3200]{1,0:T(8,128)(2,1)S(1)}, bf16[24,3200]{1,0:T(8,128)(2,1)S(1)}, u32[]{:S(2)}, u32[]{:S(2)}) %collective-permute-start.13) | collective-permute-done | bytes 153632 | tf_op jit(solution)/shard_map/ppermute | solution.py:504
  73.7 0.7 shard_map.96
  74.4 1.2 %collective-permute-start.16 = (bf16[8,3200]{1,0:T(8,128)(2,1)S(1)}, bf16[8,3200]{1,0:T(8,128)(2,1)S(1)}, u32[]{:S(2)}, u32[]{:S(2)}) collective-permute-start(bf16[8,3200]{1,0:T(8,128)(2,1)S(1)} %get-tuple-element.22), channel_id=1, source_target_pairs={{0,3},{1,2},{2,1},{3,0},{4,7},{5,6},{6,5},{7,4},{8,11},{9,10},{10,... | collective-permute-start | bytes 153608 | tf_op jit(solution)/shard_map/ppermute | solution.py:508
  75.6 3.2 %collective-permute-start.14 = (bf16[8,3200]{1,0:T(8,128)(2,1)S(1)}, bf16[8,3200]{1,0:T(8,128)(2,1)S(1)}, u32[]{:S(2)}, u32[]{:S(2)}) collective-permute-start(bf16[8,3200]{1,0:T(8,128)(2,1)S(1)} %get-tuple-element.20), channel_id=1, source_target_pairs={{0,1},{1,0},{2,3},{3,2},{4,5},{5,4},{6,7},{7,6},{8,9},{9,8},{10,11... | collective-permute-start | bytes 153608 | tf_op jit(solution)/shard_map/ppermute | solution.py:508
  78.9 1.7 %collective-permute-done.16 = bf16[8,3200]{1,0:T(8,128)(2,1)S(1)} collective-permute-done((bf16[8,3200]{1,0:T(8,128)(2,1)S(1)}, bf16[8,3200]{1,0:T(8,128)(2,1)S(1)}, u32[]{:S(2)}, u32[]{:S(2)}) %collective-permute-start.16) | collective-permute-done | bytes 51232 | tf_op jit(solution)/shard_map/ppermute | solution.py:508
  80.6 1.0 %collective-permute-done.15 = bf16[8,3200]{1,0:T(8,128)(2,1)S(1)} collective-permute-done((bf16[8,3200]{1,0:T(8,128)(2,1)S(1)}, bf16[8,3200]{1,0:T(8,128)(2,1)S(1)}, u32[]{:S(2)}, u32[]{:S(2)}) %collective-permute-start.15) | collective-permute-done | bytes 51232 | tf_op jit(solution)/shard_map/ppermute | solution.py:508
  81.7 0.6 fusion.6
  82.3 0.6 copy.53
  (45 shorter events, 1.8 us)
Async XLA Ops:
  2.1 8.2 %collective-permute-start = (bf16[8,3072]{1,0:T(8,128)(2,1)S(1)}, bf16[8,3072]{1,0:T(8,128)(2,1)S(1)}, u32[]{:S(2)}, u32[]{:S(2)}) collective-permute-start(bf16[8,3072]{1,0:T(8,128)(2,1)S(1)} %constant_dynamic-update-slice_fusion.refs_0_), channel_id=1, source_target_pairs={{0,1},{1,0},{2,3},{3,2},{4,5},{5,4},{6,7},{7,6},{8,9},{9,8},{10,11... | collective-permute-start | bytes 147464 | tf_op jit(solution)/shard_map/ppermute | solution.py:451
  5.1 5.9 %collective-permute-start.1 = (bf16[8,3072]{1,0:T(8,128)(2,1)S(1)}, bf16[8,3072]{1,0:T(8,128)(2,1)S(1)}, u32[]{:S(2)}, u32[]{:S(2)}) collective-permute-start(bf16[8,3072]{1,0:T(8,128)(2,1)S(1)} %constant_dynamic-update-slice_fusion.refs_0_), channel_id=1, source_target_pairs={{0,2},{1,3},{2,0},{3,1},{4,6},{5,7},{6,4},{7,5},{8,10},{9,11},{10,... | collective-permute-start | bytes 147464 | tf_op jit(solution)/shard_map/ppermute | solution.py:451
  7.7 5.9 %collective-permute-start.2 = (bf16[8,3072]{1,0:T(8,128)(2,1)S(1)}, bf16[8,3072]{1,0:T(8,128)(2,1)S(1)}, u32[]{:S(2)}, u32[]{:S(2)}) collective-permute-start(bf16[8,3072]{1,0:T(8,128)(2,1)S(1)} %constant_dynamic-update-slice_fusion.refs_0_), channel_id=1, source_target_pairs={{0,3},{1,2},{2,1},{3,0},{4,7},{5,6},{6,5},{7,4},{8,11},{9,10},{10,... | collective-permute-start | bytes 147464 | tf_op jit(solution)/shard_map/ppermute | solution.py:451
  13.9 6.4 %collective-permute-start.3 = (bf16[24,3072]{1,0:T(8,128)(2,1)S(1)}, bf16[24,3072]{1,0:T(8,128)(2,1)S(1)}, u32[]{:S(2)}, u32[]{:S(2)}) collective-permute-start(bf16[24,3072]{1,0:T(8,128)(2,1)S(1)} %get-tuple-element.14), channel_id=1, source_target_pairs={{0,8},{4,12},{8,0},{12,4},{16,24},{20,28},{24,16},{28,20},{1,9},{5... | collective-permute-start | bytes 442376 | tf_op jit(solution)/shard_map/ppermute | solution.py:481
  15.5 7.7 %collective-permute-start.4 = (bf16[24,3072]{1,0:T(8,128)(2,1)S(1)}, bf16[24,3072]{1,0:T(8,128)(2,1)S(1)}, u32[]{:S(2)}, u32[]{:S(2)}) collective-permute-start(bf16[24,3072]{1,0:T(8,128)(2,1)S(1)} %get-tuple-element.15), channel_id=1, source_target_pairs={{0,16},{4,20},{8,24},{12,28},{16,0},{20,4},{24,8},{28,12},{1,17},{... | collective-permute-start | bytes 442376 | tf_op jit(solution)/shard_map/ppermute | solution.py:481
  17.0 6.2 %collective-permute-start.5 = (bf16[24,3072]{1,0:T(8,128)(2,1)S(1)}, bf16[24,3072]{1,0:T(8,128)(2,1)S(1)}, u32[]{:S(2)}, u32[]{:S(2)}) collective-permute-start(bf16[24,3072]{1,0:T(8,128)(2,1)S(1)} %get-tuple-element.16), channel_id=1, source_target_pairs={{0,24},{4,28},{8,16},{12,20},{16,8},{20,12},{24,0},{28,4},{1,25},{... | collective-permute-start | bytes 442376 | tf_op jit(solution)/shard_map/ppermute | solution.py:481
  17.5 44.4 %copy-start = (s32[8,2]{0,1:T(2,128)S(1)}, s32[8,2]{0,1:T(2,128)}, u32[]{:S(2)}) copy-start(s32[8,2]{0,1:T(2,128)} %param.8) | copy-start | bytes 196
  17.5 61.4 %copy-start.1 = (f32[8,2]{0,1:T(2,128)S(1)}, f32[8,2]{0,1:T(2,128)}, u32[]{:S(2)}) copy-start(f32[8,2]{0,1:T(2,128)} %param.9) | copy-start | bytes 196
  17.5 6.2 %collective-permute-start.6 = (bf16[24,3072]{1,0:T(8,128)(2,1)S(1)}, bf16[24,3072]{1,0:T(8,128)(2,1)S(1)}, u32[]{:S(2)}, u32[]{:S(2)}) collective-permute-start(bf16[24,3072]{1,0:T(8,128)(2,1)S(1)} %get-tuple-element.13.refs_3_), channel_id=1, source_target_pairs={{0,4},{4,0},{8,12},{12,8},{16,20},{20,16},{24,28},{28,24},{1,5},{5... | collective-permute-start | bytes 442376 | tf_op jit(solution)/shard_map/ppermute | solution.py:483
  20.3 3.3 %collective-permute-start.7 = (bf16[24,3072]{1,0:T(8,128)(2,1)S(1)}, bf16[24,3072]{1,0:T(8,128)(2,1)S(1)}, u32[]{:S(2)}, u32[]{:S(2)}) collective-permute-start(bf16[24,3072]{1,0:T(8,128)(2,1)S(1)} %collective-permute-done.3.refs_4_), channel_id=1, source_target_pairs={{0,4},{4,0},{8,12},{12,8},{16,20},{20,16},{24,28},{28,24},{1,5},{5... | collective-permute-start | bytes 442376 | tf_op jit(solution)/shard_map/ppermute | solution.py:483
  23.2 1.4 %collective-permute-start.8 = (bf16[24,3072]{1,0:T(8,128)(2,1)S(1)}, bf16[24,3072]{1,0:T(8,128)(2,1)S(1)}, u32[]{:S(2)}, u32[]{:S(2)}) collective-permute-start(bf16[24,3072]{1,0:T(8,128)(2,1)S(1)} %collective-permute-done.4.refs_5_), channel_id=1, source_target_pairs={{0,4},{4,0},{8,12},{12,8},{16,20},{20,16},{24,28},{28,24},{1,5},{5... | collective-permute-start | bytes 442376 | tf_op jit(solution)/shard_map/ppermute | solution.py:483
  23.2 1.6 %collective-permute-start.9 = (bf16[24,3072]{1,0:T(8,128)(2,1)S(1)}, bf16[24,3072]{1,0:T(8,128)(2,1)S(1)}, u32[]{:S(2)}, u32[]{:S(2)}) collective-permute-start(bf16[24,3072]{1,0:T(8,128)(2,1)S(1)} %collective-permute-done.5.refs_6_), channel_id=1, source_target_pairs={{0,4},{4,0},{8,12},{12,8},{16,20},{20,16},{24,28},{28,24},{1,5},{5... | collective-permute-start | bytes 442376 | tf_op jit(solution)/shard_map/ppermute | solution.py:483
  61.4 2.1 %collective-permute-start.10 = (bf16[96,3200]{1,0:T(8,128)(2,1)S(1)}, bf16[96,3200]{1,0:T(8,128)(2,1)S(1)}, u32[]{:S(2)}, u32[]{:S(2)}) collective-permute-start(bf16[96,3200]{1,0:T(8,128)(2,1)S(1)} %get-tuple-element.18), channel_id=1, source_target_pairs={{0,4},{4,0},{8,12},{12,8},{16,20},{20,16},{24,28},{28,24},{1,5},{5... | collective-permute-start | bytes 1843208 | tf_op jit(solution)/shard_map/ppermute | solution.py:502
  63.7 6.9 %collective-permute-start.11 = (bf16[24,3200]{1,0:T(8,128)(2,1)S(1)}, bf16[24,3200]{1,0:T(8,128)(2,1)S(1)}, u32[]{:S(2)}, u32[]{:S(2)}) collective-permute-start(bf16[24,3200]{1,0:T(8,128)(2,1)S(1)} %get-tuple-element.44), channel_id=1, source_target_pairs={{0,8},{4,12},{8,0},{12,4},{16,24},{20,28},{24,16},{28,20},{1,9},{5... | collective-permute-start | bytes 460808 | tf_op jit(solution)/shard_map/ppermute | solution.py:504
  63.9 6.6 %collective-permute-start.12 = (bf16[24,3200]{1,0:T(8,128)(2,1)S(1)}, bf16[24,3200]{1,0:T(8,128)(2,1)S(1)}, u32[]{:S(2)}, u32[]{:S(2)}) collective-permute-start(bf16[24,3200]{1,0:T(8,128)(2,1)S(1)} %get-tuple-element.43), channel_id=1, source_target_pairs={{0,16},{4,20},{8,24},{12,28},{16,0},{20,4},{24,8},{28,12},{1,17},{... | collective-permute-start | bytes 460808 | tf_op jit(solution)/shard_map/ppermute | solution.py:504
  65.0 8.7 %collective-permute-start.13 = (bf16[24,3200]{1,0:T(8,128)(2,1)S(1)}, bf16[24,3200]{1,0:T(8,128)(2,1)S(1)}, u32[]{:S(2)}, u32[]{:S(2)}) collective-permute-start(bf16[24,3200]{1,0:T(8,128)(2,1)S(1)} %get-tuple-element.42), channel_id=1, source_target_pairs={{0,24},{4,28},{8,16},{12,20},{16,8},{20,12},{24,0},{28,4},{1,25},{... | collective-permute-start | bytes 460808 | tf_op jit(solution)/shard_map/ppermute | solution.py:504
  74.4 6.2 %collective-permute-start.16 = (bf16[8,3200]{1,0:T(8,128)(2,1)S(1)}, bf16[8,3200]{1,0:T(8,128)(2,1)S(1)}, u32[]{:S(2)}, u32[]{:S(2)}) collective-permute-start(bf16[8,3200]{1,0:T(8,128)(2,1)S(1)} %get-tuple-element.22), channel_id=1, source_target_pairs={{0,3},{1,2},{2,1},{3,0},{4,7},{5,6},{6,5},{7,4},{8,11},{9,10},{10,... | collective-permute-start | bytes 153608 | tf_op jit(solution)/shard_map/ppermute | solution.py:508
  75.6 6.0 %collective-permute-start.15 = (bf16[8,3200]{1,0:T(8,128)(2,1)S(1)}, bf16[8,3200]{1,0:T(8,128)(2,1)S(1)}, u32[]{:S(2)}, u32[]{:S(2)}) collective-permute-start(bf16[8,3200]{1,0:T(8,128)(2,1)S(1)} %get-tuple-element.21), channel_id=1, source_target_pairs={{0,2},{1,3},{2,0},{3,1},{4,6},{5,7},{6,4},{7,5},{8,10},{9,11},{10,... | collective-permute-start | bytes 153608 | tf_op jit(solution)/shard_map/ppermute | solution.py:508
  75.6 6.0 %collective-permute-start.14 = (bf16[8,3200]{1,0:T(8,128)(2,1)S(1)}, bf16[8,3200]{1,0:T(8,128)(2,1)S(1)}, u32[]{:S(2)}, u32[]{:S(2)}) collective-permute-start(bf16[8,3200]{1,0:T(8,128)(2,1)S(1)} %get-tuple-element.20), channel_id=1, source_target_pairs={{0,1},{1,0},{2,3},{3,2},{4,5},{5,4},{6,7},{7,6},{8,9},{9,8},{10,11... | collective-permute-start | bytes 153608 | tf_op jit(solution)/shard_map/ppermute | solution.py:508

commit v4 on v3

--- a/solution.py
+++ b/solution.py
@@ -94,7 +94,7 @@
     sent = n_et * CAP + -(n_et * CAP) % 8
     if members * EXPERTS * sent > TILE or n_et * rows > TILE:
         return False
-    return rows <= 128 and members == 2 and width % TILE == 0 and ff % (2 * TILE) == 0 and n_et * (width // TILE) % (2 * GROUP) == 0
+    return rows <= 128 and members == 2 and width % TILE == 0 and ff % (4 * TILE) == 0 and n_et * (width // TILE) % (2 * GROUP) == 0
 
 
 def sorter(n_et, members, rows, sent, turned):
@@ -162,11 +162,45 @@
     )(pick, named, scale, *parts)
 
 
+def first_chunk_kernel(after_ref, wg_hbm, wu_hbm, wg_ref, wu_ref, here_ref, sems):
+    chunk = wg_ref.shape[1]
+    copies = (
+        pltpu.make_async_copy(wg_hbm.at[:, pl.ds(0, chunk)], wg_ref, sems.at[0]),
+        pltpu.make_async_copy(wu_hbm.at[:, pl.ds(0, chunk)], wu_ref, sems.at[1]),
+    )
+    for copy in copies:
+        copy.start()
+    here_ref[...] = jnp.zeros_like(here_ref)
+    for copy in copies:
+        copy.wait()
+
+
+def first_chunk(after, w_gate, w_up):
+    d, chunk = w_gate.shape[0], 2 * TILE
+    weights = [pltpu.with_memory_space_constraint(w, pltpu.HBM) for w in (w_gate, w_up)]
+    hbm, vmem = pl.BlockSpec(memory_space=pltpu.HBM), pl.BlockSpec(memory_space=pltpu.VMEM)
+    return pl.pallas_call(
+        first_chunk_kernel,
+        in_specs=[pl.BlockSpec(memory_space=pl.ANY)] + [hbm] * 2,
+        out_specs=[vmem] * 3,
+        out_shape=[
+            pltpu.VMEM((d, chunk), BF16),
+            pltpu.VMEM((d, chunk), BF16),
+            pltpu.VMEM(after.shape, BF16),
+        ],
+        scratch_shapes=[pltpu.SemaphoreType.DMA((2,))],
+        compiler_params=pltpu.CompilerParams(vmem_limit_bytes=2 * 2**20),
+        cost_estimate=pl.CostEstimate(flops=0, bytes_accessed=8 * d * chunk, transcendentals=0),
+    )(after, *weights)
+
+
 def tiled_kernel(n_et, width, members, accs, *refs):
     wg_hbm, wu_hbm, wd_hbm = refs[:3]
     parts = refs[3 : 3 + EXPERTS * members]
-    (out_ref, sib_ref, xg_ref, wg_buf, wu_buf, wd_buf, gt_ref, h_ref, dg_ref, du_ref, dgt_ref, dut_ref,
-     y_ref, dx_ref, dxt_ref, score_ref, sems) = refs[3 + EXPERTS * members :]
+    refs = refs[3 + EXPERTS * members + 2 :]
+    one, refs = refs[2:4], refs[:2] + refs[4:]
+    (out_ref, sib_ref, xg_ref, wg_buf, wu_buf, wd_one, wd_buf, gt_ref, h_ref, dg_ref, du_ref, dgt_ref, dut_ref,
+     y_ref, dx_ref, dxt_ref, score_ref, sems) = refs
     t = lax.axis_index("et")
     rows = xg_ref.shape[1]
     chunk = 2 * TILE
@@ -185,21 +219,27 @@
         pad = jnp.zeros((128 - rows, a.shape[1]), F32)
         return jnp.concatenate([a, pad], axis=0).T
 
-    def copies(c, slot, i):
+    one, two = (*one, wd_one), (wg_buf, wu_buf, wd_buf)
+
+    def copies(c, bufs):
         cols = pl.ds(pl.multiple_of(c * chunk, chunk), chunk)
-        d = piece(i)
+        slot = 0 if bufs is one else 1
         return (
-            pltpu.make_async_copy(wd_hbm.at[cols, d], wd_buf.at[slot, :, d], sems.at[slot, i, 0]),
-            pltpu.make_async_copy(wg_hbm.at[d, cols], wg_buf.at[slot, d, :], sems.at[slot, i, 1]),
-            pltpu.make_async_copy(wu_hbm.at[d, cols], wu_buf.at[slot, d, :], sems.at[slot, i, 2]),
+            pltpu.make_async_copy(wg_hbm.at[:, cols], bufs[0], sems.at[slot, 0]),
+            pltpu.make_async_copy(wu_hbm.at[:, cols], bufs[1], sems.at[slot, 1]),
+            pltpu.make_async_copy(wd_hbm.at[cols, :], bufs[2], sems.at[slot, 2]),
         )
 
-    def fetch(c, slot):
-        for i in range(n_et):
-            for copy in copies(c, slot, i):
-                copy.start()
-
-    fetch(0, 0)
+    def fetch(c, bufs):
+        for copy in copies(c, bufs):
+            copy.start()
+
+    def arrive(c, bufs):
+        for copy in copies(c, bufs):
+            copy.wait()
+
+    copies(0, one)[2].start()
+    fetch(1, two)
     score_ref[...] = jnp.zeros_like(score_ref)
     y_ref[...] = jnp.zeros_like(y_ref)
     dx_ref[...] = jnp.zeros_like(dx_ref)
@@ -229,18 +269,23 @@
                 if u >= per:
                     gt_ref[at(i * per + u - per), :128] = turned(some).astype(BF16)
 
-        def chunk_at(c, last):
-            slot = lax.rem(c, 2)
+        def two_chunks(c, last):
+            one_chunk(False, wide, spare, first, second, *one)
+            arrive(c + 1, two)
             if not last:
-                fetch(c + 1, 1 - slot)
-            wg_ref, wu_ref, wd_ref = wg_buf.at[slot], wu_buf.at[slot], wd_buf.at[slot]
-            one_chunk(c, slot, last, wide, spare, first, second, wg_ref, wu_ref, wd_ref)
-
-        @pl.loop(0, steps - 1)
-        def _(c):
-            chunk_at(c, False)
-
-        chunk_at(steps - 1, True)
+                fetch(c + 2, one)
+            one_chunk(last, wide, spare, first, second, *two)
+            if not last:
+                arrive(c + 2, one)
+                fetch(c + 3, two)
+
+        copies(0, one)[2].wait()
+
+        @pl.loop(0, steps // 2 - 1)
+        def _(pair):
+            two_chunks(2 * pair, False)
+
+        two_chunks(steps - 2, True)
 
         back = sorter(n_et, members, rows, sent, 1)
         half = EXPERTS * sent
@@ -259,11 +304,9 @@
         out_ref[:, 2 * width :] = block[:half, :128]
         sib_ref[:, 2 * width :] = block[half : 2 * half, :128]
 
-    def one_chunk(c, slot, last, wide, spare, first, second, wg_ref, wu_ref, wd_ref):
+    def one_chunk(last, wide, spare, first, second, wg_ref, wu_ref, wd_ref):
         @pl.loop(0, n_et)
         def _(i):
-            for copy in copies(c, slot, i):
-                copy.wait()
             turn = 0
             for u in range(per):
                 k = at(jnp.bitwise_xor(t, i) * per + u)
@@ -392,25 +435,28 @@
     pl.run_scoped(inner, *accs)
 
 
-def tiled_experts(mesh, n_et, members, parts, w_gate, w_up, w_down):
+def tiled_experts(mesh, n_et, members, parts, started, w_gate, w_up, w_down):
     sent, width = parts[0].shape[0], parts[0].shape[1] // 2
     rows = members * EXPERTS * CAP + -(members * EXPERTS * CAP) % 16
     d, ff = w_gate.shape
     chunk = 2 * TILE
     with jax.sharding.use_abstract_mesh(mesh.abstract_mesh):
         accs = [pltpu.ACC(m)((n, TILE), F32) for n in (TILE, TILE, rows, rows) for m in (0, 1)]
-    vmem, hbm = pl.BlockSpec(memory_space=pltpu.VMEM), pl.BlockSpec(memory_space=pl.ANY)
+    vmem, hbm = pl.BlockSpec(memory_space=pltpu.VMEM), pl.BlockSpec(memory_space=pltpu.HBM)
+    weights = [pltpu.with_memory_space_constraint(w, pltpu.HBM) for w in (w_gate, w_up, w_down)]
     out = jax.ShapeDtypeStruct((EXPERTS * sent, 2 * width + 128), BF16)
     return pl.pallas_call(
         functools.partial(tiled_kernel, n_et, width, members, accs),
-        in_specs=[hbm] * 3 + [vmem] * len(parts),
-        out_specs=[vmem, vmem],
-        out_shape=[out, out],
+        in_specs=[hbm] * 3 + [vmem] * (len(parts) + 2),
+        out_specs=[vmem] * 4,
+        out_shape=[out, out] + [pltpu.VMEM(a.shape, BF16) for a in started],
+        input_output_aliases={3 + len(parts) + n: 2 + n for n in range(2)},
         scratch_shapes=[
             pltpu.VMEM((n_et, rows, 2 * width), BF16),
-            pltpu.VMEM((2, d, chunk), BF16),
-            pltpu.VMEM((2, d, chunk), BF16),
-            pltpu.VMEM((2, chunk, d), BF16),
+            pltpu.VMEM((d, chunk), BF16),
+            pltpu.VMEM((d, chunk), BF16),
+            pltpu.VMEM((chunk, d), BF16),
+            pltpu.VMEM((chunk, d), BF16),
             pltpu.VMEM((d, TILE), BF16),
             pltpu.VMEM((rows, chunk), BF16),
             pltpu.VMEM((rows, chunk), BF16),
@@ -421,13 +467,13 @@
             pltpu.VMEM((rows, d), F32),
             pltpu.VMEM((d, 128), F32),
             pltpu.VMEM((rows, 128), F32),
-            pltpu.SemaphoreType.DMA((2, n_et, 3)),
+            pltpu.SemaphoreType.DMA((2, 3)),
         ],
-        compiler_params=pltpu.CompilerParams(vmem_limit_bytes=50 * 2**20),
+        compiler_params=pltpu.CompilerParams(vmem_limit_bytes=38 * 2**20),
         cost_estimate=pl.CostEstimate(
             flops=12 * rows * d * ff, bytes_accessed=6 * d * ff, transcendentals=rows * ff
         ),
-    )(w_gate, w_up, w_down, *parts)
+    )(*weights, *parts, *started)
 
 
 def body(mesh, tokens, expert_ids, gate_probs, w_gate, w_up, w_down, out_grad):
@@ -479,13 +525,18 @@
 
     rows_of = select(pick.astype(BF16), scale, pieces)
     mine = [rows_of[0]] + [lax.ppermute(rows_of[r], "de", to_expert(r)) for r in range(1, EXPERTS)]
+    rows = members * EXPERTS * CAP
+    pad = -rows % 16
+    tiled = tiles_fit(members, rows + pad, n_et, width, w_gate.shape[1])
+    if tiled:
+        *started, here = first_chunk(rows_of[0], w_gate, w_up)
+        mine[-1] = mine[-1] + here
     parts = mine + [
         lax.ppermute(a, "de", to_member(k)) for k in range(1, members) for a in mine
     ]
-    rows = members * EXPERTS * CAP
-    pad = -rows % 16
-    if tiles_fit(members, rows + pad, n_et, width, w_gate.shape[1]):
-        kept, *others = tiled_experts(mesh, n_et, members, parts, w_gate, w_up, w_down)
+    if tiled:
+        kept, other, *_ = tiled_experts(mesh, n_et, members, parts, started, w_gate, w_up, w_down)
+        others = [other]
     else:
         xg = jnp.stack(parts)[:, :used].reshape(members * EXPERTS, n_et, CAP, 2 * width)
         xg = xg.transpose(1, 0, 2, 3).reshape(n_et, rows, 2 * width)

time: 83.2 us -> 80.4 us (0.966)
  waiting for transfers between devices: 20.6 us -> 15.4 us
  Pallas kernels: 37.6 us -> 39.2 us
    ppermute x3, waiting for transfers between devices: 5.69 us -> 0.5 us  [body(): lax.ppermute(rows_of[r], 'de', to_expert(r))]
    pallas_call x0 -> x1, Pallas kernels: none -> 4.64 us  [first_chunk(): pl.pallas_call(first_chunk_kernel, in_specs=[pl.BlockSpec(memory_space=pl...]
    pallas_call x1, Pallas kernels: 36.6 us -> 33.6 us  [tiled_experts(): pl.pallas_call(functools.partial(tiled_kernel, n_et, width, members, accs...]
  transfers between devices with their start and end apart: 17 -> 17, of which waited for: 11 -> 10; matrix products, arithmetic and copies ran while one was open for 4% -> 4% of each run, Pallas kernels for 0% -> 6%
where the time goes in v4:
time: 80.4 us; the launch traced here: 80.1 us
  Pallas kernels  39.2 us (49%)
  starting transfers between devices  18.8 us (23%)
  waiting for transfers between devices  15.4 us (19%)
  local copies, waits for them, and re-layouts  4.02 us (5%)
  other arithmetic  1.95 us (2%)
    pallas_call x1, Pallas kernels, tiled_experts(): pl.pallas_call(functools.partial(tiled_kernel, n_et, width, members, accs...  33.6 us
    ppermute x3, waiting for transfers between devices, body(): lax.ppermute(back[r], 'de', to_expert(r))  6.57 us
    ppermute x3, starting transfers between devices, body(): lax.ppermute(both, 'et', to_slice(i))  5.62 us
    pallas_call x1, Pallas kernels, first_chunk(): pl.pallas_call(first_chunk_kernel, in_specs=[pl.BlockSpec(memory_space=pl...  4.64 us
    ppermute x3, starting transfers between devices, body(): result += lax.ppermute(ends[i], 'et', to_slice(i)).astype(F32)  4.45 us
    ppermute x3, starting transfers between devices, body(): lax.ppermute(back[r], 'de', to_expert(r))  3.57 us
    ppermute x3, starting transfers between devices, body(): lax.ppermute(rows_of[r], 'de', to_expert(r))  3.55 us
    ppermute x3, waiting for transfers between devices, body(): lax.ppermute(both, 'et', to_slice(i))  3.3 us
  transfers between devices with their start and end apart: 17, of which 10 were waited for; matrix products, arithmetic and copies ran while one was open for 4% of the time, Pallas kernels for 6%

profile of v4, /device:TPU:0, one launch (start us, length us, event | category | flops | bytes accessed | tf_op | source)
XLA Modules:
  0.0 80.1 jit_solution(4601549001899737951)
XLA Ops:
  0.6 0.7 constant_dynamic-update-slice_fusion.1
  1.4 0.7 constant_dynamic-update-slice_fusion.refs_0_
  2.1 3.0 %collective-permute-start = (bf16[8,3072]{1,0:T(8,128)(2,1)S(1)}, bf16[8,3072]{1,0:T(8,128)(2,1)S(1)}, u32[]{:S(2)}, u32[]{:S(2)}) collective-permute-start(bf16[8,3072]{1,0:T(8,128)(2,1)S(1)} %constant_dynamic-update-slice_fusion.refs_0_), channel_id=1, source_target_pairs={{0,1},{1,0},{2,3},{3,2},{4,5},{5,4},{6,7},{7,6},{8,9},{9,8},{10,11... | collective-permute-start | bytes 147464 | tf_op jit(solution)/shard_map/ppermute | solution.py:497
  5.1 2.6 %collective-permute-start.1 = (bf16[8,3072]{1,0:T(8,128)(2,1)S(1)}, bf16[8,3072]{1,0:T(8,128)(2,1)S(1)}, u32[]{:S(2)}, u32[]{:S(2)}) collective-permute-start(bf16[8,3072]{1,0:T(8,128)(2,1)S(1)} %constant_dynamic-update-slice_fusion.refs_0_), channel_id=1, source_target_pairs={{0,2},{1,3},{2,0},{3,1},{4,6},{5,7},{6,4},{7,5},{8,10},{9,11},{10,... | collective-permute-start | bytes 147464 | tf_op jit(solution)/shard_map/ppermute | solution.py:497
  7.8 0.7 broadcast_xor_fusion
  8.4 0.7 select_reduce_fusion
  10.3 0.7 collective-permute-done.1.refs_2_
  11.1 2.6 %collective-permute-done.2.refs_3_ = bf16[8,3072]{1,0:T(8,128)(2,1)S(1)} collective-permute-done((bf16[8,3072]{1,0:T(8,128)(2,1)S(1)}, bf16[8,3072]{1,0:T(8,128)(2,1)S(1)}, u32[]{:S(2)}, u32[]{:S(2)}) %collective-permute-start.2) | collective-permute-done | bytes 49184 | tf_op jit(solution)/shard_map/ppermute | solution.py:497
  13.6 0.3 shard_map.94
  13.9 1.6 %collective-permute-start.3 = (bf16[24,3072]{1,0:T(8,128)(2,1)S(1)}, bf16[24,3072]{1,0:T(8,128)(2,1)S(1)}, u32[]{:S(2)}, u32[]{:S(2)}) collective-permute-start(bf16[24,3072]{1,0:T(8,128)(2,1)S(1)} %get-tuple-element.17), channel_id=1, source_target_pairs={{0,8},{4,12},{8,0},{12,4},{16,24},{20,28},{24,16},{28,20},{1,9},{5... | collective-permute-start | bytes 442376 | tf_op jit(solution)/shard_map/ppermute | solution.py:527
  15.5 1.5 %collective-permute-start.4 = (bf16[24,3072]{1,0:T(8,128)(2,1)S(1)}, bf16[24,3072]{1,0:T(8,128)(2,1)S(1)}, u32[]{:S(2)}, u32[]{:S(2)}) collective-permute-start(bf16[24,3072]{1,0:T(8,128)(2,1)S(1)} %get-tuple-element.18), channel_id=1, source_target_pairs={{0,16},{4,20},{8,24},{12,28},{16,0},{20,4},{24,8},{28,12},{1,17},{... | collective-permute-start | bytes 442376 | tf_op jit(solution)/shard_map/ppermute | solution.py:527
  17.0 0.5 collective-permute-start.5
  17.5 4.6 %shard_map.95 = (bf16[6144,512]{1,0:T(8,128)(2,1)S(1)}, bf16[6144,512]{1,0:T(8,128)(2,1)S(1)}, bf16[24,3072]{1,0:T(8,128)(2,1)S(1)}) custom-call(bf16[24,3072]{1,0:T(8,128)(2,1)S(1)} %get-tuple-element.16.after_ref.refs_3_, bf16[6144,2048]{1,0:T(8,128)(2,1)} %refs_0_.1, bf16[6144,2048]{1,0:T(8,128)(2,1)} %refs_1_.1), custom_call_target="tpu_custom_call" | custom-call | bytes 25165824 | tf_op jit(solution)/shard_map/pallas_call | solution.py:182
  22.1 0.6 collective-permute-start.7
  22.7 0.5 collective-permute-done.4.refs_5_
  23.2 0.6 collective-permute-start.9
  23.8 0.7 collective-permute-done.8.refs_9_
  24.8 33.6 %shard_map.96 = (bf16[96,3200]{1,0:T(8,128)(2,1)S(1)}, bf16[96,3200]{1,0:T(8,128)(2,1)S(1)}, bf16[6144,512]{1,0:T(8,128)(2,1)S(1)}, bf16[6144,512]{1,0:T(8,128)(2,1)S(1)}) custom-call(bf16[6144,2048]{1,0:T(8,128)(2,1)} %refs_0_.1, bf16[6144,2048]{1,0:T(8,128)(2,1)} %refs_1_.1, ...), custom_call_target="tpu_custom_call", output_to_operand_aliasing={{2}: (11, {}), {3}: (12, {})} | custom-call | flops 7247757312 | bytes 75497472 | tf_op jit(solution)/shard_map/pallas_call | solution.py:448
  58.4 0.4 collective-permute-start.10
  59.0 1.5 %collective-permute-done.10 = bf16[96,3200]{1,0:T(8,128)(2,1)S(1)} collective-permute-done((bf16[96,3200]{1,0:T(8,128)(2,1)S(1)}, bf16[96,3200]{1,0:T(8,128)(2,1)S(1)}, u32[]{:S(2)}, u32[]{:S(2)}) %collective-permute-start.10) | collective-permute-done | bytes 614432 | tf_op jit(solution)/shard_map/ppermute | solution.py:553
  60.7 1.1 %collective-permute-start.11 = (bf16[24,3200]{1,0:T(8,128)(2,1)S(1)}, bf16[24,3200]{1,0:T(8,128)(2,1)S(1)}, u32[]{:S(2)}, u32[]{:S(2)}) collective-permute-start(bf16[24,3200]{1,0:T(8,128)(2,1)S(1)} %get-tuple-element.50), channel_id=1, source_target_pairs={{0,8},{4,12},{8,0},{12,4},{16,24},{20,28},{24,16},{28,20},{1,9},{5... | collective-permute-start | bytes 460808 | tf_op jit(solution)/shard_map/ppermute | solution.py:555
  61.8 1.5 %collective-permute-start.12 = (bf16[24,3200]{1,0:T(8,128)(2,1)S(1)}, bf16[24,3200]{1,0:T(8,128)(2,1)S(1)}, u32[]{:S(2)}, u32[]{:S(2)}) collective-permute-start(bf16[24,3200]{1,0:T(8,128)(2,1)S(1)} %get-tuple-element.49), channel_id=1, source_target_pairs={{0,16},{4,20},{8,24},{12,28},{16,0},{20,4},{24,8},{28,12},{1,17},{... | collective-permute-start | bytes 460808 | tf_op jit(solution)/shard_map/ppermute | solution.py:555
  63.3 1.0 %collective-permute-start.13 = (bf16[24,3200]{1,0:T(8,128)(2,1)S(1)}, bf16[24,3200]{1,0:T(8,128)(2,1)S(1)}, u32[]{:S(2)}, u32[]{:S(2)}) collective-permute-start(bf16[24,3200]{1,0:T(8,128)(2,1)S(1)} %get-tuple-element.48), channel_id=1, source_target_pairs={{0,24},{4,28},{8,16},{12,20},{16,8},{20,12},{24,0},{28,4},{1,25},{... | collective-permute-start | bytes 460808 | tf_op jit(solution)/shard_map/ppermute | solution.py:555
  64.5 3.1 %collective-permute-done.11.refs_1_ = bf16[24,3200]{1,0:T(8,128)(2,1)S(1)} collective-permute-done((bf16[24,3200]{1,0:T(8,128)(2,1)S(1)}, bf16[24,3200]{1,0:T(8,128)(2,1)S(1)}, u32[]{:S(2)}, u32[]{:S(2)}) %collective-permute-start.11) | collective-permute-done | bytes 153632 | tf_op jit(solution)/shard_map/ppermute | solution.py:555
  67.6 3.4 %collective-permute-done.12.refs_2_ = bf16[24,3200]{1,0:T(8,128)(2,1)S(1)} collective-permute-done((bf16[24,3200]{1,0:T(8,128)(2,1)S(1)}, bf16[24,3200]{1,0:T(8,128)(2,1)S(1)}, u32[]{:S(2)}, u32[]{:S(2)}) %collective-permute-start.12) | collective-permute-done | bytes 153632 | tf_op jit(solution)/shard_map/ppermute | solution.py:555
  71.1 0.7 shard_map.97
  71.8 0.9 %collective-permute-start.16 = (bf16[8,3200]{1,0:T(8,128)(2,1)S(1)}, bf16[8,3200]{1,0:T(8,128)(2,1)S(1)}, u32[]{:S(2)}, u32[]{:S(2)}) collective-permute-start(bf16[8,3200]{1,0:T(8,128)(2,1)S(1)} %get-tuple-element.28), channel_id=1, source_target_pairs={{0,3},{1,2},{2,1},{3,0},{4,7},{5,6},{6,5},{7,4},{8,11},{9,10},{10,... | collective-permute-start | bytes 153608 | tf_op jit(solution)/shard_map/ppermute | solution.py:559
  72.7 3.5 %collective-permute-start.14 = (bf16[8,3200]{1,0:T(8,128)(2,1)S(1)}, bf16[8,3200]{1,0:T(8,128)(2,1)S(1)}, u32[]{:S(2)}, u32[]{:S(2)}) collective-permute-start(bf16[8,3200]{1,0:T(8,128)(2,1)S(1)} %get-tuple-element.26), channel_id=1, source_target_pairs={{0,1},{1,0},{2,3},{3,2},{4,5},{5,4},{6,7},{7,6},{8,9},{9,8},{10,11... | collective-permute-start | bytes 153608 | tf_op jit(solution)/shard_map/ppermute | solution.py:559
  76.3 1.6 %collective-permute-done.16 = bf16[8,3200]{1,0:T(8,128)(2,1)S(1)} collective-permute-done((bf16[8,3200]{1,0:T(8,128)(2,1)S(1)}, bf16[8,3200]{1,0:T(8,128)(2,1)S(1)}, u32[]{:S(2)}, u32[]{:S(2)}) %collective-permute-start.16) | collective-permute-done | bytes 51232 | tf_op jit(solution)/shard_map/ppermute | solution.py:559
  77.9 0.9 %collective-permute-done.15 = bf16[8,3200]{1,0:T(8,128)(2,1)S(1)} collective-permute-done((bf16[8,3200]{1,0:T(8,128)(2,1)S(1)}, bf16[8,3200]{1,0:T(8,128)(2,1)S(1)}, u32[]{:S(2)}, u32[]{:S(2)}) %collective-permute-start.15) | collective-permute-done | bytes 51232 | tf_op jit(solution)/shard_map/ppermute | solution.py:559
  78.8 0.6 fusion.6
  79.5 0.6 copy.55
  (47 shorter events, 2.1 us)
Async XLA Ops:
  2.1 8.2 %collective-permute-start = (bf16[8,3072]{1,0:T(8,128)(2,1)S(1)}, bf16[8,3072]{1,0:T(8,128)(2,1)S(1)}, u32[]{:S(2)}, u32[]{:S(2)}) collective-permute-start(bf16[8,3072]{1,0:T(8,128)(2,1)S(1)} %constant_dynamic-update-slice_fusion.refs_0_), channel_id=1, source_target_pairs={{0,1},{1,0},{2,3},{3,2},{4,5},{5,4},{6,7},{7,6},{8,9},{9,8},{10,11... | collective-permute-start | bytes 147464 | tf_op jit(solution)/shard_map/ppermute | solution.py:497
  5.1 5.9 %collective-permute-start.1 = (bf16[8,3072]{1,0:T(8,128)(2,1)S(1)}, bf16[8,3072]{1,0:T(8,128)(2,1)S(1)}, u32[]{:S(2)}, u32[]{:S(2)}) collective-permute-start(bf16[8,3072]{1,0:T(8,128)(2,1)S(1)} %constant_dynamic-update-slice_fusion.refs_0_), channel_id=1, source_target_pairs={{0,2},{1,3},{2,0},{3,1},{4,6},{5,7},{6,4},{7,5},{8,10},{9,11},{10,... | collective-permute-start | bytes 147464 | tf_op jit(solution)/shard_map/ppermute | solution.py:497
  7.7 5.9 %collective-permute-start.2 = (bf16[8,3072]{1,0:T(8,128)(2,1)S(1)}, bf16[8,3072]{1,0:T(8,128)(2,1)S(1)}, u32[]{:S(2)}, u32[]{:S(2)}) collective-permute-start(bf16[8,3072]{1,0:T(8,128)(2,1)S(1)} %constant_dynamic-update-slice_fusion.refs_0_), channel_id=1, source_target_pairs={{0,3},{1,2},{2,1},{3,0},{4,7},{5,6},{6,5},{7,4},{8,11},{9,10},{10,... | collective-permute-start | bytes 147464 | tf_op jit(solution)/shard_map/ppermute | solution.py:497
  13.9 8.2 %collective-permute-start.3 = (bf16[24,3072]{1,0:T(8,128)(2,1)S(1)}, bf16[24,3072]{1,0:T(8,128)(2,1)S(1)}, u32[]{:S(2)}, u32[]{:S(2)}) collective-permute-start(bf16[24,3072]{1,0:T(8,128)(2,1)S(1)} %get-tuple-element.17), channel_id=1, source_target_pairs={{0,8},{4,12},{8,0},{12,4},{16,24},{20,28},{24,16},{28,20},{1,9},{5... | collective-permute-start | bytes 442376 | tf_op jit(solution)/shard_map/ppermute | solution.py:527
  15.5 7.7 %collective-permute-start.4 = (bf16[24,3072]{1,0:T(8,128)(2,1)S(1)}, bf16[24,3072]{1,0:T(8,128)(2,1)S(1)}, u32[]{:S(2)}, u32[]{:S(2)}) collective-permute-start(bf16[24,3072]{1,0:T(8,128)(2,1)S(1)} %get-tuple-element.18), channel_id=1, source_target_pairs={{0,16},{4,20},{8,24},{12,28},{16,0},{20,4},{24,8},{28,12},{1,17},{... | collective-permute-start | bytes 442376 | tf_op jit(solution)/shard_map/ppermute | solution.py:527
  17.0 6.2 %collective-permute-start.5 = (bf16[24,3072]{1,0:T(8,128)(2,1)S(1)}, bf16[24,3072]{1,0:T(8,128)(2,1)S(1)}, u32[]{:S(2)}, u32[]{:S(2)}) collective-permute-start(bf16[24,3072]{1,0:T(8,128)(2,1)S(1)} %get-tuple-element.19), channel_id=1, source_target_pairs={{0,24},{4,28},{8,16},{12,20},{16,8},{20,12},{24,0},{28,4},{1,25},{... | collective-permute-start | bytes 442376 | tf_op jit(solution)/shard_map/ppermute | solution.py:527
  17.5 6.4 %collective-permute-start.6 = (bf16[24,3072]{1,0:T(8,128)(2,1)S(1)}, bf16[24,3072]{1,0:T(8,128)(2,1)S(1)}, u32[]{:S(2)}, u32[]{:S(2)}) collective-permute-start(bf16[24,3072]{1,0:T(8,128)(2,1)S(1)} %get-tuple-element.16.after_ref.refs_3_), channel_id=1, source_target_pairs={{0,4},{4,0},{8,12},{12,8},{16,20},{20,16},{24,28},{28,24},{1,5},{5... | collective-permute-start | bytes 442376 | tf_op jit(solution)/shard_map/ppermute | solution.py:535
  22.1 1.7 %collective-permute-start.7 = (bf16[24,3072]{1,0:T(8,128)(2,1)S(1)}, bf16[24,3072]{1,0:T(8,128)(2,1)S(1)}, u32[]{:S(2)}, u32[]{:S(2)}) collective-permute-start(bf16[24,3072]{1,0:T(8,128)(2,1)S(1)} %collective-permute-done.3.refs_4_), channel_id=1, source_target_pairs={{0,4},{4,0},{8,12},{12,8},{16,20},{20,16},{24,28},{28,24},{1,5},{5... | collective-permute-start | bytes 442376 | tf_op jit(solution)/shard_map/ppermute | solution.py:535
  23.2 1.4 %collective-permute-start.8 = (bf16[24,3072]{1,0:T(8,128)(2,1)S(1)}, bf16[24,3072]{1,0:T(8,128)(2,1)S(1)}, u32[]{:S(2)}, u32[]{:S(2)}) collective-permute-start(bf16[24,3072]{1,0:T(8,128)(2,1)S(1)} %collective-permute-done.4.refs_5_), channel_id=1, source_target_pairs={{0,4},{4,0},{8,12},{12,8},{16,20},{20,16},{24,28},{28,24},{1,5},{5... | collective-permute-start | bytes 442376 | tf_op jit(solution)/shard_map/ppermute | solution.py:535
  23.2 1.6 %collective-permute-start.9 = (bf16[24,3072]{1,0:T(8,128)(2,1)S(1)}, bf16[24,3072]{1,0:T(8,128)(2,1)S(1)}, u32[]{:S(2)}, u32[]{:S(2)}) collective-permute-start(bf16[24,3072]{1,0:T(8,128)(2,1)S(1)} %add.22.refs_6_), channel_id=1, source_target_pairs={{0,4},{4,0},{8,12},{12,8},{16,20},{20,16},{24,28},{28,24},{1,5},{5... | collective-permute-start | bytes 442376 | tf_op jit(solution)/shard_map/ppermute | solution.py:535
  24.8 34.1 %copy-start = (s32[8,2]{0,1:T(2,128)S(1)}, s32[8,2]{0,1:T(2,128)}, u32[]{:S(2)}) copy-start(s32[8,2]{0,1:T(2,128)} %param.8) | copy-start | bytes 196
  24.8 51.4 %copy-start.1 = (f32[8,2]{0,1:T(2,128)S(1)}, f32[8,2]{0,1:T(2,128)}, u32[]{:S(2)}) copy-start(f32[8,2]{0,1:T(2,128)} %param.9) | copy-start | bytes 196
  58.4 2.1 %collective-permute-start.10 = (bf16[96,3200]{1,0:T(8,128)(2,1)S(1)}, bf16[96,3200]{1,0:T(8,128)(2,1)S(1)}, u32[]{:S(2)}, u32[]{:S(2)}) collective-permute-start(bf16[96,3200]{1,0:T(8,128)(2,1)S(1)} %get-tuple-element.24), channel_id=1, source_target_pairs={{0,4},{4,0},{8,12},{12,8},{16,20},{20,16},{24,28},{28,24},{1,5},{5... | collective-permute-start | bytes 1843208 | tf_op jit(solution)/shard_map/ppermute | solution.py:553
  60.7 6.9 %collective-permute-start.11 = (bf16[24,3200]{1,0:T(8,128)(2,1)S(1)}, bf16[24,3200]{1,0:T(8,128)(2,1)S(1)}, u32[]{:S(2)}, u32[]{:S(2)}) collective-permute-start(bf16[24,3200]{1,0:T(8,128)(2,1)S(1)} %get-tuple-element.50), channel_id=1, source_target_pairs={{0,8},{4,12},{8,0},{12,4},{16,24},{20,28},{24,16},{28,20},{1,9},{5... | collective-permute-start | bytes 460808 | tf_op jit(solution)/shard_map/ppermute | solution.py:555
  61.8 9.2 %collective-permute-start.12 = (bf16[24,3200]{1,0:T(8,128)(2,1)S(1)}, bf16[24,3200]{1,0:T(8,128)(2,1)S(1)}, u32[]{:S(2)}, u32[]{:S(2)}) collective-permute-start(bf16[24,3200]{1,0:T(8,128)(2,1)S(1)} %get-tuple-element.49), channel_id=1, source_target_pairs={{0,16},{4,20},{8,24},{12,28},{16,0},{20,4},{24,8},{28,12},{1,17},{... | collective-permute-start | bytes 460808 | tf_op jit(solution)/shard_map/ppermute | solution.py:555
  63.3 7.7 %collective-permute-start.13 = (bf16[24,3200]{1,0:T(8,128)(2,1)S(1)}, bf16[24,3200]{1,0:T(8,128)(2,1)S(1)}, u32[]{:S(2)}, u32[]{:S(2)}) collective-permute-start(bf16[24,3200]{1,0:T(8,128)(2,1)S(1)} %get-tuple-element.48), channel_id=1, source_target_pairs={{0,24},{4,28},{8,16},{12,20},{16,8},{20,12},{24,0},{28,4},{1,25},{... | collective-permute-start | bytes 460808 | tf_op jit(solution)/shard_map/ppermute | solution.py:555
  71.8 6.1 %collective-permute-start.16 = (bf16[8,3200]{1,0:T(8,128)(2,1)S(1)}, bf16[8,3200]{1,0:T(8,128)(2,1)S(1)}, u32[]{:S(2)}, u32[]{:S(2)}) collective-permute-start(bf16[8,3200]{1,0:T(8,128)(2,1)S(1)} %get-tuple-element.28), channel_id=1, source_target_pairs={{0,3},{1,2},{2,1},{3,0},{4,7},{5,6},{6,5},{7,4},{8,11},{9,10},{10,... | collective-permute-start | bytes 153608 | tf_op jit(solution)/shard_map/ppermute | solution.py:559
  72.7 6.1 %collective-permute-start.15 = (bf16[8,3200]{1,0:T(8,128)(2,1)S(1)}, bf16[8,3200]{1,0:T(8,128)(2,1)S(1)}, u32[]{:S(2)}, u32[]{:S(2)}) collective-permute-start(bf16[8,3200]{1,0:T(8,128)(2,1)S(1)} %get-tuple-element.27), channel_id=1, source_target_pairs={{0,2},{1,3},{2,0},{3,1},{4,6},{5,7},{6,4},{7,5},{8,10},{9,11},{10,... | collective-permute-start | bytes 153608 | tf_op jit(solution)/shard_map/ppermute | solution.py:559
  72.7 6.1 %collective-permute-start.14 = (bf16[8,3200]{1,0:T(8,128)(2,1)S(1)}, bf16[8,3200]{1,0:T(8,128)(2,1)S(1)}, u32[]{:S(2)}, u32[]{:S(2)}) collective-permute-start(bf16[8,3200]{1,0:T(8,128)(2,1)S(1)} %get-tuple-element.26), channel_id=1, source_target_pairs={{0,1},{1,0},{2,3},{3,2},{4,5},{5,4},{6,7},{7,6},{8,9},{9,8},{10,11... | collective-permute-start | bytes 153608 | tf_op jit(solution)/shard_map/ppermute | solution.py:559

commit v5 on v4

--- a/solution.py
+++ b/solution.py
@@ -493,7 +493,7 @@
     def to_slice(i):
         return [(z, z ^ i) for z in range(n_et)]
 
-    both = jnp.concatenate([tokens, out_grad], axis=1)
+    both = jnp.pad(tokens, [(0, 0), (0, width)]) + jnp.pad(out_grad, [(0, 0), (width, 0)])
     pieces = [both] + [lax.ppermute(both, "et", to_slice(i)) for i in range(1, n_et)]
 
     rel = jnp.bitwise_xor(expert_ids, q)

time: 80.4 us -> 79.6 us (0.990)
  local copies, waits for them, and re-layouts: 4.02 us -> 2.54 us
where the time goes in v5:
time: 79.6 us; the launch traced here: 79.4 us
  Pallas kernels  39.2 us (49%)
  starting transfers between devices  18.8 us (24%)
  waiting for transfers between devices  15.4 us (19%)
  other arithmetic  2.71 us (3%)
  local copies, waits for them, and re-layouts  2.54 us (3%)
    pallas_call x1, Pallas kernels, tiled_experts(): pl.pallas_call(functools.partial(tiled_kernel, n_et, width, members, accs...  33.6 us
    ppermute x3, waiting for transfers between devices, body(): lax.ppermute(back[r], 'de', to_expert(r))  6.61 us
    ppermute x3, starting transfers between devices, body(): lax.ppermute(both, 'et', to_slice(i))  5.62 us
    pallas_call x1, Pallas kernels, first_chunk(): pl.pallas_call(first_chunk_kernel, in_specs=[pl.BlockSpec(memory_space=pl...  4.64 us
    ppermute x3, starting transfers between devices, body(): result += lax.ppermute(ends[i], 'et', to_slice(i)).astype(F32)  4.45 us
    ppermute x3, starting transfers between devices, body(): lax.ppermute(back[r], 'de', to_expert(r))  3.57 us
    ppermute x3, starting transfers between devices, body(): lax.ppermute(rows_of[r], 'de', to_expert(r))  3.55 us
    ppermute x3, waiting for transfers between devices, body(): lax.ppermute(both, 'et', to_slice(i))  3.3 us
  transfers between devices with their start and end apart: 17, of which 10 were waited for; matrix products, arithmetic and copies ran while one was open for 4% of the time, Pallas kernels for 6%

profile of v5, /device:TPU:0, one launch (start us, length us, event | category | flops | bytes accessed | tf_op | source)
XLA Modules:
  0.0 79.4 jit_solution(3479408181362291028)
XLA Ops:
  0.6 0.8 pad_add_fusion.refs_0_
  1.4 3.0 %collective-permute-start = (bf16[8,3072]{1,0:T(8,128)(2,1)S(1)}, bf16[8,3072]{1,0:T(8,128)(2,1)S(1)}, u32[]{:S(2)}, u32[]{:S(2)}) collective-permute-start(bf16[8,3072]{1,0:T(8,128)(2,1)S(1)} %pad_add_fusion.refs_0_), channel_id=1, source_target_pairs={{0,1},{1,0},{2,3},{3,2},{4,5},{5,4},{6,7},{7,6},{8,9},{9,8},{10,11... | collective-permute-start | bytes 147464 | tf_op jit(solution)/shard_map/ppermute | solution.py:497
  4.4 2.6 %collective-permute-start.1 = (bf16[8,3072]{1,0:T(8,128)(2,1)S(1)}, bf16[8,3072]{1,0:T(8,128)(2,1)S(1)}, u32[]{:S(2)}, u32[]{:S(2)}) collective-permute-start(bf16[8,3072]{1,0:T(8,128)(2,1)S(1)} %pad_add_fusion.refs_0_), channel_id=1, source_target_pairs={{0,2},{1,3},{2,0},{3,1},{4,6},{5,7},{6,4},{7,5},{8,10},{9,11},{10,... | collective-permute-start | bytes 147464 | tf_op jit(solution)/shard_map/ppermute | solution.py:497
  7.0 0.7 broadcast_xor_fusion
  7.7 0.7 select_reduce_fusion
  9.6 0.7 collective-permute-done.1.refs_2_
  10.3 2.6 %collective-permute-done.2.refs_3_ = bf16[8,3072]{1,0:T(8,128)(2,1)S(1)} collective-permute-done((bf16[8,3072]{1,0:T(8,128)(2,1)S(1)}, bf16[8,3072]{1,0:T(8,128)(2,1)S(1)}, u32[]{:S(2)}, u32[]{:S(2)}) %collective-permute-start.2) | collective-permute-done | bytes 49184 | tf_op jit(solution)/shard_map/ppermute | solution.py:497
  12.9 0.3 shard_map.94
  13.2 1.6 %collective-permute-start.3 = (bf16[24,3072]{1,0:T(8,128)(2,1)S(1)}, bf16[24,3072]{1,0:T(8,128)(2,1)S(1)}, u32[]{:S(2)}, u32[]{:S(2)}) collective-permute-start(bf16[24,3072]{1,0:T(8,128)(2,1)S(1)} %get-tuple-element.17), channel_id=1, source_target_pairs={{0,8},{4,12},{8,0},{12,4},{16,24},{20,28},{24,16},{28,20},{1,9},{5... | collective-permute-start | bytes 442376 | tf_op jit(solution)/shard_map/ppermute | solution.py:527
  14.7 1.5 %collective-permute-start.4 = (bf16[24,3072]{1,0:T(8,128)(2,1)S(1)}, bf16[24,3072]{1,0:T(8,128)(2,1)S(1)}, u32[]{:S(2)}, u32[]{:S(2)}) collective-permute-start(bf16[24,3072]{1,0:T(8,128)(2,1)S(1)} %get-tuple-element.18), channel_id=1, source_target_pairs={{0,16},{4,20},{8,24},{12,28},{16,0},{20,4},{24,8},{28,12},{1,17},{... | collective-permute-start | bytes 442376 | tf_op jit(solution)/shard_map/ppermute | solution.py:527
  16.3 0.5 collective-permute-start.5
  16.7 4.6 %shard_map.95 = (bf16[6144,512]{1,0:T(8,128)(2,1)S(1)}, bf16[6144,512]{1,0:T(8,128)(2,1)S(1)}, bf16[24,3072]{1,0:T(8,128)(2,1)S(1)}) custom-call(bf16[24,3072]{1,0:T(8,128)(2,1)S(1)} %get-tuple-element.16.after_ref.refs_3_, bf16[6144,2048]{1,0:T(8,128)(2,1)} %refs_0_.1, bf16[6144,2048]{1,0:T(8,128)(2,1)} %refs_1_.1), custom_call_target="tpu_custom_call" | custom-call | bytes 25165824 | tf_op jit(solution)/shard_map/pallas_call | solution.py:182
  21.4 0.6 collective-permute-start.7
  22.0 0.5 collective-permute-done.4.refs_5_
  22.5 0.6 collective-permute-start.9
  23.1 0.7 collective-permute-done.8.refs_9_
  23.8 0.3 collective-permute-done.9.refs_10_
  24.1 33.6 %shard_map.96 = (bf16[96,3200]{1,0:T(8,128)(2,1)S(1)}, bf16[96,3200]{1,0:T(8,128)(2,1)S(1)}, bf16[6144,512]{1,0:T(8,128)(2,1)S(1)}, bf16[6144,512]{1,0:T(8,128)(2,1)S(1)}) custom-call(bf16[6144,2048]{1,0:T(8,128)(2,1)} %refs_0_.1, bf16[6144,2048]{1,0:T(8,128)(2,1)} %refs_1_.1, ...), custom_call_target="tpu_custom_call", output_to_operand_aliasing={{2}: (11, {}), {3}: (12, {})} | custom-call | flops 7247757312 | bytes 75497472 | tf_op jit(solution)/shard_map/pallas_call | solution.py:448
  57.7 0.4 collective-permute-start.10
  58.3 1.5 %collective-permute-done.10 = bf16[96,3200]{1,0:T(8,128)(2,1)S(1)} collective-permute-done((bf16[96,3200]{1,0:T(8,128)(2,1)S(1)}, bf16[96,3200]{1,0:T(8,128)(2,1)S(1)}, u32[]{:S(2)}, u32[]{:S(2)}) %collective-permute-start.10) | collective-permute-done | bytes 614432 | tf_op jit(solution)/shard_map/ppermute | solution.py:553
  60.0 1.1 %collective-permute-start.11 = (bf16[24,3200]{1,0:T(8,128)(2,1)S(1)}, bf16[24,3200]{1,0:T(8,128)(2,1)S(1)}, u32[]{:S(2)}, u32[]{:S(2)}) collective-permute-start(bf16[24,3200]{1,0:T(8,128)(2,1)S(1)} %get-tuple-element.50), channel_id=1, source_target_pairs={{0,8},{4,12},{8,0},{12,4},{16,24},{20,28},{24,16},{28,20},{1,9},{5... | collective-permute-start | bytes 460808 | tf_op jit(solution)/shard_map/ppermute | solution.py:555
  61.1 1.5 %collective-permute-start.12 = (bf16[24,3200]{1,0:T(8,128)(2,1)S(1)}, bf16[24,3200]{1,0:T(8,128)(2,1)S(1)}, u32[]{:S(2)}, u32[]{:S(2)}) collective-permute-start(bf16[24,3200]{1,0:T(8,128)(2,1)S(1)} %get-tuple-element.49), channel_id=1, source_target_pairs={{0,16},{4,20},{8,24},{12,28},{16,0},{20,4},{24,8},{28,12},{1,17},{... | collective-permute-start | bytes 460808 | tf_op jit(solution)/shard_map/ppermute | solution.py:555
  62.6 0.9 %collective-permute-start.13 = (bf16[24,3200]{1,0:T(8,128)(2,1)S(1)}, bf16[24,3200]{1,0:T(8,128)(2,1)S(1)}, u32[]{:S(2)}, u32[]{:S(2)}) collective-permute-start(bf16[24,3200]{1,0:T(8,128)(2,1)S(1)} %get-tuple-element.48), channel_id=1, source_target_pairs={{0,24},{4,28},{8,16},{12,20},{16,8},{20,12},{24,0},{28,4},{1,25},{... | collective-permute-start | bytes 460808 | tf_op jit(solution)/shard_map/ppermute | solution.py:555
  63.7 3.1 %collective-permute-done.11.refs_1_ = bf16[24,3200]{1,0:T(8,128)(2,1)S(1)} collective-permute-done((bf16[24,3200]{1,0:T(8,128)(2,1)S(1)}, bf16[24,3200]{1,0:T(8,128)(2,1)S(1)}, u32[]{:S(2)}, u32[]{:S(2)}) %collective-permute-start.11) | collective-permute-done | bytes 153632 | tf_op jit(solution)/shard_map/ppermute | solution.py:555
  66.8 3.5 %collective-permute-done.12.refs_2_ = bf16[24,3200]{1,0:T(8,128)(2,1)S(1)} collective-permute-done((bf16[24,3200]{1,0:T(8,128)(2,1)S(1)}, bf16[24,3200]{1,0:T(8,128)(2,1)S(1)}, u32[]{:S(2)}, u32[]{:S(2)}) %collective-permute-start.12) | collective-permute-done | bytes 153632 | tf_op jit(solution)/shard_map/ppermute | solution.py:555
  70.3 0.7 shard_map.97
  71.1 0.9 %collective-permute-start.16 = (bf16[8,3200]{1,0:T(8,128)(2,1)S(1)}, bf16[8,3200]{1,0:T(8,128)(2,1)S(1)}, u32[]{:S(2)}, u32[]{:S(2)}) collective-permute-start(bf16[8,3200]{1,0:T(8,128)(2,1)S(1)} %get-tuple-element.28), channel_id=1, source_target_pairs={{0,3},{1,2},{2,1},{3,0},{4,7},{5,6},{6,5},{7,4},{8,11},{9,10},{10,... | collective-permute-start | bytes 153608 | tf_op jit(solution)/shard_map/ppermute | solution.py:559
  72.0 3.5 %collective-permute-start.14 = (bf16[8,3200]{1,0:T(8,128)(2,1)S(1)}, bf16[8,3200]{1,0:T(8,128)(2,1)S(1)}, u32[]{:S(2)}, u32[]{:S(2)}) collective-permute-start(bf16[8,3200]{1,0:T(8,128)(2,1)S(1)} %get-tuple-element.26), channel_id=1, source_target_pairs={{0,1},{1,0},{2,3},{3,2},{4,5},{5,4},{6,7},{7,6},{8,9},{9,8},{10,11... | collective-permute-start | bytes 153608 | tf_op jit(solution)/shard_map/ppermute | solution.py:559
  75.6 1.6 %collective-permute-done.16 = bf16[8,3200]{1,0:T(8,128)(2,1)S(1)} collective-permute-done((bf16[8,3200]{1,0:T(8,128)(2,1)S(1)}, bf16[8,3200]{1,0:T(8,128)(2,1)S(1)}, u32[]{:S(2)}, u32[]{:S(2)}) %collective-permute-start.16) | collective-permute-done | bytes 51232 | tf_op jit(solution)/shard_map/ppermute | solution.py:559
  77.2 0.9 %collective-permute-done.15 = bf16[8,3200]{1,0:T(8,128)(2,1)S(1)} collective-permute-done((bf16[8,3200]{1,0:T(8,128)(2,1)S(1)}, bf16[8,3200]{1,0:T(8,128)(2,1)S(1)}, u32[]{:S(2)}, u32[]{:S(2)}) %collective-permute-start.15) | collective-permute-done | bytes 51232 | tf_op jit(solution)/shard_map/ppermute | solution.py:559
  78.1 0.6 fusion.6
  78.8 0.6 copy.55
  (46 shorter events, 1.9 us)
Async XLA Ops:
  1.4 8.2 %collective-permute-start = (bf16[8,3072]{1,0:T(8,128)(2,1)S(1)}, bf16[8,3072]{1,0:T(8,128)(2,1)S(1)}, u32[]{:S(2)}, u32[]{:S(2)}) collective-permute-start(bf16[8,3072]{1,0:T(8,128)(2,1)S(1)} %pad_add_fusion.refs_0_), channel_id=1, source_target_pairs={{0,1},{1,0},{2,3},{3,2},{4,5},{5,4},{6,7},{7,6},{8,9},{9,8},{10,11... | collective-permute-start | bytes 147464 | tf_op jit(solution)/shard_map/ppermute | solution.py:497
  4.4 5.9 %collective-permute-start.1 = (bf16[8,3072]{1,0:T(8,128)(2,1)S(1)}, bf16[8,3072]{1,0:T(8,128)(2,1)S(1)}, u32[]{:S(2)}, u32[]{:S(2)}) collective-permute-start(bf16[8,3072]{1,0:T(8,128)(2,1)S(1)} %pad_add_fusion.refs_0_), channel_id=1, source_target_pairs={{0,2},{1,3},{2,0},{3,1},{4,6},{5,7},{6,4},{7,5},{8,10},{9,11},{10,... | collective-permute-start | bytes 147464 | tf_op jit(solution)/shard_map/ppermute | solution.py:497
  7.0 5.9 %collective-permute-start.2 = (bf16[8,3072]{1,0:T(8,128)(2,1)S(1)}, bf16[8,3072]{1,0:T(8,128)(2,1)S(1)}, u32[]{:S(2)}, u32[]{:S(2)}) collective-permute-start(bf16[8,3072]{1,0:T(8,128)(2,1)S(1)} %pad_add_fusion.refs_0_), channel_id=1, source_target_pairs={{0,3},{1,2},{2,1},{3,0},{4,7},{5,6},{6,5},{7,4},{8,11},{9,10},{10,... | collective-permute-start | bytes 147464 | tf_op jit(solution)/shard_map/ppermute | solution.py:497
  13.2 8.2 %collective-permute-start.3 = (bf16[24,3072]{1,0:T(8,128)(2,1)S(1)}, bf16[24,3072]{1,0:T(8,128)(2,1)S(1)}, u32[]{:S(2)}, u32[]{:S(2)}) collective-permute-start(bf16[24,3072]{1,0:T(8,128)(2,1)S(1)} %get-tuple-element.17), channel_id=1, source_target_pairs={{0,8},{4,12},{8,0},{12,4},{16,24},{20,28},{24,16},{28,20},{1,9},{5... | collective-permute-start | bytes 442376 | tf_op jit(solution)/shard_map/ppermute | solution.py:527
  14.7 7.7 %collective-permute-start.4 = (bf16[24,3072]{1,0:T(8,128)(2,1)S(1)}, bf16[24,3072]{1,0:T(8,128)(2,1)S(1)}, u32[]{:S(2)}, u32[]{:S(2)}) collective-permute-start(bf16[24,3072]{1,0:T(8,128)(2,1)S(1)} %get-tuple-element.18), channel_id=1, source_target_pairs={{0,16},{4,20},{8,24},{12,28},{16,0},{20,4},{24,8},{28,12},{1,17},{... | collective-permute-start | bytes 442376 | tf_op jit(solution)/shard_map/ppermute | solution.py:527
  16.3 6.2 %collective-permute-start.5 = (bf16[24,3072]{1,0:T(8,128)(2,1)S(1)}, bf16[24,3072]{1,0:T(8,128)(2,1)S(1)}, u32[]{:S(2)}, u32[]{:S(2)}) collective-permute-start(bf16[24,3072]{1,0:T(8,128)(2,1)S(1)} %get-tuple-element.19), channel_id=1, source_target_pairs={{0,24},{4,28},{8,16},{12,20},{16,8},{20,12},{24,0},{28,4},{1,25},{... | collective-permute-start | bytes 442376 | tf_op jit(solution)/shard_map/ppermute | solution.py:527
  16.7 6.3 %collective-permute-start.6 = (bf16[24,3072]{1,0:T(8,128)(2,1)S(1)}, bf16[24,3072]{1,0:T(8,128)(2,1)S(1)}, u32[]{:S(2)}, u32[]{:S(2)}) collective-permute-start(bf16[24,3072]{1,0:T(8,128)(2,1)S(1)} %get-tuple-element.16.after_ref.refs_3_), channel_id=1, source_target_pairs={{0,4},{4,0},{8,12},{12,8},{16,20},{20,16},{24,28},{28,24},{1,5},{5... | collective-permute-start | bytes 442376 | tf_op jit(solution)/shard_map/ppermute | solution.py:535
  21.4 1.7 %collective-permute-start.7 = (bf16[24,3072]{1,0:T(8,128)(2,1)S(1)}, bf16[24,3072]{1,0:T(8,128)(2,1)S(1)}, u32[]{:S(2)}, u32[]{:S(2)}) collective-permute-start(bf16[24,3072]{1,0:T(8,128)(2,1)S(1)} %collective-permute-done.3.refs_4_), channel_id=1, source_target_pairs={{0,4},{4,0},{8,12},{12,8},{16,20},{20,16},{24,28},{28,24},{1,5},{5... | collective-permute-start | bytes 442376 | tf_op jit(solution)/shard_map/ppermute | solution.py:535
  22.4 1.4 %collective-permute-start.8 = (bf16[24,3072]{1,0:T(8,128)(2,1)S(1)}, bf16[24,3072]{1,0:T(8,128)(2,1)S(1)}, u32[]{:S(2)}, u32[]{:S(2)}) collective-permute-start(bf16[24,3072]{1,0:T(8,128)(2,1)S(1)} %collective-permute-done.4.refs_5_), channel_id=1, source_target_pairs={{0,4},{4,0},{8,12},{12,8},{16,20},{20,16},{24,28},{28,24},{1,5},{5... | collective-permute-start | bytes 442376 | tf_op jit(solution)/shard_map/ppermute | solution.py:535
  22.5 1.6 %collective-permute-start.9 = (bf16[24,3072]{1,0:T(8,128)(2,1)S(1)}, bf16[24,3072]{1,0:T(8,128)(2,1)S(1)}, u32[]{:S(2)}, u32[]{:S(2)}) collective-permute-start(bf16[24,3072]{1,0:T(8,128)(2,1)S(1)} %add.30.refs_6_), channel_id=1, source_target_pairs={{0,4},{4,0},{8,12},{12,8},{16,20},{20,16},{24,28},{28,24},{1,5},{5... | collective-permute-start | bytes 442376 | tf_op jit(solution)/shard_map/ppermute | solution.py:535
  24.1 34.1 %copy-start = (s32[8,2]{0,1:T(2,128)S(1)}, s32[8,2]{0,1:T(2,128)}, u32[]{:S(2)}) copy-start(s32[8,2]{0,1:T(2,128)} %param.8) | copy-start | bytes 196
  24.1 51.4 %copy-start.1 = (f32[8,2]{0,1:T(2,128)S(1)}, f32[8,2]{0,1:T(2,128)}, u32[]{:S(2)}) copy-start(f32[8,2]{0,1:T(2,128)} %param.9) | copy-start | bytes 196
  57.7 2.1 %collective-permute-start.10 = (bf16[96,3200]{1,0:T(8,128)(2,1)S(1)}, bf16[96,3200]{1,0:T(8,128)(2,1)S(1)}, u32[]{:S(2)}, u32[]{:S(2)}) collective-permute-start(bf16[96,3200]{1,0:T(8,128)(2,1)S(1)} %get-tuple-element.24), channel_id=1, source_target_pairs={{0,4},{4,0},{8,12},{12,8},{16,20},{20,16},{24,28},{28,24},{1,5},{5... | collective-permute-start | bytes 1843208 | tf_op jit(solution)/shard_map/ppermute | solution.py:553
  60.0 6.9 %collective-permute-start.11 = (bf16[24,3200]{1,0:T(8,128)(2,1)S(1)}, bf16[24,3200]{1,0:T(8,128)(2,1)S(1)}, u32[]{:S(2)}, u32[]{:S(2)}) collective-permute-start(bf16[24,3200]{1,0:T(8,128)(2,1)S(1)} %get-tuple-element.50), channel_id=1, source_target_pairs={{0,8},{4,12},{8,0},{12,4},{16,24},{20,28},{24,16},{28,20},{1,9},{5... | collective-permute-start | bytes 460808 | tf_op jit(solution)/shard_map/ppermute | solution.py:555
  61.1 9.2 %collective-permute-start.12 = (bf16[24,3200]{1,0:T(8,128)(2,1)S(1)}, bf16[24,3200]{1,0:T(8,128)(2,1)S(1)}, u32[]{:S(2)}, u32[]{:S(2)}) collective-permute-start(bf16[24,3200]{1,0:T(8,128)(2,1)S(1)} %get-tuple-element.49), channel_id=1, source_target_pairs={{0,16},{4,20},{8,24},{12,28},{16,0},{20,4},{24,8},{28,12},{1,17},{... | collective-permute-start | bytes 460808 | tf_op jit(solution)/shard_map/ppermute | solution.py:555
  62.6 7.7 %collective-permute-start.13 = (bf16[24,3200]{1,0:T(8,128)(2,1)S(1)}, bf16[24,3200]{1,0:T(8,128)(2,1)S(1)}, u32[]{:S(2)}, u32[]{:S(2)}) collective-permute-start(bf16[24,3200]{1,0:T(8,128)(2,1)S(1)} %get-tuple-element.48), channel_id=1, source_target_pairs={{0,24},{4,28},{8,16},{12,20},{16,8},{20,12},{24,0},{28,4},{1,25},{... | collective-permute-start | bytes 460808 | tf_op jit(solution)/shard_map/ppermute | solution.py:555
  71.1 6.1 %collective-permute-start.16 = (bf16[8,3200]{1,0:T(8,128)(2,1)S(1)}, bf16[8,3200]{1,0:T(8,128)(2,1)S(1)}, u32[]{:S(2)}, u32[]{:S(2)}) collective-permute-start(bf16[8,3200]{1,0:T(8,128)(2,1)S(1)} %get-tuple-element.28), channel_id=1, source_target_pairs={{0,3},{1,2},{2,1},{3,0},{4,7},{5,6},{6,5},{7,4},{8,11},{9,10},{10,... | collective-permute-start | bytes 153608 | tf_op jit(solution)/shard_map/ppermute | solution.py:559
  72.0 6.1 %collective-permute-start.15 = (bf16[8,3200]{1,0:T(8,128)(2,1)S(1)}, bf16[8,3200]{1,0:T(8,128)(2,1)S(1)}, u32[]{:S(2)}, u32[]{:S(2)}) collective-permute-start(bf16[8,3200]{1,0:T(8,128)(2,1)S(1)} %get-tuple-element.27), channel_id=1, source_target_pairs={{0,2},{1,3},{2,0},{3,1},{4,6},{5,7},{6,4},{7,5},{8,10},{9,11},{10,... | collective-permute-start | bytes 153608 | tf_op jit(solution)/shard_map/ppermute | solution.py:559
  72.0 6.1 %collective-permute-start.14 = (bf16[8,3200]{1,0:T(8,128)(2,1)S(1)}, bf16[8,3200]{1,0:T(8,128)(2,1)S(1)}, u32[]{:S(2)}, u32[]{:S(2)}) collective-permute-start(bf16[8,3200]{1,0:T(8,128)(2,1)S(1)} %get-tuple-element.26), channel_id=1, source_target_pairs={{0,1},{1,0},{2,3},{3,2},{4,5},{5,4},{6,7},{7,6},{8,9},{9,8},{10,11... | collective-permute-start | bytes 153608 | tf_op jit(solution)/shard_map/ppermute | solution.py:559

commit v6 on v5

--- a/solution.py
+++ b/solution.py
@@ -425,7 +425,7 @@
                 for op, _ in both:
                     op(i % 2)
                 late.append([end for _, end in both if end is not None])
-                if len(late) > 2:
+                if len(late) > 4:
                     for end in late.pop(0):
                         end()
             for ends in late:
@@ -515,15 +515,21 @@
         return jnp.pad(a, [(0, sent - used if d == axis else 0) for d in range(a.ndim)])
 
     same = jnp.eye(n_et, dtype=F32)
-    pick = place[:, None, :, None, :] * same[None, :, None, :, None]
-    pick = padded(pick.reshape(EXPERTS, used, n_et * count), 1).reshape(EXPERTS * sent, n_et * count)
+
+    def one_hot(same):
+        pick = place[:, None, :, None, :] * same[None, :, None, :, None]
+        pick = padded(pick.reshape(EXPERTS, used, n_et * count), 1)
+        return pick.reshape(EXPERTS * sent, n_et * count)
+
+    pick = one_hot(same)
+    order = [0, *range(n_et - 1, 0, -1)]
     scale = jnp.broadcast_to(slot_weight[:, None, :], (EXPERTS, n_et, CAP)).reshape(EXPERTS, used)
     scale = padded(scale, 1).reshape(EXPERTS * sent, 1)
     first = place * picks.transpose(1, 2, 0)[:, :, None, :]
     first = jnp.pad(first, [(0, 0), (0, 0), (0, sent - CAP), (0, 0)])
     first = first.transpose(0, 3, 1, 2).reshape(top * count, EXPERTS * sent)
 
-    rows_of = select(pick.astype(BF16), scale, pieces)
+    rows_of = select(one_hot(same[:, jnp.array(order)]).astype(BF16), scale, [pieces[i] for i in order])
     mine = [rows_of[0]] + [lax.ppermute(rows_of[r], "de", to_expert(r)) for r in range(1, EXPERTS)]
     rows = members * EXPERTS * CAP
     pad = -rows % 16

time: 79.6 us -> 79.7 us (level)
  waiting for transfers between devices: 15.4 us -> 13.9 us
  local copies, waits for them, and re-layouts: 2.54 us -> 3.36 us
    ppermute x3, waiting for transfers between devices: 3.3 us -> 0.53 us  [body(): lax.ppermute(both, 'et', to_slice(i))]
    ppermute x3, waiting for transfers between devices: 2.51 us -> 3.82 us  [body(): result += lax.ppermute(ends[i], 'et', to_slice(i)).astype(F32)]
  transfers between devices with their start and end apart: 17 -> 17, of which waited for: 10 -> 10; matrix products, arithmetic and copies ran while one was open for 4% -> 6% of each run, Pallas kernels for 6% -> 6%
where the time goes in v6:
time: 79.7 us; the launch traced here: 79.4 us
  Pallas kernels  39.2 us (49%)
  starting transfers between devices  18.8 us (24%)
  waiting for transfers between devices  13.9 us (17%)
  other arithmetic  3.37 us (4%)
  local copies, waits for them, and re-layouts  3.36 us (4%)
    pallas_call x1, Pallas kernels, tiled_experts(): pl.pallas_call(functools.partial(tiled_kernel, n_et, width, members, accs...  33.6 us
    ppermute x3, waiting for transfers between devices, body(): lax.ppermute(back[r], 'de', to_expert(r))  6.08 us
    ppermute x3, starting transfers between devices, body(): lax.ppermute(both, 'et', to_slice(i))  5.67 us
    pallas_call x1, Pallas kernels, first_chunk(): pl.pallas_call(first_chunk_kernel, in_specs=[pl.BlockSpec(memory_space=pl...  4.64 us
    ppermute x3, starting transfers between devices, body(): result += lax.ppermute(ends[i], 'et', to_slice(i)).astype(F32)  4.45 us
    ppermute x3, waiting for transfers between devices, body(): result += lax.ppermute(ends[i], 'et', to_slice(i)).astype(F32)  3.82 us
    ppermute x3, starting transfers between devices, body(): lax.ppermute(back[r], 'de', to_expert(r))  3.57 us
    ppermute x3, starting transfers between devices, body(): lax.ppermute(rows_of[r], 'de', to_expert(r))  3.55 us
  transfers between devices with their start and end apart: 17, of which 10 were waited for; matrix products, arithmetic and copies ran while one was open for 6% of the time, Pallas kernels for 6%

profile of v6, /device:TPU:0, one launch (start us, length us, event | category | flops | bytes accessed | tf_op | source)
XLA Modules:
  0.0 79.4 jit_solution(976727178279850371)
XLA Ops:
  0.6 0.8 pad_add_fusion.refs_0_
  1.4 5.0 %collective-permute-start = (bf16[8,3072]{1,0:T(8,128)(2,1)S(1)}, bf16[8,3072]{1,0:T(8,128)(2,1)S(1)}, u32[]{:S(2)}, u32[]{:S(2)}) collective-permute-start(bf16[8,3072]{1,0:T(8,128)(2,1)S(1)} %pad_add_fusion.refs_0_), channel_id=1, source_target_pairs={{0,3},{1,2},{2,1},{3,0},{4,7},{5,6},{6,5},{7,4},{8,11},{9,10},{10,... | collective-permute-start | bytes 147464 | tf_op jit(solution)/shard_map/ppermute | solution.py:497
  6.4 0.6 collective-permute-start.2
  7.1 0.7 broadcast_xor_fusion
  7.8 0.7 select_reduce_fusion
  8.8 0.7 pad_clamp_fusion
  9.5 0.6 gather_fusion
  10.9 0.5 collective-permute-done.1.refs_2_
  11.7 1.6 %collective-permute-start.3 = (bf16[24,3072]{1,0:T(8,128)(2,1)S(1)}, bf16[24,3072]{1,0:T(8,128)(2,1)S(1)}, u32[]{:S(2)}, u32[]{:S(2)}) collective-permute-start(bf16[24,3072]{1,0:T(8,128)(2,1)S(1)} %get-tuple-element.17), channel_id=1, source_target_pairs={{0,8},{4,12},{8,0},{12,4},{16,24},{20,28},{24,16},{28,20},{1,9},{5... | collective-permute-start | bytes 442376 | tf_op jit(solution)/shard_map/ppermute | solution.py:533
  13.3 1.5 %collective-permute-start.4 = (bf16[24,3072]{1,0:T(8,128)(2,1)S(1)}, bf16[24,3072]{1,0:T(8,128)(2,1)S(1)}, u32[]{:S(2)}, u32[]{:S(2)}) collective-permute-start(bf16[24,3072]{1,0:T(8,128)(2,1)S(1)} %get-tuple-element.18), channel_id=1, source_target_pairs={{0,16},{4,20},{8,24},{12,28},{16,0},{20,4},{24,8},{28,12},{1,17},{... | collective-permute-start | bytes 442376 | tf_op jit(solution)/shard_map/ppermute | solution.py:533
  14.8 0.5 collective-permute-start.5
  15.3 4.6 %shard_map.104 = (bf16[6144,512]{1,0:T(8,128)(2,1)S(1)}, bf16[6144,512]{1,0:T(8,128)(2,1)S(1)}, bf16[24,3072]{1,0:T(8,128)(2,1)S(1)}) custom-call(bf16[24,3072]{1,0:T(8,128)(2,1)S(1)} %get-tuple-element.16.after_ref.refs_3_, bf16[6144,2048]{1,0:T(8,128)(2,1)} %refs_0_.1, bf16[6144,2048]{1,0:T(8,128)(2,1)} %refs_1_.1), custom_call_target="tpu_custom_call" | custom-call | bytes 25165824 | tf_op jit(solution)/shard_map/pallas_call | solution.py:182
  19.9 0.6 collective-permute-start.7
  20.5 0.9 %collective-permute-done.4.refs_5_ = bf16[24,3072]{1,0:T(8,128)(2,1)S(1)} collective-permute-done((bf16[24,3072]{1,0:T(8,128)(2,1)S(1)}, bf16[24,3072]{1,0:T(8,128)(2,1)S(1)}, u32[]{:S(2)}, u32[]{:S(2)}) %collective-permute-start.4) | collective-permute-done | bytes 147488 | tf_op jit(solution)/shard_map/ppermute | solution.py:533
  21.5 0.6 collective-permute-start.9
  22.1 0.7 collective-permute-done.8.refs_9_
  23.1 33.6 %shard_map.105 = (bf16[96,3200]{1,0:T(8,128)(2,1)S(1)}, bf16[96,3200]{1,0:T(8,128)(2,1)S(1)}, bf16[6144,512]{1,0:T(8,128)(2,1)S(1)}, bf16[6144,512]{1,0:T(8,128)(2,1)S(1)}) custom-call(bf16[6144,2048]{1,0:T(8,128)(2,1)} %refs_0_.1, bf16[6144,2048]{1,0:T(8,128)(2,1)} %refs_1_.1, ...), custom_call_target="tpu_custom_call", output_to_operand_aliasing={{2}: (11, {}), {3}: (12, {})} | custom-call | flops 7247757312 | bytes 75497472 | tf_op jit(solution)/shard_map/pallas_call | solution.py:448
  56.7 0.4 collective-permute-start.10
  57.3 1.5 %collective-permute-done.10 = bf16[96,3200]{1,0:T(8,128)(2,1)S(1)} collective-permute-done((bf16[96,3200]{1,0:T(8,128)(2,1)S(1)}, bf16[96,3200]{1,0:T(8,128)(2,1)S(1)}, u32[]{:S(2)}, u32[]{:S(2)}) %collective-permute-start.10) | collective-permute-done | bytes 614432 | tf_op jit(solution)/shard_map/ppermute | solution.py:559
  59.0 0.6 collective-permute-start.11
  59.6 1.5 %collective-permute-start.12 = (bf16[24,3200]{1,0:T(8,128)(2,1)S(1)}, bf16[24,3200]{1,0:T(8,128)(2,1)S(1)}, u32[]{:S(2)}, u32[]{:S(2)}) collective-permute-start(bf16[24,3200]{1,0:T(8,128)(2,1)S(1)} %get-tuple-element.46), channel_id=1, source_target_pairs={{0,16},{4,20},{8,24},{12,28},{16,0},{20,4},{24,8},{28,12},{1,17},{... | collective-permute-start | bytes 460808 | tf_op jit(solution)/shard_map/ppermute | solution.py:561
  61.1 1.4 %collective-permute-start.13 = (bf16[24,3200]{1,0:T(8,128)(2,1)S(1)}, bf16[24,3200]{1,0:T(8,128)(2,1)S(1)}, u32[]{:S(2)}, u32[]{:S(2)}) collective-permute-start(bf16[24,3200]{1,0:T(8,128)(2,1)S(1)} %get-tuple-element.45), channel_id=1, source_target_pairs={{0,24},{4,28},{8,16},{12,20},{16,8},{20,12},{24,0},{28,4},{1,25},{... | collective-permute-start | bytes 460808 | tf_op jit(solution)/shard_map/ppermute | solution.py:561
  63.0 2.9 %collective-permute-done.11.refs_1_ = bf16[24,3200]{1,0:T(8,128)(2,1)S(1)} collective-permute-done((bf16[24,3200]{1,0:T(8,128)(2,1)S(1)}, bf16[24,3200]{1,0:T(8,128)(2,1)S(1)}, u32[]{:S(2)}, u32[]{:S(2)}) %collective-permute-start.11) | collective-permute-done | bytes 153632 | tf_op jit(solution)/shard_map/ppermute | solution.py:561
  65.9 2.1 %collective-permute-done.12.refs_2_ = bf16[24,3200]{1,0:T(8,128)(2,1)S(1)} collective-permute-done((bf16[24,3200]{1,0:T(8,128)(2,1)S(1)}, bf16[24,3200]{1,0:T(8,128)(2,1)S(1)}, u32[]{:S(2)}, u32[]{:S(2)}) %collective-permute-start.12) | collective-permute-done | bytes 153632 | tf_op jit(solution)/shard_map/ppermute | solution.py:561
  67.9 1.1 %collective-permute-done.13.refs_3_ = bf16[24,3200]{1,0:T(8,128)(2,1)S(1)} collective-permute-done((bf16[24,3200]{1,0:T(8,128)(2,1)S(1)}, bf16[24,3200]{1,0:T(8,128)(2,1)S(1)}, u32[]{:S(2)}, u32[]{:S(2)}) %collective-permute-start.13) | collective-permute-done | bytes 153632 | tf_op jit(solution)/shard_map/ppermute | solution.py:561
  69.1 0.7 shard_map.106
  69.8 3.3 %collective-permute-start.16 = (bf16[8,3200]{1,0:T(8,128)(2,1)S(1)}, bf16[8,3200]{1,0:T(8,128)(2,1)S(1)}, u32[]{:S(2)}, u32[]{:S(2)}) collective-permute-start(bf16[8,3200]{1,0:T(8,128)(2,1)S(1)} %get-tuple-element.28), channel_id=1, source_target_pairs={{0,3},{1,2},{2,1},{3,0},{4,7},{5,6},{6,5},{7,4},{8,11},{9,10},{10,... | collective-permute-start | bytes 153608 | tf_op jit(solution)/shard_map/ppermute | solution.py:565
  73.1 1.1 %collective-permute-start.14 = (bf16[8,3200]{1,0:T(8,128)(2,1)S(1)}, bf16[8,3200]{1,0:T(8,128)(2,1)S(1)}, u32[]{:S(2)}, u32[]{:S(2)}) collective-permute-start(bf16[8,3200]{1,0:T(8,128)(2,1)S(1)} %get-tuple-element.26), channel_id=1, source_target_pairs={{0,1},{1,0},{2,3},{3,2},{4,5},{5,4},{6,7},{7,6},{8,9},{9,8},{10,11... | collective-permute-start | bytes 153608 | tf_op jit(solution)/shard_map/ppermute | solution.py:565
  74.3 1.6 %collective-permute-done.16 = bf16[8,3200]{1,0:T(8,128)(2,1)S(1)} collective-permute-done((bf16[8,3200]{1,0:T(8,128)(2,1)S(1)}, bf16[8,3200]{1,0:T(8,128)(2,1)S(1)}, u32[]{:S(2)}, u32[]{:S(2)}) %collective-permute-start.16) | collective-permute-done | bytes 51232 | tf_op jit(solution)/shard_map/ppermute | solution.py:565
  75.9 2.2 %collective-permute-done.15 = bf16[8,3200]{1,0:T(8,128)(2,1)S(1)} collective-permute-done((bf16[8,3200]{1,0:T(8,128)(2,1)S(1)}, bf16[8,3200]{1,0:T(8,128)(2,1)S(1)}, u32[]{:S(2)}, u32[]{:S(2)}) %collective-permute-start.15) | collective-permute-done | bytes 51232 | tf_op jit(solution)/shard_map/ppermute | solution.py:565
  78.2 0.6 fusion.6
  78.8 0.6 copy.54
  (52 shorter events, 2.7 us)
Async XLA Ops:
  1.4 9.5 %collective-permute-start = (bf16[8,3072]{1,0:T(8,128)(2,1)S(1)}, bf16[8,3072]{1,0:T(8,128)(2,1)S(1)}, u32[]{:S(2)}, u32[]{:S(2)}) collective-permute-start(bf16[8,3072]{1,0:T(8,128)(2,1)S(1)} %pad_add_fusion.refs_0_), channel_id=1, source_target_pairs={{0,3},{1,2},{2,1},{3,0},{4,7},{5,6},{6,5},{7,4},{8,11},{9,10},{10,... | collective-permute-start | bytes 147464 | tf_op jit(solution)/shard_map/ppermute | solution.py:497
  6.4 5.0 %collective-permute-start.1 = (bf16[8,3072]{1,0:T(8,128)(2,1)S(1)}, bf16[8,3072]{1,0:T(8,128)(2,1)S(1)}, u32[]{:S(2)}, u32[]{:S(2)}) collective-permute-start(bf16[8,3072]{1,0:T(8,128)(2,1)S(1)} %pad_add_fusion.refs_0_), channel_id=1, source_target_pairs={{0,2},{1,3},{2,0},{3,1},{4,6},{5,7},{6,4},{7,5},{8,10},{9,11},{10,... | collective-permute-start | bytes 147464 | tf_op jit(solution)/shard_map/ppermute | solution.py:497
  6.4 5.0 %collective-permute-start.2 = (bf16[8,3072]{1,0:T(8,128)(2,1)S(1)}, bf16[8,3072]{1,0:T(8,128)(2,1)S(1)}, u32[]{:S(2)}, u32[]{:S(2)}) collective-permute-start(bf16[8,3072]{1,0:T(8,128)(2,1)S(1)} %pad_add_fusion.refs_0_), channel_id=1, source_target_pairs={{0,1},{1,0},{2,3},{3,2},{4,5},{5,4},{6,7},{7,6},{8,9},{9,8},{10,11... | collective-permute-start | bytes 147464 | tf_op jit(solution)/shard_map/ppermute | solution.py:497
  11.7 8.2 %collective-permute-start.3 = (bf16[24,3072]{1,0:T(8,128)(2,1)S(1)}, bf16[24,3072]{1,0:T(8,128)(2,1)S(1)}, u32[]{:S(2)}, u32[]{:S(2)}) collective-permute-start(bf16[24,3072]{1,0:T(8,128)(2,1)S(1)} %get-tuple-element.17), channel_id=1, source_target_pairs={{0,8},{4,12},{8,0},{12,4},{16,24},{20,28},{24,16},{28,20},{1,9},{5... | collective-permute-start | bytes 442376 | tf_op jit(solution)/shard_map/ppermute | solution.py:533
  13.3 8.2 %collective-permute-start.4 = (bf16[24,3072]{1,0:T(8,128)(2,1)S(1)}, bf16[24,3072]{1,0:T(8,128)(2,1)S(1)}, u32[]{:S(2)}, u32[]{:S(2)}) collective-permute-start(bf16[24,3072]{1,0:T(8,128)(2,1)S(1)} %get-tuple-element.18), channel_id=1, source_target_pairs={{0,16},{4,20},{8,24},{12,28},{16,0},{20,4},{24,8},{28,12},{1,17},{... | collective-permute-start | bytes 442376 | tf_op jit(solution)/shard_map/ppermute | solution.py:533
  14.8 6.7 %collective-permute-start.5 = (bf16[24,3072]{1,0:T(8,128)(2,1)S(1)}, bf16[24,3072]{1,0:T(8,128)(2,1)S(1)}, u32[]{:S(2)}, u32[]{:S(2)}) collective-permute-start(bf16[24,3072]{1,0:T(8,128)(2,1)S(1)} %get-tuple-element.19), channel_id=1, source_target_pairs={{0,24},{4,28},{8,16},{12,20},{16,8},{20,12},{24,0},{28,4},{1,25},{... | collective-permute-start | bytes 442376 | tf_op jit(solution)/shard_map/ppermute | solution.py:533
  15.3 6.8 %collective-permute-start.6 = (bf16[24,3072]{1,0:T(8,128)(2,1)S(1)}, bf16[24,3072]{1,0:T(8,128)(2,1)S(1)}, u32[]{:S(2)}, u32[]{:S(2)}) collective-permute-start(bf16[24,3072]{1,0:T(8,128)(2,1)S(1)} %get-tuple-element.16.after_ref.refs_3_), channel_id=1, source_target_pairs={{0,4},{4,0},{8,12},{12,8},{16,20},{20,16},{24,28},{28,24},{1,5},{5... | collective-permute-start | bytes 442376 | tf_op jit(solution)/shard_map/ppermute | solution.py:541
  19.9 2.1 %collective-permute-start.7 = (bf16[24,3072]{1,0:T(8,128)(2,1)S(1)}, bf16[24,3072]{1,0:T(8,128)(2,1)S(1)}, u32[]{:S(2)}, u32[]{:S(2)}) collective-permute-start(bf16[24,3072]{1,0:T(8,128)(2,1)S(1)} %collective-permute-done.3.refs_4_), channel_id=1, source_target_pairs={{0,4},{4,0},{8,12},{12,8},{16,20},{20,16},{24,28},{28,24},{1,5},{5... | collective-permute-start | bytes 442376 | tf_op jit(solution)/shard_map/ppermute | solution.py:541
  21.5 1.4 %collective-permute-start.8 = (bf16[24,3072]{1,0:T(8,128)(2,1)S(1)}, bf16[24,3072]{1,0:T(8,128)(2,1)S(1)}, u32[]{:S(2)}, u32[]{:S(2)}) collective-permute-start(bf16[24,3072]{1,0:T(8,128)(2,1)S(1)} %collective-permute-done.4.refs_5_), channel_id=1, source_target_pairs={{0,4},{4,0},{8,12},{12,8},{16,20},{20,16},{24,28},{28,24},{1,5},{5... | collective-permute-start | bytes 442376 | tf_op jit(solution)/shard_map/ppermute | solution.py:541
  21.5 1.6 %collective-permute-start.9 = (bf16[24,3072]{1,0:T(8,128)(2,1)S(1)}, bf16[24,3072]{1,0:T(8,128)(2,1)S(1)}, u32[]{:S(2)}, u32[]{:S(2)}) collective-permute-start(bf16[24,3072]{1,0:T(8,128)(2,1)S(1)} %add.36.refs_6_), channel_id=1, source_target_pairs={{0,4},{4,0},{8,12},{12,8},{16,20},{20,16},{24,28},{28,24},{1,5},{5... | collective-permute-start | bytes 442376 | tf_op jit(solution)/shard_map/ppermute | solution.py:541
  23.1 34.1 %copy-start = (s32[8,2]{0,1:T(2,128)S(1)}, s32[8,2]{0,1:T(2,128)}, u32[]{:S(2)}) copy-start(s32[8,2]{0,1:T(2,128)} %param.9) | copy-start | bytes 196
  23.1 51.1 %copy-start.1 = (f32[8,2]{0,1:T(2,128)S(1)}, f32[8,2]{0,1:T(2,128)}, u32[]{:S(2)}) copy-start(f32[8,2]{0,1:T(2,128)} %param.10) | copy-start | bytes 196
  56.7 2.1 %collective-permute-start.10 = (bf16[96,3200]{1,0:T(8,128)(2,1)S(1)}, bf16[96,3200]{1,0:T(8,128)(2,1)S(1)}, u32[]{:S(2)}, u32[]{:S(2)}) collective-permute-start(bf16[96,3200]{1,0:T(8,128)(2,1)S(1)} %get-tuple-element.24), channel_id=1, source_target_pairs={{0,4},{4,0},{8,12},{12,8},{16,20},{20,16},{24,28},{28,24},{1,5},{5... | collective-permute-start | bytes 1843208 | tf_op jit(solution)/shard_map/ppermute | solution.py:559
  59.0 6.9 %collective-permute-start.11 = (bf16[24,3200]{1,0:T(8,128)(2,1)S(1)}, bf16[24,3200]{1,0:T(8,128)(2,1)S(1)}, u32[]{:S(2)}, u32[]{:S(2)}) collective-permute-start(bf16[24,3200]{1,0:T(8,128)(2,1)S(1)} %get-tuple-element.47), channel_id=1, source_target_pairs={{0,8},{4,12},{8,0},{12,4},{16,24},{20,28},{24,16},{28,20},{1,9},{5... | collective-permute-start | bytes 460808 | tf_op jit(solution)/shard_map/ppermute | solution.py:561
  59.6 8.3 %collective-permute-start.12 = (bf16[24,3200]{1,0:T(8,128)(2,1)S(1)}, bf16[24,3200]{1,0:T(8,128)(2,1)S(1)}, u32[]{:S(2)}, u32[]{:S(2)}) collective-permute-start(bf16[24,3200]{1,0:T(8,128)(2,1)S(1)} %get-tuple-element.46), channel_id=1, source_target_pairs={{0,16},{4,20},{8,24},{12,28},{16,0},{20,4},{24,8},{28,12},{1,17},{... | collective-permute-start | bytes 460808 | tf_op jit(solution)/shard_map/ppermute | solution.py:561
  61.1 7.9 %collective-permute-start.13 = (bf16[24,3200]{1,0:T(8,128)(2,1)S(1)}, bf16[24,3200]{1,0:T(8,128)(2,1)S(1)}, u32[]{:S(2)}, u32[]{:S(2)}) collective-permute-start(bf16[24,3200]{1,0:T(8,128)(2,1)S(1)} %get-tuple-element.45), channel_id=1, source_target_pairs={{0,24},{4,28},{8,16},{12,20},{16,8},{20,12},{24,0},{28,4},{1,25},{... | collective-permute-start | bytes 460808 | tf_op jit(solution)/shard_map/ppermute | solution.py:561
  69.8 6.1 %collective-permute-start.16 = (bf16[8,3200]{1,0:T(8,128)(2,1)S(1)}, bf16[8,3200]{1,0:T(8,128)(2,1)S(1)}, u32[]{:S(2)}, u32[]{:S(2)}) collective-permute-start(bf16[8,3200]{1,0:T(8,128)(2,1)S(1)} %get-tuple-element.28), channel_id=1, source_target_pairs={{0,3},{1,2},{2,1},{3,0},{4,7},{5,6},{6,5},{7,4},{8,11},{9,10},{10,... | collective-permute-start | bytes 153608 | tf_op jit(solution)/shard_map/ppermute | solution.py:565
  73.1 5.0 %collective-permute-start.15 = (bf16[8,3200]{1,0:T(8,128)(2,1)S(1)}, bf16[8,3200]{1,0:T(8,128)(2,1)S(1)}, u32[]{:S(2)}, u32[]{:S(2)}) collective-permute-start(bf16[8,3200]{1,0:T(8,128)(2,1)S(1)} %get-tuple-element.27), channel_id=1, source_target_pairs={{0,2},{1,3},{2,0},{3,1},{4,6},{5,7},{6,4},{7,5},{8,10},{9,11},{10,... | collective-permute-start | bytes 153608 | tf_op jit(solution)/shard_map/ppermute | solution.py:565
  73.1 5.0 %collective-permute-start.14 = (bf16[8,3200]{1,0:T(8,128)(2,1)S(1)}, bf16[8,3200]{1,0:T(8,128)(2,1)S(1)}, u32[]{:S(2)}, u32[]{:S(2)}) collective-permute-start(bf16[8,3200]{1,0:T(8,128)(2,1)S(1)} %get-tuple-element.26), channel_id=1, source_target_pairs={{0,1},{1,0},{2,3},{3,2},{4,5},{5,4},{6,7},{7,6},{8,9},{9,8},{10,11... | collective-permute-start | bytes 153608 | tf_op jit(solution)/shard_map/ppermute | solution.py:565
